TPU v7x, 32 devices: a whole 2x2x4 slice. The times are simulated.
32 devices in a mesh: remap: 8 (over z, y), rep: 4 (over x, core).
Axes of the slice: x: 2, y: 2, z: 4, core: 2. Of those that a mesh axis runs over, the one named last changes fastest.
Arguments:
- amplitudes: bfloat16 [64, 1200, 1200], P('remap', None, 'rep'), may hold values from -6 to 6
- integrals: bfloat16 [1200, 1200, 128], P('remap', 'rep'), may hold values from -0.01953125 to 0.01953125
- orbital_irreps: int32 [1200], replicated, may hold values from 0 to 7
- slab_index: int32 [1], replicated, may hold values from 0 to 63
Outputs:
- residual: float32 [64, 128], P('remap', 'rep')
All inputs are finite; a program needn't handle non-finite values.
Results may differ from a plain program's by a relative error of at most 0.0003.
Values may be sent and summed in bfloat16 or wider, within the bound.
No kernel may reach another device: no remote copies, remote signals or barrier semaphores. Data moves between devices by JAX's collectives and lax.ppermute only.
A program may use at most 128 MiB of HBM per device.

v0:
```python
import jax
import jax.numpy as jnp
from jax import lax
from jax.sharding import PartitionSpec as P

SLABS = 64


def irrep_of(indices, table):
    matches = indices[:, None] == jnp.arange(table.shape[0], dtype=jnp.int32)[None, :]
    return jnp.sum(jnp.where(matches, table[None, :], 0), axis=1)


def body(amplitudes, integrals, orbital_irreps, slab_index):
    c_rows, d_cols, ab_cols = integrals.shape
    virtual = orbital_irreps.shape[0]
    c_first = lax.axis_index("remap") * c_rows
    d_first = lax.axis_index("rep") * d_cols
    irr_c = lax.dynamic_slice_in_dim(orbital_irreps, c_first, c_rows, 0)
    irr_d = lax.dynamic_slice_in_dim(orbital_irreps, d_first, d_cols, 0)
    stride = virtual * virtual // SLABS
    pair_ab = slab_index[0] * stride + jnp.arange(ab_cols, dtype=jnp.int32)
    sym_ab = jnp.bitwise_xor(
        irrep_of(pair_ab // virtual, orbital_irreps), irrep_of(pair_ab % virtual, orbital_irreps)
    )
    sym_cd = jnp.bitwise_xor(irr_c[:, None], irr_d[None, :])
    allowed = sym_cd[:, :, None] == sym_ab[None, None, :]
    blocked = jnp.where(allowed, integrals, jnp.zeros((), jnp.bfloat16)).reshape(
        c_rows * d_cols, ab_cols
    )
    arrived = lax.all_to_all(amplitudes, "remap", split_axis=1, concat_axis=0, tiled=True)
    flattened = arrived.reshape(arrived.shape[0], c_rows * d_cols)
    partial_term = lax.psum_scatter(
        jnp.dot(flattened, blocked, preferred_element_type=jnp.float32),
        "remap",
        scatter_dimension=0,
        tiled=True,
    )
    return 0.5 * lax.psum_scatter(partial_term, "rep", scatter_dimension=1, tiled=True)


def solution(mesh):
    in_specs = (P("remap", None, "rep"), P("remap", "rep", None), P(), P())
    out_specs = P("remap", "rep")
    return jax.shard_map(body, mesh=mesh, in_specs=in_specs, out_specs=out_specs, check_vma=False)
```

profile of v0, /device:TPU:0, one launch (start us, length us, event | category | flops | bytes accessed | tf_op | source)
XLA Modules:
  0.0 272.5 jit_solution(1407684155490132877)
XLA Ops:
  6.5 0.0 copy-start
  6.5 10.9 %copy.9 = bf16[8,1200,300]{2,0,1:T(8,128)(2,1)} copy(bf16[8,1200,300]{1,0,2:T(8,128)(2,1)} %param.4) | data formatting | bytes 11520000 | tf_op args[0]
  17.4 7.3 %all-to-all-start = ((bf16[8,1200,300]{2,0,1:T(8,128)(2,1)}), bf16[8,1200,300]{2,0,1:T(8,128)(2,1)}, u32[]{:S(2)}, u32[]{:S(2)}) async-start(bf16[8,1200,300]{2,0,1:T(8,128)(2,1)} %copy.9), calls=%async_computation | async-start | bytes 14745600 | tf_op jit(solution)/shard_map/all_to_all | solution.py:31
  24.7 0.0 reduce-scatter.4.cloned.1.call-start
  24.8 0.0 copy-done
  24.8 0.1 dynamic_slice.6
  24.9 0.1 dynamic_slice.7
  25.6 0.2 select_reduce_fusion
  25.9 0.1 broadcast_xor_fusion
  26.0 10.6 %compare_select_fusion = bf16[150,300,128]{2,1,0:T(8,128)(2,1)} fusion(bf16[150,300,128]{2,1,0:T(8,128)(2,1)} %param.5, s32[128]{0:T(128)S(1)} %xor.27, s32[150,300]{1,0:T(8,128)S(1)} %broadcast_xor_fusion), kind=kLoop, calls=%fused_computation | loop fusion | flops 11520000 | bytes 23220512 | tf_op jit(solution)/shard_map/jit(_where)/select_n | solution.py:28
  36.6 0.0 copy-start.1
  36.6 15.4 %reshape.60 = bf16[45000,128]{1,0:T(8,128)(2,1)} reshape(bf16[150,300,128]{2,1,0:T(8,128)(2,1)} %compare_select_fusion) | data formatting | bytes 23040000 | tf_op jit(solution)/shard_map/reshape | solution.py:28
  52.0 0.0 copy-done.1
  52.0 0.6 dynamic-slice
  53.2 132.9 %all-to-all-done = bf16[8,1200,300]{2,0,1:T(8,128)(2,1)} async-done(((bf16[8,1200,300]{2,0,1:T(8,128)(2,1)}), bf16[8,1200,300]{2,0,1:T(8,128)(2,1)}, u32[]{:S(2)}, u32[]{:S(2)}) %all-to-all-start) | async-done | bytes 5760032 | tf_op jit(solution)/shard_map/all_to_all | solution.py:31
  186.1 7.3 %copy.10 = bf16[8,8,150,300]{3,2,1,0:T(8,128)(2,1)} copy(bf16[8,8,150,300]{3,1,2,0:T(8,128)(2,1)} %bitcast.2) | data formatting | bytes 11520000 | tf_op jit(solution)/shard_map/all_to_all | solution.py:31
  193.5 10.2 %reshape.61 = bf16[64,45000]{1,0:T(8,128)(2,1)} reshape(bf16[8,8,150,300]{3,2,1,0:T(8,128)(2,1)} %copy.10) | data formatting | bytes 11520000 | tf_op jit(solution)/shard_map/reshape | solution.py:32
  203.6 7.8 %convolution_bitcast_fusion = f32[64,128]{1,0:T(8,128)S(1)} fusion(bf16[45000,128]{1,0:T(8,128)(2,1)} %reshape.60, bf16[64,45000]{1,0:T(8,128)(2,1)} %reshape.61), kind=kOutput, calls=%fused_computation.1 | convolution fusion | flops 737280000 | bytes 17312768 | tf_op jit(solution)/shard_map/dot_general | solution.py:34
  211.4 35.2 %all-reduce = f32[64,128]{1,0:T(8,128)S(1)} all-reduce(f32[64,128]{1,0:T(8,128)S(1)} %convolution_bitcast_fusion), channel_id=2, replica_groups=mesh['remap'=8,'rep'=4] {'remap'}, use_global_device_ids=true, to_apply=%region_2.3.clone | all-reduce | flops 8192 | bytes 65536
  246.6 0.7 copy.11
  247.4 0.0 reduce-scatter.4.cloned.1.call-update
  247.4 16.8 %reduce-scatter.4.cloned.1.call-done = f32[32,8]{1,0:T(8,128)} async-done(((f32[128,8]{1,0:T(8,128)}), f32[32,8]{1,0:T(8,128)}) %reduce-scatter.4.cloned.1.call-update) | async-done | bytes 1040
  264.2 0.8 copy.12
  265.0 0.6 broadcast_multiply_fusion
  (3 shorter events, 0.0 us)
Async XLA Ops:
  6.5 18.3 %copy-start = (s32[1200]{0:T(1024)S(1)}, s32[1200]{0:T(1024)}, u32[]{:S(2)}) copy-start(s32[1200]{0:T(1024)} %param.6) | copy-start | bytes 14404
  17.4 168.7 %all-to-all-start = ((bf16[8,1200,300]{2,0,1:T(8,128)(2,1)}), bf16[8,1200,300]{2,0,1:T(8,128)(2,1)}, u32[]{:S(2)}, u32[]{:S(2)}) async-start(bf16[8,1200,300]{2,0,1:T(8,128)(2,1)} %copy.9), calls=%async_computation | async-start | bytes 14745600 | tf_op jit(solution)/shard_map/all_to_all | solution.py:31
  24.7 239.5 %reduce-scatter.4.cloned.1.call-start = ((), (), s32[]{:S(2)}) async-start(), calls=%async_computation.2 | async-start | bytes 81920
  36.6 15.4 %copy-start.1 = (u32[32]{0:T(128)S(1)}, u32[32]{0:T(128)}, u32[]{:S(2)}) copy-start(u32[32]{0:T(128)} %constant.44) | copy-start | bytes 388
Sparse Core Ops, SparseCore 0:
  247.5 16.6 reduce-scatter.3
where the time goes:
time: 274 us; the launch traced here: 272 us
  waiting for transfers between devices  150 us (55%)
  local copies, waits for them, and re-layouts  46.1 us (17%)
  blocking collectives  35.2 us (13%)
  between operations  14.8 us (5%)
  other arithmetic  11.5 us (4%)
  matrix products  7.76 us (3%)
  starting transfers between devices  7.32 us (3%)
    all_to_all x1, waiting for transfers between devices, body(): lax.all_to_all(amplitudes, 'remap', split_axis=1, concat_axis=0, tiled=True)  133 us
    unnamed x1, blocking collectives  35.2 us
    unnamed x2, waiting for transfers between devices  16.9 us
    reshape x1, local copies, waits for them, and re-layouts, body(): jnp.where(allowed, integrals, jnp.zeros((), jnp.bfloat16))  15.4 us
    unnamed x9, local copies, waits for them, and re-layouts  13 us
    select_n x1, other arithmetic, body(): jnp.where(allowed, integrals, jnp.zeros((), jnp.bfloat16))  10.6 us
    reshape x1, local copies, waits for them, and re-layouts, body(): flattened = arrived.reshape(arrived.shape[0], c_rows * d_cols)  10.2 us
    dot_general x1, matrix products, body(): jnp.dot(flattened, blocked, preferred_element_type=jnp.float32)  7.76 us
  transfers between devices with their start and end apart: 2, of which 2 were waited for; matrix products, arithmetic and copies ran while one was open for 10% of the time, Pallas kernels for 0%

commit v1 on v0

--- a/solution.py
+++ b/solution.py
@@ -9,6 +9,15 @@
 def irrep_of(indices, table):
     matches = indices[:, None] == jnp.arange(table.shape[0], dtype=jnp.int32)[None, :]
     return jnp.sum(jnp.where(matches, table[None, :], 0), axis=1)
+
+
+def reduce_to_owners(partial_term):
+    remap, rep = lax.axis_size("remap"), lax.axis_size("rep")
+    rows, cols = partial_term.shape
+    blocks = partial_term.reshape(remap, rows // remap, rep, cols // rep)
+    blocks = blocks.transpose(0, 2, 1, 3).reshape(remap * rep, rows // remap, cols // rep)
+    arrived = lax.all_to_all(blocks, ("remap", "rep"), split_axis=0, concat_axis=0, tiled=True)
+    return jnp.sum(arrived, axis=0)
 
 
 def body(amplitudes, integrals, orbital_irreps, slab_index):
@@ -30,13 +39,8 @@
     )
     arrived = lax.all_to_all(amplitudes, "remap", split_axis=1, concat_axis=0, tiled=True)
     flattened = arrived.reshape(arrived.shape[0], c_rows * d_cols)
-    partial_term = lax.psum_scatter(
-        jnp.dot(flattened, blocked, preferred_element_type=jnp.float32),
-        "remap",
-        scatter_dimension=0,
-        tiled=True,
-    )
-    return 0.5 * lax.psum_scatter(partial_term, "rep", scatter_dimension=1, tiled=True)
+    partial_term = jnp.dot(flattened, blocked, preferred_element_type=jnp.float32)
+    return 0.5 * reduce_to_owners(partial_term)
 
 
 def solution(mesh):

time: 274 us -> 219 us (0.80)
  blocking collectives: 35.2 us -> 10.7 us
  waiting for transfers between devices: 150 us -> 134 us
  between operations: 14.8 us -> 0.72 us
    unnamed x1 -> x0, blocking collectives: 35.2 us -> none
    unnamed x2 -> x0, waiting for transfers between devices: 16.9 us -> none
    all_to_all x0 -> x1, blocking collectives: none -> 10.7 us  [reduce_to_owners(): lax.all_to_all(blocks, ('remap', 'rep'), split_axis=0, concat_axis=0, til...]
    unnamed x9 -> x5, local copies, waits for them, and re-layouts: 13 us -> 11.1 us
  transfers between devices with their start and end apart: 2 -> 1, of which waited for: 2 -> 1; matrix products, arithmetic and copies ran while one was open for 10% -> 12% of each run, Pallas kernels for 0% -> 0%
where the time goes in v1:
time: 219 us; the launch traced here: 218 us
  waiting for transfers between devices  134 us (61%)
  local copies, waits for them, and re-layouts  44.8 us (20%)
  other arithmetic  12.3 us (6%)
  blocking collectives  10.7 us (5%)
  matrix products  7.76 us (4%)
  starting transfers between devices  7.28 us (3%)
    all_to_all x1, waiting for transfers between devices, body(): lax.all_to_all(amplitudes, 'remap', split_axis=1, concat_axis=0, tiled=True)  134 us
    reshape x1, local copies, waits for them, and re-layouts, body(): jnp.where(allowed, integrals, jnp.zeros((), jnp.bfloat16))  15.4 us
    unnamed x5, local copies, waits for them, and re-layouts  11.1 us
    all_to_all x1, blocking collectives, reduce_to_owners(): lax.all_to_all(blocks, ('remap', 'rep'), split_axis=0, concat_axis=0, til...  10.7 us
    select_n x1, other arithmetic, body(): jnp.where(allowed, integrals, jnp.zeros((), jnp.bfloat16))  10.6 us
    reshape x1, local copies, waits for them, and re-layouts, body(): flattened = arrived.reshape(arrived.shape[0], c_rows * d_cols)  10.2 us
    dot_general x1, matrix products, body(): jnp.dot(flattened, blocked, preferred_element_type=jnp.float32)  7.76 us
    all_to_all x1, local copies, waits for them, and re-layouts, body(): lax.all_to_all(amplitudes, 'remap', split_axis=1, concat_axis=0, tiled=True)  7.33 us
  transfers between devices with their start and end apart: 1, of which 1 were waited for; matrix products, arithmetic and copies ran while one was open for 12% of the time, Pallas kernels for 0%

profile of v1, /device:TPU:0, one launch (start us, length us, event | category | flops | bytes accessed | tf_op | source)
XLA Modules:
  0.0 217.8 jit_solution(4103703532121465784)
XLA Ops:
  0.0 0.0 copy-start
  0.0 10.9 %copy.8 = bf16[8,1200,300]{2,0,1:T(8,128)(2,1)} copy(bf16[8,1200,300]{1,0,2:T(8,128)(2,1)} %param.4) | data formatting | bytes 11520000 | tf_op args[0]
  10.9 7.3 %all-to-all-start = ((bf16[8,1200,300]{2,0,1:T(8,128)(2,1)}), bf16[8,1200,300]{2,0,1:T(8,128)(2,1)}, u32[]{:S(2)}, u32[]{:S(2)}) async-start(bf16[8,1200,300]{2,0,1:T(8,128)(2,1)} %copy.8), calls=%async_computation | async-start | bytes 14745600 | tf_op jit(solution)/shard_map/all_to_all | solution.py:40
  18.2 0.0 copy-done
  18.2 0.1 dynamic_slice.6
  18.3 0.1 dynamic_slice.7
  19.0 0.2 select_reduce_fusion
  19.3 0.1 broadcast_xor_fusion
  19.4 10.6 %compare_select_fusion = bf16[150,300,128]{2,1,0:T(8,128)(2,1)} fusion(bf16[150,300,128]{2,1,0:T(8,128)(2,1)} %param.5, s32[128]{0:T(128)S(1)} %xor.27, s32[150,300]{1,0:T(8,128)S(1)} %broadcast_xor_fusion), kind=kLoop, calls=%fused_computation | loop fusion | flops 11520000 | bytes 23220512 | tf_op jit(solution)/shard_map/jit(_where)/select_n | solution.py:37
  30.0 15.4 %reshape.66 = bf16[45000,128]{1,0:T(8,128)(2,1)} reshape(bf16[150,300,128]{2,1,0:T(8,128)(2,1)} %compare_select_fusion) | data formatting | bytes 23040000 | tf_op jit(solution)/shard_map/reshape | solution.py:37
  45.4 134.2 %all-to-all-done = bf16[8,1200,300]{2,0,1:T(8,128)(2,1)} async-done(((bf16[8,1200,300]{2,0,1:T(8,128)(2,1)}), bf16[8,1200,300]{2,0,1:T(8,128)(2,1)}, u32[]{:S(2)}, u32[]{:S(2)}) %all-to-all-start) | async-done | bytes 5760032 | tf_op jit(solution)/shard_map/all_to_all | solution.py:40
  179.6 7.3 %copy.9 = bf16[8,8,150,300]{3,2,1,0:T(8,128)(2,1)} copy(bf16[8,8,150,300]{3,1,2,0:T(8,128)(2,1)} %bitcast.2) | data formatting | bytes 11520000 | tf_op jit(solution)/shard_map/all_to_all | solution.py:40
  186.9 10.2 %reshape.67 = bf16[64,45000]{1,0:T(8,128)(2,1)} reshape(bf16[8,8,150,300]{3,2,1,0:T(8,128)(2,1)} %copy.9) | data formatting | bytes 11520000 | tf_op jit(solution)/shard_map/reshape | solution.py:41
  197.1 7.8 %convolution_bitcast_fusion = f32[64,128]{1,0:T(8,128)S(1)} fusion(bf16[45000,128]{1,0:T(8,128)(2,1)} %reshape.66, bf16[64,45000]{1,0:T(8,128)(2,1)} %reshape.67), kind=kOutput, calls=%fused_computation.1 | convolution fusion | flops 737280000 | bytes 17312768 | tf_op jit(solution)/shard_map/dot_general | solution.py:42
  204.9 0.1 reshape.68
  205.0 0.1 reshape.70
  205.1 10.7 %all_to_all.20 = f32[32,1,256]{2,1,0:T(1,128)S(1)} all-to-all(f32[32,1,256]{2,1,0:T(1,128)S(1)} %reshape.70), channel_id=1, replica_groups=mesh['remap'=8,'rep'=4] {'remap','rep'}, dimensions={0} | all-to-all | bytes 65536 | tf_op jit(solution)/shard_map/all_to_all | solution.py:19
  215.9 0.5 broadcast.64
  216.4 0.7 reduce
  217.1 0.1 reshape.71
  217.2 0.6 broadcast_multiply_fusion
  (4 shorter events, 0.1 us)
Async XLA Ops:
  0.0 18.2 %copy-start = (s32[1200]{0:T(1024)S(1)}, s32[1200]{0:T(1024)}, u32[]{:S(2)}) copy-start(s32[1200]{0:T(1024)} %param.6) | copy-start | bytes 14404
  10.9 168.7 %all-to-all-start = ((bf16[8,1200,300]{2,0,1:T(8,128)(2,1)}), bf16[8,1200,300]{2,0,1:T(8,128)(2,1)}, u32[]{:S(2)}, u32[]{:S(2)}) async-start(bf16[8,1200,300]{2,0,1:T(8,128)(2,1)} %copy.8), calls=%async_computation | async-start | bytes 14745600 | tf_op jit(solution)/shard_map/all_to_all | solution.py:40

commit v2 on v1

v2 whole, which is shorter than its diff:
```python
import functools

import jax
import jax.numpy as jnp
import numpy as np
from jax import lax
from jax.experimental import pallas as pl
from jax.experimental.pallas import tpu as pltpu
from jax.sharding import PartitionSpec as P

SLABS = 64
IRREPS = 8
BINS = 10
LEFT = 9
VMEM_BYTES = 48 * 1024 * 1024
BYTES_A_US = 3_600_000


def irrep_of(indices, table):
    matches = indices[:, None] == jnp.arange(table.shape[0], dtype=jnp.int32)[None, :]
    return jnp.sum(jnp.where(matches, table[None, :], 0), axis=1)


def reduce_to_owners(partial_term):
    remap, rep = lax.axis_size("remap"), lax.axis_size("rep")
    rows, cols = partial_term.shape
    blocks = partial_term.reshape(remap, rows // remap, rep, cols // rep)
    blocks = blocks.transpose(0, 2, 1, 3).reshape(remap * rep, rows // remap, cols // rep)
    arrived = lax.all_to_all(blocks, ("remap", "rep"), split_axis=0, concat_axis=0, tiled=True)
    return jnp.sum(arrived, axis=0)


def first_plus_one(match):
    c_plus_one = jnp.arange(1, match.shape[1] + 1, dtype=jnp.int32)
    return jnp.sum(jnp.where(match, c_plus_one[None, :, None], 0), axis=1)


def takes(us):
    return pl.CostEstimate(flops=0, bytes_accessed=int(us * BYTES_A_US), transcendentals=0)


def whole(array):
    zeros = (0,) * array.ndim
    return pl.BlockSpec(array.shape, lambda *_: zeros)


def split_lanes(d_cols):
    main = d_cols // 128 * 128
    tail = d_cols - main
    pitch = -(-tail // 8) * 8
    return main, tail, pitch


def pack_kernel(c_at, irrep_at, code_ref, integrals, out_ref, rows, arrived):
    bins = out_ref.shape[0]
    code = code_ref[...]

    def fetch(i):
        return pltpu.make_async_copy(integrals.at[c_at[i]], rows.at[i], arrived.at[i])

    def start(i, carry):
        fetch(i).start()
        return carry

    def one(g, carry):
        total = jnp.zeros(code.shape, jnp.float32)
        for h in range(IRREPS):
            i = g * IRREPS + h
            fetch(i).wait()
            total = jnp.where(code == irrep_at[i], rows[i].astype(jnp.float32), total)
        out_ref[g, pl.ds(0, code.shape[0])] = total.astype(out_ref.dtype)
        return carry

    lax.fori_loop(0, bins * IRREPS, start, 0)
    lax.fori_loop(0, bins, one, 0)


def pack(integrals, code, slots):
    _, d_cols, ab = integrals.shape
    padded = -(-d_cols // 16) * 16
    count = slots.shape[0]
    irrep = jnp.arange(count, dtype=jnp.int32) % IRREPS
    c_at = jnp.maximum(slots - 1, 0)
    irrep_at = jnp.where(slots > 0, irrep, IRREPS)
    out = jax.ShapeDtypeStruct((count // IRREPS, padded, ab), integrals.dtype)
    return pl.pallas_call(
        pack_kernel,
        out_shape=out,
        grid_spec=pltpu.PrefetchScalarGridSpec(
            num_scalar_prefetch=2,
            grid=(1,),
            in_specs=[whole(code), pl.BlockSpec(memory_space=pl.ANY)],
            out_specs=whole(out),
            scratch_shapes=[
                pltpu.VMEM((count, d_cols, ab), integrals.dtype),
                pltpu.SemaphoreType.DMA((count,)),
            ],
        ),
        cost_estimate=takes(4),
        compiler_params=pltpu.CompilerParams(vmem_limit_bytes=VMEM_BYTES),
        name="pack_bins",
    )(c_at, irrep_at, code, integrals)


def route_kernel(firsts, width, c_at, blocks, rows_ref, *outs):
    base = blocks[pl.program_id(0)] * width
    pair_rows, d_cols = rows_ref.shape[1:]
    main, tail, pitch = split_lanes(d_cols)
    for first, out in zip(firsts, outs):

        def one(group, carry):
            tails = []
            for i in range(IRREPS):
                at = c_at[base + (first + group) * IRREPS + i]
                out[0, group, :, pl.ds(i * main, main)] = rows_ref[at, :, pl.ds(0, main)]
                end = rows_ref[at, :, pl.ds(main, tail)].astype(jnp.float32)
                tails += [end, jnp.zeros((pair_rows, pitch - tail), jnp.float32)]
            ends = jnp.concatenate([x for x in tails if x.shape[1]], axis=1)
            out[0, group, :, pl.ds(IRREPS * main, IRREPS * pitch)] = ends.astype(out.dtype)
            return carry

        lax.fori_loop(0, out.shape[1], one, 0)


def route(by_c, c_at, blocks, spans, c_rows, by_block):
    pair_rows, d_cols = by_c.shape[1:]
    steps = blocks.shape[0]
    main, _, pitch = split_lanes(d_cols)
    lanes = IRREPS * (main + pitch)
    at_block = lambda i, c_at, blocks: (blocks[i], 0, 0, 0)
    in_order = lambda i, c_at, blocks: (i, 0, 0, 0)
    return pl.pallas_call(
        functools.partial(route_kernel, [first for first, _ in spans], c_at.shape[1]),
        out_shape=[
            jax.ShapeDtypeStruct((steps, groups, pair_rows, lanes), by_c.dtype)
            for _, groups in spans
        ],
        grid_spec=pltpu.PrefetchScalarGridSpec(
            num_scalar_prefetch=2,
            grid=(steps,),
            in_specs=[
                pl.BlockSpec(
                    (c_rows, pair_rows, d_cols), lambda i, c_at, blocks: (blocks[i], 0, 0)
                )
            ],
            out_specs=[
                pl.BlockSpec((1, groups, pair_rows, lanes), at_block if by_block else in_order)
                for _, groups in spans
            ],
        ),
        cost_estimate=takes(0.1 * steps * sum(groups for _, groups in spans)),
        compiler_params=pltpu.CompilerParams(vmem_limit_bytes=VMEM_BYTES),
        name="route_rows",
    )(c_at.reshape(-1), blocks, by_c)


def add_bins(total, bins, own, other, level, other_level, irr_d):
    pair_rows, d_cols = irr_d.shape
    main, tail, pitch = split_lanes(d_cols)

    def one(g, carry):
        def choose(lo, size, at):
            sides = [
                [
                    side[index, g, :, pl.ds(at(h), size)].astype(jnp.float32)
                    for h in range(IRREPS)
                ]
                for side, index in ((own, level), (other, other_level))
            ]
            irr = irr_d[:, lo : lo + size]
            rows = []
            for s in range(IRREPS):
                for side in sides:
                    value = side[s]
                    for j in range(1, IRREPS):
                        value = jnp.where(irr == j, side[s ^ j], value)
                    rows.append(value)
            lhs = jnp.concatenate(rows, axis=0).astype(bins.dtype)
            return jnp.dot(lhs, bins[g, pl.ds(lo, size)], preferred_element_type=jnp.float32)

        sum_ = choose(0, main, lambda h: h * main)
        if tail:
            sum_ += choose(main, tail, lambda h: IRREPS * main + h * pitch)
        total[...] += sum_
        return carry

    lax.fori_loop(0, bins.shape[0], one, 0)


def bins_kernel(places, info, irr_ref, sym_ref, own, near, far, *refs):
    half = near.shape[0]
    bins, (out, total) = refs[:-2], refs[-2:]
    irr_d, sym = irr_ref[...], sym_ref[...]
    total[...] = jnp.zeros_like(total)
    for place, part in zip(places, bins):

        @pl.when((info[place] >= 0) & (info[place] < half))
        def _():
            add_bins(total, part, own, near, info[place], info[place], irr_d)

        @pl.when(info[place] >= half)
        def _():
            add_bins(total, part, own, far, info[place], info[place] - half, irr_d)

    rows = out.shape[0]
    picked = jnp.zeros(out.shape, jnp.float32)
    for s in range(IRREPS):
        picked = jnp.where(sym == s, total[pl.ds(s * rows, rows), :], picked)
    out[...] = picked


def bins_product(places, parts, own, other, info, irr_d, sym):
    pair_rows, ab = irr_d.shape[0], sym.shape[1]
    out = jax.ShapeDtypeStruct((2 * pair_rows, ab), jnp.float32)
    tensors = [irr_d, sym, own, *other, *parts]
    return pl.pallas_call(
        functools.partial(bins_kernel, places),
        out_shape=out,
        grid_spec=pltpu.PrefetchScalarGridSpec(
            num_scalar_prefetch=1,
            grid=(1,),
            in_specs=[whole(x) for x in tensors],
            out_specs=whole(out),
            scratch_shapes=[pltpu.VMEM((IRREPS * 2 * pair_rows, ab), jnp.float32)],
        ),
        cost_estimate=takes(3),
        compiler_params=pltpu.CompilerParams(vmem_limit_bytes=VMEM_BYTES),
        name="bins_product",
    )(info, *tensors)


def left_kernel(c_at, irrep_at, code_ref, amp_ref, integrals, out_ref, rows, arrived):
    sources, groups, pair_rows, _ = amp_ref.shape
    d_cols, ab = code_ref.shape
    main, tail, pitch = split_lanes(d_cols)

    def fetch(i):
        return pltpu.make_async_copy(integrals.at[c_at[i]], rows.at[i], arrived.at[i])

    def start(i, carry):
        fetch(i).start()
        return carry

    lax.fori_loop(0, groups * IRREPS, start, 0)
    out_ref[...] = jnp.zeros_like(out_ref)

    def one(group, carry):
        amps = amp_ref[:, group].astype(jnp.float32)
        amps = amps.reshape(sources * pair_rows, amps.shape[2]).astype(rows.dtype)
        total = jnp.zeros(out_ref.shape, jnp.float32)
        ends = []
        for h in range(IRREPS):
            i = group * IRREPS + h
            fetch(i).wait()
            row = jnp.where(code_ref[...] == irrep_at[i], rows[i].astype(jnp.float32), 0.0)
            total += jnp.dot(
                amps[:, h * main : (h + 1) * main], row[:main].astype(rows.dtype),
                preferred_element_type=jnp.float32,
            )
            ends += [row[main:], jnp.zeros((pitch - tail, ab), jnp.float32)]
        if tail:
            total += jnp.dot(
                amps[:, IRREPS * main :],
                jnp.concatenate([x for x in ends if x.shape[0]], axis=0).astype(rows.dtype),
                preferred_element_type=jnp.float32,
            )
        out_ref[...] += total
        return carry

    lax.fori_loop(0, groups, one, 0)


def left_product(amps, integrals, code, slots, irreps):
    sources, groups, pair_rows, _ = amps.shape
    d_cols, ab = code.shape
    count = groups * IRREPS
    c_at = jnp.maximum(slots - 1, 0)
    irrep_at = jnp.where(slots > 0, irreps, IRREPS)
    out = jax.ShapeDtypeStruct((sources * pair_rows, ab), jnp.float32)
    return pl.pallas_call(
        left_kernel,
        out_shape=out,
        grid_spec=pltpu.PrefetchScalarGridSpec(
            num_scalar_prefetch=2,
            grid=(1,),
            in_specs=[whole(code), whole(amps), pl.BlockSpec(memory_space=pl.ANY)],
            out_specs=whole(out),
            scratch_shapes=[
                pltpu.VMEM((count, d_cols, ab), integrals.dtype),
                pltpu.SemaphoreType.DMA((count,)),
            ],
        ),
        cost_estimate=takes(1.5 * groups),
        compiler_params=pltpu.CompilerParams(vmem_limit_bytes=VMEM_BYTES),
        name="left_product",
    )(c_at, irrep_at, code, amps, integrals)


def body(amplitudes, integrals, orbital_irreps, slab_index):
    c_rows, d_cols, ab_cols = integrals.shape
    pair_rows = amplitudes.shape[0]
    virtual = orbital_irreps.shape[0]
    blocks = lax.axis_size("remap")
    sides = 2
    levels = blocks // sides
    assert levels >= 2 and blocks == levels * sides
    block = lax.axis_index("remap")
    level, side = block // sides, block % sides
    left = LEFT * IRREPS

    irr_blocks = orbital_irreps.reshape(blocks, c_rows)
    earlier = jnp.arange(c_rows)[:, None] < jnp.arange(c_rows)[None, :]
    alike = (irr_blocks[:, :, None] == irr_blocks[:, None, :]) & earlier[None]
    rank = jnp.sum(alike.astype(jnp.int32), axis=1)
    over = rank >= BINS
    left_rank = jnp.sum((over[:, :, None] & earlier[None]).astype(jnp.int32), axis=1)
    left_rounds = (jnp.max(jnp.sum(over.astype(jnp.int32), axis=1)) + left - 1) // left
    key = jnp.where(over, BINS * IRREPS + left_rank, rank * IRREPS + irr_blocks)

    def table(first, count):
        wanted = first + jnp.arange(count, dtype=jnp.int32)
        return first_plus_one(key[:, :, None] == wanted[None, None, :])

    slots = table(0, BINS * IRREPS + left)
    own_slots = lax.dynamic_index_in_dim(slots, block, 0, False)
    own_irr = lax.dynamic_index_in_dim(irr_blocks, block, 0, False)

    irr_d = lax.dynamic_slice_in_dim(orbital_irreps, lax.axis_index("rep") * d_cols, d_cols, 0)
    stride = virtual * virtual // SLABS
    pair_ab = slab_index[0] * stride + jnp.arange(ab_cols, dtype=jnp.int32)
    sym_ab = jnp.bitwise_xor(
        irrep_of(pair_ab // virtual, orbital_irreps), irrep_of(pair_ab % virtual, orbital_irreps)
    )
    code = jnp.bitwise_xor(irr_d[:, None], sym_ab[None, :])
    irr_rows = jnp.broadcast_to(irr_d[None, :], (pair_rows, d_cols))

    order = [1, 0] + list(range(2, levels))

    def at_level(z, a):
        return a if z < levels // 2 else levels - 1 - a

    plan = []
    for z in range(levels):
        for b in range(sides):
            row = [at_level(z, a) * sides + c for c in (1 - b, b) for a in order]
            for t in range(levels):
                for a in (z - t, z + t):
                    row.append(order.index(at_level(z, a)) if 0 <= a < levels else -1)
            plan.append(row)
    info = lax.dynamic_index_in_dim(jnp.asarray(np.array(plan, np.int32)), block, 0, False)

    bins = pack(integrals, code, own_slots[: BINS * IRREPS])
    amplitudes, bins = lax.optimization_barrier((amplitudes, bins))
    by_c = amplitudes.transpose(1, 0, 2)

    def hops(pairs, swap):
        return [
            (a * sides + b, c * sides + (sides - 1 - b if swap else b))
            for a, c in pairs
            for b in range(sides)
        ]

    rounds = [(bins, bins)]
    for t in range(1, levels):
        up = [(z, z + 1) for z in range(t - 1, levels - 1)]
        down = [(levels - 1 - a, levels - 1 - c) for a, c in up]
        rounds.append(
            (
                lax.ppermute(rounds[-1][0], "remap", hops(up, False)),
                lax.ppermute(rounds[-1][1], "remap", hops(down, False)),
            )
        )
    c_at = jnp.maximum(slots - 1, 0)
    in_bins = [(0, BINS)]
    cuts = [(0, LEFT)]
    half = levels // 2
    stay = hops([(z, z) for z in range(levels)], True)
    other = []
    for lo, hi in ((0, half), (half, levels)):
        (cross,) = route(by_c, c_at, info[lo:hi], in_bins, c_rows, False)
        other.append(lax.ppermute(cross, "remap", stay))
    by_c, rounds[1] = lax.optimization_barrier((by_c, rounds[1]))
    (own,) = route(by_c, c_at, info[levels:blocks], in_bins, c_rows, False)
    every = jnp.arange(blocks, dtype=jnp.int32)
    sent = route(
        by_c, c_at, every, [(BINS + first, groups) for first, groups in cuts], c_rows, True
    )
    sent = list(sent)
    sent, rounds[2], other[0] = lax.optimization_barrier((sent, rounds[2], other[0]))
    mine = 0
    for t, parts in enumerate(rounds):
        places = [blocks + 2 * t, blocks + 2 * t + 1]
        if t == 0:
            places, parts = places[:1], parts[:1]
        mine += bins_product(places, parts, own, other, info, irr_rows, sym_ab[None, :])

    def left_term(sent, left_slots):
        arrived = lax.all_to_all(sent, "remap", split_axis=0, concat_axis=0, tiled=True)
        mine = lax.dynamic_index_in_dim(left_slots, block, 0, False)
        at = jnp.arange(1, c_rows + 1, dtype=jnp.int32)
        irreps = jnp.sum(jnp.where(mine[:, None] == at[None, :], own_irr[None, :], 0), axis=1)
        return left_product(arrived, integrals, code, mine, irreps)

    def next_round(index, total):
        left_slots = table(BINS * IRREPS + index * left, left)
        (sent,) = route(
            by_c, jnp.maximum(left_slots - 1, 0), every, [(0, LEFT)], c_rows, True
        )
        return total + left_term(sent, left_slots)

    total = 0
    for (first, _), part in zip(cuts, sent):
        lo = (BINS + first) * IRREPS
        total += left_term(part, slots[:, lo : lo + part.shape[1] * IRREPS])
    total = lax.fori_loop(1, left_rounds, next_round, total)

    total = total.reshape(blocks, pair_rows, ab_cols)
    ids = jnp.arange(blocks)[:, None, None]
    total = total + jnp.where(ids == block, mine[None, :pair_rows], 0.0)
    total = total + jnp.where(ids == level * sides + 1 - side, mine[None, pair_rows:], 0.0)
    return 0.5 * reduce_to_owners(total.reshape(blocks * pair_rows, ab_cols))


def solution(mesh):
    in_specs = (P("remap", None, "rep"), P("remap", "rep", None), P(), P())
    out_specs = P("remap", "rep")
    return jax.shard_map(body, mesh=mesh, in_specs=in_specs, out_specs=out_specs, check_vma=False)
```

time: 219 us -> 156 us (0.71)
  waiting for transfers between devices: 134 us -> 50.5 us
  Pallas kernels: 0 us -> 51.2 us
  local copies, waits for them, and re-layouts: 44.8 us -> 17 us
  starting transfers between devices: 7.28 us -> 18.2 us
  matrix products: 7.76 us -> 0 us
  other arithmetic: 12.3 us -> 4.91 us
    all_to_all x1, waiting for transfers between devices: 134 us -> 0.01 us  [left_term(): lax.all_to_all(sent, 'remap', split_axis=0, concat_axis=0, tiled=True)]
    pallas_call x0 -> x10, Pallas kernels: none -> 51.2 us  [the longest x4 19 us: route(): pl.pallas_call(functools.partial(route_kernel, [first for first, _ in spa...]
    ppermute x0 -> x8, waiting for transfers between devices: none -> 50.5 us  [the longest x2 38.3 us: body(): other.append(lax.ppermute(cross, 'remap', stay))]
    reshape x4 -> x0, local copies, waits for them, and re-layouts: 25.7 us -> none  [the longest x1 15.4 us: body(): jnp.where(allowed, integrals, jnp.zeros((), jnp.bfloat16))]
    ppermute x0 -> x8, starting transfers between devices: none -> 13.8 us  [the longest x3 6.39 us: body(): lax.ppermute(rounds[-1][0], 'remap', hops(up, False))]
    optimization_barrier x0 -> x1, local copies, waits for them, and re-layouts: none -> 10.9 us  [body(): amplitudes, bins = lax.optimization_barrier((amplitudes, bins))]
    select_n x1 -> x3, other arithmetic: 10.6 us -> 0.02 us  [the longest x1 0.01 us: pack(): irrep_at = jnp.where(slots > 0, irrep, IRREPS)]
    unnamed x5 -> x14, local copies, waits for them, and re-layouts: 11.1 us -> 2.68 us
  transfers between devices with their start and end apart: 1 -> 9, of which waited for: 1 -> 5; matrix products, arithmetic and copies ran while one was open for 12% -> 8% of each run, Pallas kernels for 0% -> 21%
where the time goes in v2:
time: 156 us; the launch traced here: 155 us
  Pallas kernels  51.2 us (33%)
  waiting for transfers between devices  50.5 us (32%)
  starting transfers between devices  18.2 us (12%)
  local copies, waits for them, and re-layouts  17 us (11%)
  blocking collectives  11.6 us (7%)
  other arithmetic  4.91 us (3%)
  between operations  1.74 us (1%)
    ppermute x2, waiting for transfers between devices, body(): other.append(lax.ppermute(cross, 'remap', stay))  38.3 us
    pallas_call x4, Pallas kernels, route(): pl.pallas_call(functools.partial(route_kernel, [first for first, _ in spa...  19 us
    pallas_call x1, Pallas kernels, left_product(): pl.pallas_call(left_kernel, out_shape=out, grid_spec=pltpu.PrefetchScalar...  14 us
    pallas_call x4, Pallas kernels, bins_product(): pl.pallas_call(functools.partial(bins_kernel, places), out_shape=out, gri...  13.9 us
    ppermute x3, waiting for transfers between devices, body(): lax.ppermute(rounds[-1][1], 'remap', hops(down, False))  12.2 us
    all_to_all x1, blocking collectives, reduce_to_owners(): lax.all_to_all(blocks, ('remap', 'rep'), split_axis=0, concat_axis=0, til...  11.6 us
    optimization_barrier x1, local copies, waits for them, and re-layouts, body(): amplitudes, bins = lax.optimization_barrier((amplitudes, bins))  10.9 us
    ppermute x3, starting transfers between devices, body(): lax.ppermute(rounds[-1][0], 'remap', hops(up, False))  6.39 us
  transfers between devices with their start and end apart: 9, of which 5 were waited for; matrix products, arithmetic and copies ran while one was open for 8% of the time, Pallas kernels for 21%

profile of v2, /device:TPU:0, one launch (start us, length us, event | category | flops | bytes accessed | tf_op | source)
XLA Modules:
  0.0 155.2 jit_solution(16251491772285411875)
XLA Ops:
  0.0 0.8 eq.148
  1.8 0.8 select_reduce_fusion.2
  3.4 0.8 dynamic_slice.29
  4.2 0.9 select_reduce_fusion.3
  5.2 4.2 %pack_bins.1.refs_0_ = bf16[10,304,128]{2,1,0:T(8,128)(2,1)S(1)} custom-call(s32[80]{0:T(128)S(1)} %maximum_bitcast_fusion.c_at, s32[80]{0:T(128)S(1)} %bitcast_select_fusion.irrep_at, s32[300,128]{1,0:T(8,128)S(1)} %broadcast_xor_fusion.1.code_ref, bf16[150,300,128]{2,1,0:T(8,128)(2,1)} %integrals.3), custom_call_target="tpu_custom_call" | custom-call | bytes 14400000 | tf_op jit(solution)/shard_map/pack_bins/pallas_call | solution.py:86
  9.4 5.0 %collective-permute-start = (bf16[10,304,128]{2,1,0:T(8,128)(2,1)S(1)}, bf16[10,304,128]{2,1,0:T(8,128)(2,1)S(1)}, u32[]{:S(2)}, u32[]{:S(2)}) collective-permute-start(bf16[10,304,128]{2,1,0:T(8,128)(2,1)S(1)} %pack_bins.1.refs_0_), channel_id=1, source_target_pairs={{0,8},{4,12},{8,16},{12,20},{16,24},{20,28},{1,9},{5,13},{9,17},{1... | collective-permute-start | bytes 2334728 | tf_op jit(solution)/shard_map/ppermute | solution.py:369
  14.4 1.3 collective-permute-start.1
  15.8 10.9 %copy.10 = bf16[8,1200,300]{2,0,1:T(8,128)(2,1)} copy(bf16[8,1200,300]{1,0,2:T(8,128)(2,1)} %param.7) | data formatting | bytes 11520000 | tf_op jit(solution)/shard_map/optimization_barrier | solution.py:353
  27.5 3.7 %route_rows.10 = bf16[2,10,8,2432]{3,2,1,0:T(8,128)(2,1)S(1)} custom-call(s32[1216]{0:T(1024)S(1)} %max.35.c_at, s32[2]{0:T(128)S(1)} %get-tuple-element.248.blocks, bf16[1200,8,300]{2,1,0:T(8,128)(2,1)} %bitcast.27), custom_call_target="tpu_custom_call" | custom-call | bytes 7200000 | tf_op jit(solution)/shard_map/route_rows/pallas_call | solution.py:132
  31.1 1.6 %collective-permute-start.4 = (bf16[2,10,8,2432]{3,2,1,0:T(8,128)(2,1)S(1)}, bf16[2,10,8,2432]{3,2,1,0:T(8,128)(2,1)S(1)}, u32[]{:S(2)}, u32[]{:S(2)}) collective-permute-start(bf16[2,10,8,2432]{3,2,1,0:T(8,128)(2,1)S(1)} %route_rows.10), channel_id=1, source_target_pairs={{0,4},{4,0},{8,12},{12,8},{16,20},{20,16},{24,28},{28,24},{1,5},{5... | collective-permute-start | bytes 2334728 | tf_op jit(solution)/shard_map/ppermute | solution.py:381
  33.4 1.8 %collective-permute-done.1.refs_1_ = bf16[10,304,128]{2,1,0:T(8,128)(2,1)} collective-permute-done((bf16[10,304,128]{2,1,0:T(8,128)(2,1)S(1)}, bf16[10,304,128]{2,1,0:T(8,128)(2,1)}, u32[]{:S(2)}, u32[]{:S(2)}) %collective-permute-start.1) | collective-permute-done | bytes 778272 | tf_op jit(solution)/shard_map/ppermute | solution.py:370
  35.3 1.3 collective-permute-start.3
  36.6 6.4 %route_rows.9 = bf16[8,9,8,2432]{3,2,1,0:T(8,128)(2,1)S(1)} custom-call(s32[1216]{0:T(1024)S(1)} %max.35.c_at, s32[8]{0:T(128)S(1)} %iota.85.blocks, bf16[1200,8,300]{2,1,0:T(8,128)(2,1)S(1)} %bitcast.31), custom_call_target="tpu_custom_call" | custom-call | bytes 25920000 | tf_op jit(solution)/shard_map/route_rows/pallas_call | solution.py:132
  43.0 1.6 %copy-done.1 = bf16[8,9,8,2432]{3,2,1,0:T(8,128)(2,1)} copy-done((bf16[8,9,8,2432]{3,2,1,0:T(8,128)(2,1)}, bf16[8,9,8,2432]{3,2,1,0:T(8,128)(2,1)S(1)}, u32[]{:S(2)}) %copy-start.1) | copy-done | bytes 2801688
  44.6 5.4 %collective-permute-done.4.near = bf16[2,10,8,2432]{3,2,1,0:T(8,128)(2,1)S(1)} collective-permute-done((bf16[2,10,8,2432]{3,2,1,0:T(8,128)(2,1)S(1)}, bf16[2,10,8,2432]{3,2,1,0:T(8,128)(2,1)S(1)}, u32[]{:S(2)}, u32[]{:S(2)}) %collective-permute-start.4) | collective-permute-done | bytes 778272 | tf_op jit(solution)/shard_map/ppermute | solution.py:381
  50.0 0.9 copy-done.4
  50.9 6.4 %collective-permute-done.3.refs_1_ = bf16[10,304,128]{2,1,0:T(8,128)(2,1)} collective-permute-done((bf16[10,304,128]{2,1,0:T(8,128)(2,1)}, bf16[10,304,128]{2,1,0:T(8,128)(2,1)}, u32[]{:S(2)}, u32[]{:S(2)}) %collective-permute-start.3) | collective-permute-done | bytes 778272 | tf_op jit(solution)/shard_map/ppermute | solution.py:370
  57.3 4.4 %all-to-all-start.1 = ((bf16[8,9,8,2432]{3,2,1,0:T(8,128)(2,1)}), bf16[8,9,8,2432]{3,2,1,0:T(8,128)(2,1)}, u32[]{:S(2)}, u32[]{:S(2)}) async-start(bf16[8,9,8,2432]{3,2,1,0:T(8,128)(2,1)} %copy-done.1), calls=%async_computation.1 | async-start | bytes 5603328 | tf_op jit(solution)/shard_map/all_to_all | solution.py:398
  61.7 3.4 %route_rows.12 = bf16[2,10,8,2432]{3,2,1,0:T(8,128)(2,1)S(1)} custom-call(s32[1216]{0:T(1024)S(1)} %max.35.c_at, s32[2]{0:T(128)S(1)} %get-tuple-element.247.blocks, bf16[1200,8,300]{2,1,0:T(8,128)(2,1)} %bitcast.28), custom_call_target="tpu_custom_call" | custom-call | bytes 7200000 | tf_op jit(solution)/shard_map/route_rows/pallas_call | solution.py:132
  65.2 2.0 %collective-permute-start.5 = (bf16[2,10,8,2432]{3,2,1,0:T(8,128)(2,1)S(1)}, bf16[2,10,8,2432]{3,2,1,0:T(8,128)(2,1)S(1)}, u32[]{:S(2)}, u32[]{:S(2)}) collective-permute-start(bf16[2,10,8,2432]{3,2,1,0:T(8,128)(2,1)S(1)} %route_rows.12), channel_id=1, source_target_pairs={{0,4},{4,0},{8,12},{12,8},{16,20},{20,16},{24,28},{28,24},{1,5},{5... | collective-permute-start | bytes 2334728 | tf_op jit(solution)/shard_map/ppermute | solution.py:381
  68.5 0.7 collective-permute-start.6
  69.3 1.3 collective-permute-start.7
  70.8 5.5 %route_rows.11.own = bf16[4,10,8,2432]{3,2,1,0:T(8,128)(2,1)S(1)} custom-call(s32[1216]{0:T(1024)S(1)} %max.35.c_at, s32[4]{0:T(128)S(1)} %slice_bitcast_fusion.1.blocks, bf16[1200,8,300]{2,1,0:T(8,128)(2,1)} %bitcast.29), custom_call_target="tpu_custom_call" | custom-call | bytes 14400000 | tf_op jit(solution)/shard_map/route_rows/pallas_call | solution.py:132
  76.3 32.8 %collective-permute-done.5.far = bf16[2,10,8,2432]{3,2,1,0:T(8,128)(2,1)S(1)} collective-permute-done((bf16[2,10,8,2432]{3,2,1,0:T(8,128)(2,1)S(1)}, bf16[2,10,8,2432]{3,2,1,0:T(8,128)(2,1)S(1)}, u32[]{:S(2)}, u32[]{:S(2)}) %collective-permute-start.5) | collective-permute-done | bytes 778272 | tf_op jit(solution)/shard_map/ppermute | solution.py:381
  109.2 2.9 %bins_product.4 = f32[16,128]{1,0:T(8,128)S(1)} custom-call(s32[16]{0:T(128)S(1)} %get-tuple-element.245.info, s32[8,300]{1,0:T(8,128)S(1)} %broadcast_in_dim.175.irr_ref, s32[1,128]{1,0:T(1,128)S(1)} %bitcast.33, bf16[4,10,8,2432]{3,2,1,0:T(8,128)(2,1)S(1)} %route_rows.11.own, bf16[2,10,8,2432]{3,2,1,0:T(8,128)(2,1)S(1)} %collective-permute-done.4.near, ...), custom_call_target="tpu_custom_call" | custom-call | bytes 10800000 | tf_op jit(solution)/shard_map/bins_product/pallas_call | solution.py:216
  112.1 4.0 %bins_product.6 = f32[16,128]{1,0:T(8,128)S(1)} custom-call(s32[16]{0:T(128)S(1)} %get-tuple-element.245.info, s32[8,300]{1,0:T(8,128)S(1)} %broadcast_in_dim.175.irr_ref, s32[1,128]{1,0:T(1,128)S(1)} %bitcast.34, bf16[4,10,8,2432]{3,2,1,0:T(8,128)(2,1)S(1)} %route_rows.11.own, bf16[2,10,8,2432]{3,2,1,0:T(8,128)(2,1)S(1)} %collective-permute-done.4.near, ...), custom_call_target="tpu_custom_call" | custom-call | bytes 10800000 | tf_op jit(solution)/shard_map/bins_product/pallas_call | solution.py:216
  116.2 4.0 %bins_product.5 = f32[16,128]{1,0:T(8,128)S(1)} custom-call(s32[16]{0:T(128)S(1)} %get-tuple-element.245.info, s32[8,300]{1,0:T(8,128)S(1)} %broadcast_in_dim.175.irr_ref, s32[1,128]{1,0:T(1,128)S(1)} %bitcast.35, bf16[4,10,8,2432]{3,2,1,0:T(8,128)(2,1)S(1)} %route_rows.11.own, bf16[2,10,8,2432]{3,2,1,0:T(8,128)(2,1)S(1)} %collective-permute-done.4.near, ...), custom_call_target="tpu_custom_call" | custom-call | bytes 10800000 | tf_op jit(solution)/shard_map/bins_product/pallas_call | solution.py:216
  120.2 4.0 %collective-permute-done.7.refs_1_ = bf16[10,304,128]{2,1,0:T(8,128)(2,1)S(1)} collective-permute-done((bf16[10,304,128]{2,1,0:T(8,128)(2,1)}, bf16[10,304,128]{2,1,0:T(8,128)(2,1)S(1)}, u32[]{:S(2)}, u32[]{:S(2)}) %collective-permute-start.7) | collective-permute-done | bytes 778272 | tf_op jit(solution)/shard_map/ppermute | solution.py:370
  124.2 2.9 %bins_product.7 = f32[16,128]{1,0:T(8,128)S(1)} custom-call(s32[16]{0:T(128)S(1)} %get-tuple-element.245.info, s32[8,300]{1,0:T(8,128)S(1)} %broadcast_in_dim.175.irr_ref, s32[1,128]{1,0:T(1,128)S(1)} %bitcast.36, bf16[4,10,8,2432]{3,2,1,0:T(8,128)(2,1)S(1)} %route_rows.11.own, bf16[2,10,8,2432]{3,2,1,0:T(8,128)(2,1)S(1)} %collective-permute-done.4.near, ...), custom_call_target="tpu_custom_call" | custom-call | bytes 10800000 | tf_op jit(solution)/shard_map/bins_product/pallas_call | solution.py:216
  127.2 14.0 %left_product.6 = f32[64,128]{1,0:T(8,128)S(1)} custom-call(s32[72]{0:T(128)S(1)} %get-tuple-element.237.c_at, s32[72]{0:T(128)S(1)} %compare_select_fusion.1.irrep_at, s32[300,128]{1,0:T(8,128)S(1)} %broadcast_xor_fusion.1.code_ref, bf16[8,9,8,2432]{3,2,1,0:T(8,128)(2,1)} %all-to-all-done.1.amp_ref, bf16[150,300,128]{2,1,0:T(8,128)(2,1)} %integrals.3), custom_call_target="tpu_custom_call" | custom-call | bytes 48600000 | tf_op jit(solution)/shard_map/left_product/pallas_call | solution.py:280
  141.6 11.6 %all_to_all.17 = f32[32,1,256]{2,1,0:T(1,128)S(1)} all-to-all(f32[32,1,256]{2,1,0:T(1,128)S(1)} %reshape.140), channel_id=1, replica_groups=mesh['remap'=8,'rep'=4] {'remap','rep'}, dimensions={0} | all-to-all | bytes 65536 | tf_op jit(solution)/shard_map/all_to_all | solution.py:29
  153.7 0.7 reduce
  (54 shorter events, 5.3 us)
Async XLA Ops:
  9.4 23.3 %collective-permute-start = (bf16[10,304,128]{2,1,0:T(8,128)(2,1)S(1)}, bf16[10,304,128]{2,1,0:T(8,128)(2,1)S(1)}, u32[]{:S(2)}, u32[]{:S(2)}) collective-permute-start(bf16[10,304,128]{2,1,0:T(8,128)(2,1)S(1)} %pack_bins.1.refs_0_), channel_id=1, source_target_pairs={{0,8},{4,12},{8,16},{12,20},{16,24},{20,28},{1,9},{5,13},{9,17},{1... | collective-permute-start | bytes 2334728 | tf_op jit(solution)/shard_map/ppermute | solution.py:369
  14.4 20.8 %collective-permute-start.1 = (bf16[10,304,128]{2,1,0:T(8,128)(2,1)S(1)}, bf16[10,304,128]{2,1,0:T(8,128)(2,1)}, u32[]{:S(2)}, u32[]{:S(2)}) collective-permute-start(bf16[10,304,128]{2,1,0:T(8,128)(2,1)S(1)} %pack_bins.1.refs_0_), channel_id=1, source_target_pairs={{24,16},{28,20},{16,8},{20,12},{8,0},{12,4},{25,17},{29,21},{17,9}... | collective-permute-start | bytes 2334728 | tf_op jit(solution)/shard_map/ppermute | solution.py:370
  27.5 9.1 %copy-start.6 = (bf16[8,1200,300]{2,0,1:T(8,128)(2,1)S(1)}, bf16[8,1200,300]{2,0,1:T(8,128)(2,1)}, u32[]{:S(2)}) copy-start(bf16[8,1200,300]{2,0,1:T(8,128)(2,1)} %copy.10) | copy-start | bytes 17280004
  31.1 18.9 %collective-permute-start.4 = (bf16[2,10,8,2432]{3,2,1,0:T(8,128)(2,1)S(1)}, bf16[2,10,8,2432]{3,2,1,0:T(8,128)(2,1)S(1)}, u32[]{:S(2)}, u32[]{:S(2)}) collective-permute-start(bf16[2,10,8,2432]{3,2,1,0:T(8,128)(2,1)S(1)} %route_rows.10), channel_id=1, source_target_pairs={{0,4},{4,0},{8,12},{12,8},{16,20},{20,16},{24,28},{28,24},{1,5},{5... | collective-permute-start | bytes 2334728 | tf_op jit(solution)/shard_map/ppermute | solution.py:381
  32.7 10.3 %copy-start.2 = (bf16[10,304,128]{2,1,0:T(8,128)(2,1)}, bf16[10,304,128]{2,1,0:T(8,128)(2,1)S(1)}, u32[]{:S(2)}) copy-start(bf16[10,304,128]{2,1,0:T(8,128)(2,1)S(1)} %collective-permute-done.refs_0_) | copy-start | bytes 2334724
  32.7 17.3 %collective-permute-start.2 = (bf16[10,304,128]{2,1,0:T(8,128)(2,1)S(1)}, bf16[10,304,128]{2,1,0:T(8,128)(2,1)S(1)}, u32[]{:S(2)}, u32[]{:S(2)}) collective-permute-start(bf16[10,304,128]{2,1,0:T(8,128)(2,1)S(1)} %collective-permute-done.refs_0_), channel_id=1, source_target_pairs={{8,16},{12,20},{16,24},{20,28},{9,17},{13,21},{17,25},{21,29},{10,... | collective-permute-start | bytes 2334728 | tf_op jit(solution)/shard_map/ppermute | solution.py:369
  35.3 22.1 %collective-permute-start.3 = (bf16[10,304,128]{2,1,0:T(8,128)(2,1)}, bf16[10,304,128]{2,1,0:T(8,128)(2,1)}, u32[]{:S(2)}, u32[]{:S(2)}) collective-permute-start(bf16[10,304,128]{2,1,0:T(8,128)(2,1)} %collective-permute-done.1.refs_1_), channel_id=1, source_target_pairs={{16,8},{20,12},{8,0},{12,4},{17,9},{21,13},{9,1},{13,5},{18,10},{2... | collective-permute-start | bytes 2334728 | tf_op jit(solution)/shard_map/ppermute | solution.py:370
  43.0 1.6 %copy-start.1 = (bf16[8,9,8,2432]{3,2,1,0:T(8,128)(2,1)}, bf16[8,9,8,2432]{3,2,1,0:T(8,128)(2,1)S(1)}, u32[]{:S(2)}) copy-start(bf16[8,9,8,2432]{3,2,1,0:T(8,128)(2,1)S(1)} %route_rows.9) | copy-start | bytes 8404996
  50.0 0.9 copy-start.4
  57.3 69.9 %all-to-all-start.1 = ((bf16[8,9,8,2432]{3,2,1,0:T(8,128)(2,1)}), bf16[8,9,8,2432]{3,2,1,0:T(8,128)(2,1)}, u32[]{:S(2)}, u32[]{:S(2)}) async-start(bf16[8,9,8,2432]{3,2,1,0:T(8,128)(2,1)} %copy-done.1), calls=%async_computation.1 | async-start | bytes 5603328 | tf_op jit(solution)/shard_map/all_to_all | solution.py:398
  65.2 44.0 %collective-permute-start.5 = (bf16[2,10,8,2432]{3,2,1,0:T(8,128)(2,1)S(1)}, bf16[2,10,8,2432]{3,2,1,0:T(8,128)(2,1)S(1)}, u32[]{:S(2)}, u32[]{:S(2)}) collective-permute-start(bf16[2,10,8,2432]{3,2,1,0:T(8,128)(2,1)S(1)} %route_rows.12), channel_id=1, source_target_pairs={{0,4},{4,0},{8,12},{12,8},{16,20},{20,16},{24,28},{28,24},{1,5},{5... | collective-permute-start | bytes 2334728 | tf_op jit(solution)/shard_map/ppermute | solution.py:381
  68.5 51.7 %collective-permute-start.6 = (bf16[10,304,128]{2,1,0:T(8,128)(2,1)}, bf16[10,304,128]{2,1,0:T(8,128)(2,1)S(1)}, u32[]{:S(2)}, u32[]{:S(2)}) collective-permute-start(bf16[10,304,128]{2,1,0:T(8,128)(2,1)} %copy-done.4), channel_id=1, source_target_pairs={{16,24},{20,28},{17,25},{21,29},{18,26},{22,30},{19,27},{23,31}} | collective-permute-start | bytes 2334728 | tf_op jit(solution)/shard_map/ppermute | solution.py:369
  69.3 55.0 %collective-permute-start.7 = (bf16[10,304,128]{2,1,0:T(8,128)(2,1)}, bf16[10,304,128]{2,1,0:T(8,128)(2,1)S(1)}, u32[]{:S(2)}, u32[]{:S(2)}) collective-permute-start(bf16[10,304,128]{2,1,0:T(8,128)(2,1)} %collective-permute-done.3.refs_1_), channel_id=1, source_target_pairs={{8,0},{12,4},{9,1},{13,5},{10,2},{14,6},{11,3},{15,7}} | collective-permute-start | bytes 2334728 | tf_op jit(solution)/shard_map/ppermute | solution.py:370
  109.2 2.9 %copy-start.5 = (bf16[10,304,128]{2,1,0:T(8,128)(2,1)S(1)}, bf16[10,304,128]{2,1,0:T(8,128)(2,1)}, u32[]{:S(2)}) copy-start(bf16[10,304,128]{2,1,0:T(8,128)(2,1)} %copy-done.4) | copy-start | bytes 2334724
  112.1 4.1 %copy-start.3 = (bf16[10,304,128]{2,1,0:T(8,128)(2,1)S(1)}, bf16[10,304,128]{2,1,0:T(8,128)(2,1)}, u32[]{:S(2)}) copy-start(bf16[10,304,128]{2,1,0:T(8,128)(2,1)} %copy-done.2) | copy-start | bytes 2334724

commit v3 on v2

v3 whole, which is shorter than its diff:
```python
import functools

import jax
import jax.numpy as jnp
import numpy as np
from jax import lax
from jax.experimental import pallas as pl
from jax.experimental.pallas import tpu as pltpu
from jax.sharding import PartitionSpec as P

SLABS = 64
IRREPS = 8
BINS = 10
LEFT = 9
VMEM_BYTES = 48 * 1024 * 1024
BYTES_A_US = 3_600_000


def irrep_of(indices, table):
    matches = indices[:, None] == jnp.arange(table.shape[0], dtype=jnp.int32)[None, :]
    return jnp.sum(jnp.where(matches, table[None, :], 0), axis=1)


def sum_kernel(parts_ref, out_ref):
    rows, cols = out_ref.shape
    total = jnp.sum(parts_ref[...], axis=0)
    out_ref[...] = jnp.concatenate(
        [total[:, r * cols : (r + 1) * cols] for r in range(rows)], axis=0
    )


def reduce_to_owners(partial_term):
    remap, rep = lax.axis_size("remap"), lax.axis_size("rep")
    rows, cols = partial_term.shape
    blocks = partial_term.reshape(remap, rows // remap, rep, cols // rep)
    blocks = blocks.transpose(0, 2, 1, 3).reshape(remap * rep, 1, -1)
    arrived = lax.all_to_all(blocks, ("remap", "rep"), split_axis=0, concat_axis=0, tiled=True)
    return pl.pallas_call(
        sum_kernel,
        out_shape=jax.ShapeDtypeStruct((rows // remap, cols // rep), jnp.float32),
        name="sum_parts",
    )(arrived)


def first_plus_one(match):
    c_plus_one = jnp.arange(1, match.shape[1] + 1, dtype=jnp.int32)
    return jnp.sum(jnp.where(match, c_plus_one[None, :, None], 0), axis=1)


def takes(us):
    return pl.CostEstimate(flops=0, bytes_accessed=int(us * BYTES_A_US), transcendentals=0)


def whole(array):
    zeros = (0,) * array.ndim
    return pl.BlockSpec(array.shape, lambda *_: zeros)


def split_lanes(d_cols):
    main = d_cols // 128 * 128
    tail = d_cols - main
    pitch = -(-tail // 16) * 16
    return main, tail, pitch


def pack_kernel(irreps, slab, integrals, out_ref, rows, code_ref, counts, arrived):
    c_rows, d_cols, ab = integrals.shape
    bins = out_ref.shape[0]
    virtual = irreps.shape[0]

    def fetch(c, i):
        return pltpu.make_async_copy(integrals.at[c], rows.at[i], arrived.at[i])

    for h in range(IRREPS):
        counts[h] = 0
    c_first = lax.axis_index("remap") * c_rows

    def place(c, carry):
        h = irreps[c_first + c]
        g = counts[h]
        counts[h] = g + 1

        @pl.when(g < bins)
        def _():
            fetch(c, g * IRREPS + h).start()

        return carry

    lax.fori_loop(0, c_rows, place, 0, unroll=15)

    pair = slab[0] * (virtual * virtual // SLABS)
    a_first = pair // virtual
    b_first = pair - a_first * virtual
    lane = lax.broadcasted_iota(jnp.int32, (1, ab), 1)

    def symmetry(k, sym):
        over = (b_first + k >= virtual).astype(jnp.int32)
        value = irreps[a_first + over] ^ irreps[b_first + k - over * virtual]
        return jnp.where(lane == k, value, sym)

    sym = lax.fori_loop(0, ab, symmetry, jnp.zeros((1, ab), jnp.int32), unroll=32)
    d_first = lax.axis_index("rep") * d_cols

    def code_row(d, carry):
        code_ref[pl.ds(d, 1), :] = sym ^ irreps[d_first + d]
        return carry

    lax.fori_loop(0, d_cols, code_row, 0, unroll=50)

    code = code_ref[...].astype(jnp.float32).astype(rows.dtype)

    def one(g, carry):
        for h in range(IRREPS):
            i = g * IRREPS + h

            @pl.when(g < counts[h])
            def _():
                fetch(0, i).wait()

            @pl.when(g >= counts[h])
            def _():
                rows[i] = jnp.zeros((d_cols, ab), rows.dtype)

        total = rows[g * IRREPS]
        for h in range(1, IRREPS):
            total = jnp.where(code == h, rows[g * IRREPS + h], total)
        out_ref[g, pl.ds(0, d_cols)] = total
        return carry

    lax.fori_loop(0, bins, one, 0)


def pack(integrals, irreps, slab):
    _, d_cols, ab = integrals.shape
    padded = -(-d_cols // 16) * 16
    out = jax.ShapeDtypeStruct((BINS, padded, ab), integrals.dtype)
    return pl.pallas_call(
        pack_kernel,
        out_shape=out,
        grid_spec=pltpu.PrefetchScalarGridSpec(
            num_scalar_prefetch=2,
            grid=(1,),
            in_specs=[pl.BlockSpec(memory_space=pl.ANY)],
            out_specs=whole(out),
            scratch_shapes=[
                pltpu.VMEM((BINS * IRREPS, d_cols, ab), integrals.dtype),
                pltpu.VMEM((d_cols, ab), jnp.int32),
                pltpu.SMEM((IRREPS,), jnp.int32),
                pltpu.SemaphoreType.DMA((BINS * IRREPS,)),
            ],
        ),
        cost_estimate=takes(4),
        compiler_params=pltpu.CompilerParams(vmem_limit_bytes=VMEM_BYTES),
        name="pack_bins",
    )(irreps, slab, integrals)


def route_kernel(firsts, width, c_at, blocks, rows_ref, *outs):
    base = blocks[pl.program_id(0)] * width
    pair_rows, d_cols = rows_ref.shape[1:]
    main, tail, pitch = split_lanes(d_cols)
    for first, out in zip(firsts, outs):

        def one(group, carry):
            tails = []
            for i in range(IRREPS):
                at = c_at[base + (first + group) * IRREPS + i]
                out[0, group, :, pl.ds(i * main, main)] = rows_ref[at, :, pl.ds(0, main)]
                end = rows_ref[at, :, pl.ds(main, tail)].astype(jnp.float32)
                tails += [end, jnp.zeros((pair_rows, pitch - tail), jnp.float32)]
            ends = jnp.concatenate([x for x in tails if x.shape[1]], axis=1)
            out[0, group, :, pl.ds(IRREPS * main, IRREPS * pitch)] = ends.astype(out.dtype)
            return carry

        lax.fori_loop(0, out.shape[1], one, 0)


def route(by_c, c_at, blocks, spans, c_rows, by_block):
    pair_rows, d_cols = by_c.shape[1:]
    steps = blocks.shape[0]
    main, _, pitch = split_lanes(d_cols)
    lanes = IRREPS * (main + pitch)
    at_block = lambda i, c_at, blocks: (blocks[i], 0, 0, 0)
    in_order = lambda i, c_at, blocks: (i, 0, 0, 0)
    return pl.pallas_call(
        functools.partial(route_kernel, [first for first, _ in spans], c_at.shape[1]),
        out_shape=[
            jax.ShapeDtypeStruct((steps, groups, pair_rows, lanes), by_c.dtype)
            for _, groups in spans
        ],
        grid_spec=pltpu.PrefetchScalarGridSpec(
            num_scalar_prefetch=2,
            grid=(steps,),
            in_specs=[
                pl.BlockSpec(
                    (c_rows, pair_rows, d_cols), lambda i, c_at, blocks: (blocks[i], 0, 0)
                )
            ],
            out_specs=[
                pl.BlockSpec((1, groups, pair_rows, lanes), at_block if by_block else in_order)
                for _, groups in spans
            ],
        ),
        cost_estimate=takes(0.1 * steps * sum(groups for _, groups in spans)),
        compiler_params=pltpu.CompilerParams(vmem_limit_bytes=VMEM_BYTES),
        name="route_rows",
    )(c_at.reshape(-1), blocks, by_c)


def chosen_rows(g, lo, size, own, other, level, other_level, irr_d, dtype):
    main, _, pitch = split_lanes(irr_d.shape[1])

    def lane(h):
        return h * main if lo < main else IRREPS * main + h * pitch

    sides = [
        [side[at, g, :, pl.ds(lane(h), size)].astype(jnp.float32) for h in range(IRREPS)]
        for side, at in ((own, level), (other, other_level))
    ]
    irr = irr_d[:, lo : lo + size]
    rows = []
    for s in range(IRREPS):
        for side in sides:
            value = side[s]
            for j in range(1, IRREPS):
                value = jnp.where(irr == j, side[s ^ j], value)
            rows.append(value)
    return jnp.concatenate(rows, axis=0).astype(dtype)


def spans_of(d_cols):
    main, tail, _ = split_lanes(d_cols)
    return [(0, main), (main, tail)] if tail else [(0, main)]


def add_bins(total, bins, own, other, level, other_level, irr_d):
    def one(g, carry):
        sum_ = total[...]
        for lo, size in spans_of(irr_d.shape[1]):
            lhs = chosen_rows(g, lo, size, own, other, level, other_level, irr_d, bins.dtype)
            sum_ += jnp.dot(lhs, bins[g, pl.ds(lo, size)], preferred_element_type=jnp.float32)
        total[...] = sum_
        return carry

    lax.fori_loop(0, bins.shape[0], one, 0)


def pick_symmetry(total, sym, rows):
    picked = jnp.zeros((rows, total.shape[1]), jnp.float32)
    for s in range(IRREPS):
        picked = jnp.where(sym == s, total[pl.ds(s * rows, rows), :], picked)
    return picked


def choose_kernel(places, n_other, info, irr_ref, own, *refs):
    others, out = refs[:n_other], refs[n_other]
    irr_d = irr_ref[...]
    level, first = jnp.maximum(info[places[0]], info[places[1]]), 0
    for other in others:
        last = first + other.shape[0]

        @pl.when((level >= first) & (level < last))
        def _():
            def one(g, carry):
                for lo, size in spans_of(irr_d.shape[1]):
                    out[g, :, pl.ds(lo, size)] = chosen_rows(
                        g, lo, size, own, other, level, level - first, irr_d, out.dtype
                    )
                return carry

            lax.fori_loop(0, out.shape[0], one, 0)

        first = last


def choose(places, own, other, info, irr_d):
    pair_rows, d_cols = irr_d.shape
    tensors = [irr_d, own, *other]
    return pl.pallas_call(
        functools.partial(choose_kernel, places, len(other)),
        out_shape=jax.ShapeDtypeStruct((BINS, IRREPS * 2 * pair_rows, d_cols), own.dtype),
        grid_spec=pltpu.PrefetchScalarGridSpec(
            num_scalar_prefetch=1,
            grid=(1,),
            in_specs=[pl.BlockSpec(memory_space=pltpu.VMEM)] * len(tensors),
            out_specs=pl.BlockSpec(memory_space=pltpu.VMEM),
        ),
        cost_estimate=takes(3),
        compiler_params=pltpu.CompilerParams(vmem_limit_bytes=VMEM_BYTES // 3),
        name="choose_rows",
    )(info, *tensors)


def last_kernel(places, info, sym_ref, chosen, *refs):
    bins, (out, total) = refs[:2], refs[2:]
    total[...] = jnp.zeros_like(total)
    for place, part in zip(places, bins):

        @pl.when(info[place] >= 0)
        def _():
            sum_ = jnp.zeros(total.shape, jnp.float32)
            for g in range(part.shape[0]):
                sum_ += jnp.dot(
                    chosen[g], part[g, pl.ds(0, chosen.shape[2])],
                    preferred_element_type=jnp.float32,
                )
            total[...] = sum_

    out[...] = pick_symmetry(total, sym_ref[...], out.shape[0])


def last_product(places, parts, chosen, info, sym):
    rows, ab = chosen.shape[1], sym.shape[1]
    out = jax.ShapeDtypeStruct((rows // IRREPS, ab), jnp.float32)
    tensors = [sym, chosen, *parts]
    return pl.pallas_call(
        functools.partial(last_kernel, places),
        out_shape=out,
        grid_spec=pltpu.PrefetchScalarGridSpec(
            num_scalar_prefetch=1,
            grid=(1,),
            in_specs=[pl.BlockSpec(memory_space=pltpu.VMEM)] * len(tensors),
            out_specs=whole(out),
            scratch_shapes=[pltpu.VMEM((rows, ab), jnp.float32)],
        ),
        cost_estimate=takes(2),
        compiler_params=pltpu.CompilerParams(vmem_limit_bytes=VMEM_BYTES // 3),
        name="last_product",
    )(info, *tensors)


def bins_kernel(places, n_other, info, irr_ref, sym_ref, own, *refs):
    others, refs = refs[:n_other], refs[n_other:]
    bins, (out, total) = refs[:-2], refs[-2:]
    irr_d, sym = irr_ref[...], sym_ref[...]
    total[...] = jnp.zeros_like(total)
    for place, part in zip(places, bins):
        level, first = info[place], 0
        for other in others:
            last = first + other.shape[0]

            @pl.when((level >= first) & (level < last))
            def _():
                add_bins(total, part, own, other, level, level - first, irr_d)

            first = last

    out[...] = pick_symmetry(total, sym, out.shape[0])


def bins_product(places, parts, own, other, info, irr_d, sym):
    pair_rows, ab = irr_d.shape[0], sym.shape[1]
    out = jax.ShapeDtypeStruct((2 * pair_rows, ab), jnp.float32)
    tensors = [irr_d, sym, own, *other, *parts]
    return pl.pallas_call(
        functools.partial(bins_kernel, places, len(other)),
        out_shape=out,
        grid_spec=pltpu.PrefetchScalarGridSpec(
            num_scalar_prefetch=1,
            grid=(1,),
            in_specs=[pl.BlockSpec(memory_space=pltpu.VMEM)] * len(tensors),
            out_specs=whole(out),
            scratch_shapes=[pltpu.VMEM((IRREPS * 2 * pair_rows, ab), jnp.float32)],
        ),
        cost_estimate=takes(3),
        compiler_params=pltpu.CompilerParams(vmem_limit_bytes=VMEM_BYTES // 3),
        name="bins_product",
    )(info, *tensors)


def left_rows_kernel(slots, irreps, code_ref, integrals, out_ref, rows, arrived):
    group = pl.program_id(0)
    d_cols, ab = code_ref.shape
    main, tail, pitch = split_lanes(d_cols)

    def fetch(i):
        c = jnp.maximum(slots[i] - 1, 0)
        return pltpu.make_async_copy(integrals.at[c], rows.at[i], arrived.at[i])

    def start(i, carry):
        fetch(i).start()
        return carry

    @pl.when(group == 0)
    def _():
        lax.fori_loop(0, rows.shape[0], start, 0)

    code = code_ref[...]
    for h in range(IRREPS):
        i = group * IRREPS + h
        fetch(i).wait()
        irrep = jnp.where(slots[i] > 0, irreps[i], IRREPS)
        row = jnp.where(code == irrep, rows[i].astype(jnp.float32), 0.0)
        out_ref[0, pl.ds(h * main, main)] = row[:main].astype(out_ref.dtype)
        if tail:
            end = row[main:]
            if pitch > tail:
                end = jnp.concatenate([end, jnp.zeros((pitch - tail, ab), jnp.float32)], axis=0)
            out_ref[0, pl.ds(IRREPS * main + h * pitch, pitch)] = end.astype(out_ref.dtype)


def left_rows(integrals, code, slots, irreps):
    d_cols, ab = code.shape
    count = slots.shape[0]
    main, _, pitch = split_lanes(d_cols)
    depth = IRREPS * (main + pitch)
    return pl.pallas_call(
        left_rows_kernel,
        out_shape=jax.ShapeDtypeStruct((count // IRREPS, depth, ab), integrals.dtype),
        grid_spec=pltpu.PrefetchScalarGridSpec(
            num_scalar_prefetch=2,
            grid=(count // IRREPS,),
            in_specs=[whole(code), pl.BlockSpec(memory_space=pl.ANY)],
            out_specs=pl.BlockSpec((1, depth, ab), lambda i, *_: (i, 0, 0)),
            scratch_shapes=[
                pltpu.VMEM((count, d_cols, ab), integrals.dtype),
                pltpu.SemaphoreType.DMA((count,)),
            ],
        ),
        cost_estimate=takes(5),
        compiler_params=pltpu.CompilerParams(vmem_limit_bytes=VMEM_BYTES),
        name="left_rows",
    )(slots, irreps, code, integrals)


def left_kernel(amp_ref, row_ref, out_ref):
    sources, groups, pair_rows, depth = amp_ref.shape
    step = pl.program_id(0)

    @pl.when(step == 0)
    def _():
        out_ref[...] = jnp.zeros_like(out_ref)

    total = out_ref[...]
    for g in range(groups):
        amps = amp_ref[:, g].astype(jnp.float32).reshape(sources * pair_rows, depth)
        total += jnp.dot(
            amps.astype(row_ref.dtype), row_ref[step * groups + g],
            preferred_element_type=jnp.float32,
        )
    out_ref[...] = total


def left_product(amps, rows):
    sources, groups, pair_rows, depth = amps.shape
    ab = rows.shape[2]
    at_once = max(n for n in (1, 2, 3) if groups % n == 0)
    return pl.pallas_call(
        left_kernel,
        out_shape=jax.ShapeDtypeStruct((sources * pair_rows, ab), jnp.float32),
        grid=(groups // at_once,),
        in_specs=[
            pl.BlockSpec((sources, at_once, pair_rows, depth), lambda i: (0, i, 0, 0)),
            pl.BlockSpec(memory_space=pltpu.VMEM),
        ],
        out_specs=pl.BlockSpec((sources * pair_rows, ab), lambda i: (0, 0)),
        cost_estimate=takes(5),
        compiler_params=pltpu.CompilerParams(vmem_limit_bytes=VMEM_BYTES),
        name="left_product",
    )(amps, rows)


def body(amplitudes, integrals, orbital_irreps, slab_index):
    c_rows, d_cols, ab_cols = integrals.shape
    pair_rows = amplitudes.shape[0]
    virtual = orbital_irreps.shape[0]
    blocks = lax.axis_size("remap")
    sides = 2
    levels = blocks // sides
    assert levels >= 2 and blocks == levels * sides
    block = lax.axis_index("remap")
    level, side = block // sides, block % sides
    left = LEFT * IRREPS

    bins = pack(integrals, orbital_irreps, slab_index)
    amplitudes, orbital_irreps, bins = lax.optimization_barrier((amplitudes, orbital_irreps, bins))

    earlier = jnp.arange(c_rows)[:, None] < jnp.arange(c_rows)[None, :]

    def places_of(irr):
        alike = (irr[:, :, None] == irr[:, None, :]) & earlier[None]
        rank = jnp.sum(alike.astype(jnp.int32), axis=1)
        over = rank >= BINS
        left_rank = jnp.sum((over[:, :, None] & earlier[None]).astype(jnp.int32), axis=1)
        return jnp.where(over, BINS * IRREPS + left_rank, rank * IRREPS + irr)

    def table(places, first, count):
        wanted = first + jnp.arange(count, dtype=jnp.int32)
        return first_plus_one(places[:, :, None] == wanted[None, None, :])

    own_irr = lax.dynamic_slice_in_dim(orbital_irreps, block * c_rows, c_rows, 0)
    own_places = places_of(own_irr[None])

    def own_left(index):
        first = BINS * IRREPS + index * left
        match = own_places[0][:, None] == first + jnp.arange(left, dtype=jnp.int32)[None, :]
        irreps = jnp.sum(jnp.where(match, own_irr[:, None], 0), axis=0)
        return first_plus_one(match[None])[0], irreps

    irr_d = lax.dynamic_slice_in_dim(orbital_irreps, lax.axis_index("rep") * d_cols, d_cols, 0)
    stride = virtual * virtual // SLABS
    pair_ab = slab_index[0] * stride + jnp.arange(ab_cols, dtype=jnp.int32)
    sym_ab = jnp.bitwise_xor(
        irrep_of(pair_ab // virtual, orbital_irreps), irrep_of(pair_ab % virtual, orbital_irreps)
    )
    code = jnp.bitwise_xor(irr_d[:, None], sym_ab[None, :])
    irr_rows = jnp.broadcast_to(irr_d[None, :], (pair_rows, d_cols))

    order = [1, 0] + list(range(2, levels))

    def at_level(z, a):
        return a if z < levels // 2 else levels - 1 - a

    plan = []
    for z in range(levels):
        for b in range(sides):
            row = [at_level(z, a) * sides + c for c in (1 - b, b) for a in order]
            for t in range(levels):
                for a in (z - t, z + t):
                    row.append(order.index(at_level(z, a)) if 0 <= a < levels else -1)
            plan.append(row)
    info = lax.dynamic_index_in_dim(jnp.asarray(np.array(plan, np.int32)), block, 0, False)

    by_c = amplitudes.transpose(1, 0, 2)

    def hops(pairs, swap):
        return [
            (a * sides + b, c * sides + (sides - 1 - b if swap else b))
            for a, c in pairs
            for b in range(sides)
        ]

    rounds = [(bins, bins)]
    for t in range(1, levels):
        up = [(z, z + 1) for z in range(t - 1, levels - 1)]
        down = [(levels - 1 - a, levels - 1 - c) for a, c in up]
        rounds.append(
            (
                lax.ppermute(rounds[-1][0], "remap", hops(up, False)),
                lax.ppermute(rounds[-1][1], "remap", hops(down, False)),
            )
        )
    places = places_of(orbital_irreps.reshape(blocks, c_rows))
    left_rounds = (jnp.max(places) - BINS * IRREPS + left) // left
    c_at = jnp.maximum(table(places, 0, BINS * IRREPS + left) - 1, 0)
    in_bins = [(0, BINS)]
    split = levels // 2
    stay = hops([(z, z) for z in range(levels)], True)
    def left_term(sent, rows):
        arrived = lax.all_to_all(sent, "remap", split_axis=0, concat_axis=0, tiled=True)
        return left_product(arrived, rows)

    (near,) = route(by_c, c_at, info[:split], in_bins, c_rows, False)
    near = lax.ppermute(near, "remap", stay)
    by_c, rounds[1] = lax.optimization_barrier((by_c, rounds[1]))
    every = jnp.arange(blocks, dtype=jnp.int32)
    (sent,) = route(by_c, c_at, every, [(BINS, LEFT)], c_rows, True)
    (far,) = route(by_c, c_at, info[split:levels], in_bins, c_rows, False)
    (own,) = route(by_c, c_at, info[levels:blocks], in_bins, c_rows, False)
    left_at = own_left(0)
    sent, far, own, left_at, near, rounds[2], code, irr_rows, sym_ab = lax.optimization_barrier(
        (sent, far, own, left_at, near, rounds[2], code, irr_rows, sym_ab)
    )
    other = [near, lax.ppermute(far, "remap", stay)]
    total = left_term(sent, left_rows(integrals, code, *left_at))
    rounds[-1], total = lax.optimization_barrier((rounds[-1], total))
    mine = 0
    for t, parts in enumerate(rounds):
        ways = [blocks + 2 * t, blocks + 2 * t + 1]
        if t == 0:
            ways, parts = ways[:1], parts[:1]
        reach = max(row[way] for row in plan for way in ways)
        if t == levels - 1:
            chosen = choose(ways, own, other, info, irr_rows)
            mine += last_product(ways, parts, chosen, info, sym_ab[None, :])
            continue
        mine += bins_product(ways, parts, own, other[: 1 + (reach >= split)], info, irr_rows, sym_ab[None, :])

    def next_round(index, total):
        c_at = jnp.maximum(table(places, BINS * IRREPS + index * left, left) - 1, 0)
        (sent,) = route(by_c, c_at, every, [(0, LEFT)], c_rows, True)
        return total + left_term(sent, left_rows(integrals, code, *own_left(index)))

    total = lax.fori_loop(1, left_rounds, next_round, total)

    total = total.reshape(blocks, pair_rows, ab_cols)
    ids = jnp.arange(blocks)[:, None, None]
    total = total + jnp.where(ids == block, mine[None, :pair_rows], 0.0)
    total = total + jnp.where(ids == level * sides + 1 - side, mine[None, pair_rows:], 0.0)
    return reduce_to_owners(0.5 * total.reshape(blocks * pair_rows, ab_cols))


def solution(mesh):
    in_specs = (P("remap", None, "rep"), P("remap", "rep", None), P(), P())
    out_specs = P("remap", "rep")
    return jax.shard_map(body, mesh=mesh, in_specs=in_specs, out_specs=out_specs, check_vma=False)
```

time: 156 us -> 144 us (0.923)
  waiting for transfers between devices: 50.5 us -> 35.6 us
  starting transfers between devices: 18.2 us -> 23.6 us
  Pallas kernels: 51.2 us -> 48 us
  local copies, waits for them, and re-layouts: 17 us -> 19.6 us
    ppermute x3, waiting for transfers between devices: 12.2 us -> 0.61 us  [body(): lax.ppermute(rounds[-1][1], 'remap', hops(down, False))]
    ppermute x2, waiting for transfers between devices: 38.3 us -> 31.6 us  [the longest x1 31.6 us: body(): other = [near, lax.ppermute(far, 'remap', stay)]]
    unnamed x14 -> x20, local copies, waits for them, and re-layouts: 2.68 us -> 6.45 us
    all_to_all x1, waiting for transfers between devices: 0.01 us -> 3.41 us  [left_term(): lax.all_to_all(sent, 'remap', split_axis=0, concat_axis=0, tiled=True)]
    ppermute x3, starting transfers between devices: 6.39 us -> 9.33 us  [body(): lax.ppermute(rounds[-1][0], 'remap', hops(up, False))]
    pallas_call x5 -> x8, Pallas kernels: 27.9 us -> 25.8 us  [the longest x3 11 us: bins_product(): pl.pallas_call(functools.partial(bins_kernel, places, len(other)), out_sh...]
    all_to_all x1, starting transfers between devices: 4.41 us -> 6.18 us  [left_term(): lax.all_to_all(sent, 'remap', split_axis=0, concat_axis=0, tiled=True)]
    pallas_call x4, Pallas kernels: 19 us -> 17.4 us  [route(): pl.pallas_call(functools.partial(route_kernel, [first for first, _ in spa...]
  transfers between devices with their start and end apart: 9 -> 9, of which waited for: 5 -> 3; matrix products, arithmetic and copies ran while one was open for 8% -> 11% of each run, Pallas kernels for 21% -> 28%
where the time goes in v3:
time: 144 us; the launch traced here: 143 us
  Pallas kernels  48 us (33%)
  waiting for transfers between devices  35.6 us (25%)
  starting transfers between devices  23.6 us (16%)
  local copies, waits for them, and re-layouts  19.6 us (14%)
  blocking collectives  10.9 us (8%)
  other arithmetic  3.58 us (2%)
  between operations  1.77 us (1%)
    ppermute x1, waiting for transfers between devices, body(): other = [near, lax.ppermute(far, 'remap', stay)]  31.6 us
    pallas_call x4, Pallas kernels, route(): pl.pallas_call(functools.partial(route_kernel, [first for first, _ in spa...  17.4 us
    pallas_call x3, Pallas kernels, bins_product(): pl.pallas_call(functools.partial(bins_kernel, places, len(other)), out_sh...  11 us
    all_to_all x1, blocking collectives, reduce_to_owners(): lax.all_to_all(blocks, ('remap', 'rep'), split_axis=0, concat_axis=0, til...  10.9 us
    optimization_barrier x1, local copies, waits for them, and re-layouts, body(): lax.optimization_barrier((amplitudes, orbital_irreps, bins))  10.9 us
    ppermute x3, starting transfers between devices, body(): lax.ppermute(rounds[-1][0], 'remap', hops(up, False))  9.33 us
    unnamed x20, local copies, waits for them, and re-layouts  6.45 us
    all_to_all x1, starting transfers between devices, left_term(): lax.all_to_all(sent, 'remap', split_axis=0, concat_axis=0, tiled=True)  6.18 us
  transfers between devices with their start and end apart: 9, of which 3 were waited for; matrix products, arithmetic and copies ran while one was open for 11% of the time, Pallas kernels for 28%

profile of v3, /device:TPU:0, one launch (start us, length us, event | category | flops | bytes accessed | tf_op | source)
XLA Modules:
  0.0 143.1 jit_solution(14771200308171179864)
XLA Ops:
  1.4 4.8 %pack_bins.1.refs_1_ = bf16[10,304,128]{2,1,0:T(8,128)(2,1)S(1)} custom-call(s32[1200]{0:T(1024)S(1)} %copy-done.8, s32[1]{0:T(128)S(6)} %copy.21.slab, bf16[150,300,128]{2,1,0:T(8,128)(2,1)} %integrals.3), custom_call_target="tpu_custom_call" | custom-call | bytes 14400000 | tf_op jit(solution)/shard_map/pack_bins/pallas_call | solution.py:137
  6.2 1.3 collective-permute-start.3
  7.5 6.2 %collective-permute-start = (bf16[10,304,128]{2,1,0:T(8,128)(2,1)S(1)}, bf16[10,304,128]{2,1,0:T(8,128)(2,1)}, u32[]{:S(2)}, u32[]{:S(2)}) collective-permute-start(bf16[10,304,128]{2,1,0:T(8,128)(2,1)S(1)} %pack_bins.1.refs_1_), channel_id=1, source_target_pairs={{0,8},{4,12},{8,16},{12,20},{16,24},{20,28},{1,9},{5,13},{9,17},{1... | collective-permute-start | bytes 2334728 | tf_op jit(solution)/shard_map/ppermute | solution.py:539
  15.5 0.8 select_reduce_fusion.3
  16.4 10.9 %copy.11 = bf16[8,1200,300]{2,0,1:T(8,128)(2,1)} copy(bf16[8,1200,300]{1,0,2:T(8,128)(2,1)} %param.7) | data formatting | bytes 11520000 | tf_op jit(solution)/shard_map/optimization_barrier | solution.py:476
  27.3 3.4 %route_rows.11 = bf16[2,10,8,2432]{3,2,1,0:T(8,128)(2,1)S(1)} custom-call(s32[1216]{0:T(1024)S(1)} %max.22.c_at, s32[2]{0:T(128)S(1)} %get-tuple-element.218.blocks, bf16[1200,8,300]{2,1,0:T(8,128)(2,1)} %bitcast.36), custom_call_target="tpu_custom_call" | custom-call | bytes 7200000 | tf_op jit(solution)/shard_map/route_rows/pallas_call | solution.py:185
  30.7 2.2 %collective-permute-start.6 = (bf16[2,10,8,2432]{3,2,1,0:T(8,128)(2,1)S(1)}, bf16[2,10,8,2432]{3,2,1,0:T(8,128)(2,1)S(1)}, u32[]{:S(2)}, u32[]{:S(2)}) collective-permute-start(bf16[2,10,8,2432]{3,2,1,0:T(8,128)(2,1)S(1)} %route_rows.11), channel_id=1, source_target_pairs={{0,4},{4,0},{8,12},{12,8},{16,20},{20,16},{24,28},{28,24},{1,5},{5... | collective-permute-start | bytes 2334728 | tf_op jit(solution)/shard_map/ppermute | solution.py:554
  33.9 1.3 collective-permute-start.4
  35.2 1.6 %collective-permute-start.1 = (bf16[10,304,128]{2,1,0:T(8,128)(2,1)}, bf16[10,304,128]{2,1,0:T(8,128)(2,1)}, u32[]{:S(2)}, u32[]{:S(2)}) collective-permute-start(bf16[10,304,128]{2,1,0:T(8,128)(2,1)} %collective-permute-done.refs_2_), channel_id=1, source_target_pairs={{8,16},{12,20},{16,24},{20,28},{9,17},{13,21},{17,25},{21,29},{10,... | collective-permute-start | bytes 2334728 | tf_op jit(solution)/shard_map/ppermute | solution.py:539
  37.4 3.7 %route_rows.9 = bf16[2,10,8,2432]{3,2,1,0:T(8,128)(2,1)S(1)} custom-call(s32[1216]{0:T(1024)S(1)} %max.22.c_at, s32[2]{0:T(128)S(1)} %get-tuple-element.219.blocks, bf16[1200,8,300]{2,1,0:T(8,128)(2,1)} %bitcast.37), custom_call_target="tpu_custom_call" | custom-call | bytes 7200000 | tf_op jit(solution)/shard_map/route_rows/pallas_call | solution.py:185
  41.1 0.9 copy-done.7
  41.9 3.9 %route_rows.10.own = bf16[4,10,8,2432]{3,2,1,0:T(8,128)(2,1)S(1)} custom-call(s32[1216]{0:T(1024)S(1)} %max.22.c_at, s32[4]{0:T(128)S(1)} %slice_bitcast_fusion.1.blocks, bf16[1200,8,300]{2,1,0:T(8,128)(2,1)S(1)} %bitcast.39), custom_call_target="tpu_custom_call" | custom-call | bytes 14400000 | tf_op jit(solution)/shard_map/route_rows/pallas_call | solution.py:185
  45.8 6.4 %route_rows.8 = bf16[8,9,8,2432]{3,2,1,0:T(8,128)(2,1)S(1)} custom-call(s32[1216]{0:T(1024)S(1)} %max.22.c_at, s32[8]{0:T(128)S(1)} %iota.95.blocks, bf16[1200,8,300]{2,1,0:T(8,128)(2,1)S(1)} %bitcast.40), custom_call_target="tpu_custom_call" | custom-call | bytes 25920000 | tf_op jit(solution)/shard_map/route_rows/pallas_call | solution.py:185
  52.2 1.5 %copy-done.2 = bf16[8,9,8,2432]{3,2,1,0:T(8,128)(2,1)} copy-done((bf16[8,9,8,2432]{3,2,1,0:T(8,128)(2,1)}, bf16[8,9,8,2432]{3,2,1,0:T(8,128)(2,1)S(1)}, u32[]{:S(2)}) %copy-start.2) | copy-done | bytes 2801688
  54.4 6.2 %all-to-all-start.1 = ((bf16[8,9,8,2432]{3,2,1,0:T(8,128)(2,1)}), bf16[8,9,8,2432]{3,2,1,0:T(8,128)(2,1)}, u32[]{:S(2)}, u32[]{:S(2)}) async-start(bf16[8,9,8,2432]{3,2,1,0:T(8,128)(2,1)} %copy-done.2), calls=%async_computation.1 | async-start | bytes 5603328 | tf_op jit(solution)/shard_map/all_to_all | solution.py:550
  60.6 2.0 %collective-permute-start.7 = (bf16[2,10,8,2432]{3,2,1,0:T(8,128)(2,1)}, bf16[2,10,8,2432]{3,2,1,0:T(8,128)(2,1)S(1)}, u32[]{:S(2)}, u32[]{:S(2)}) collective-permute-start(bf16[2,10,8,2432]{3,2,1,0:T(8,128)(2,1)} %copy-done.7), channel_id=1, source_target_pairs={{0,4},{4,0},{8,12},{12,8},{16,20},{20,16},{24,28},{28,24},{1,5},{5... | collective-permute-start | bytes 2334728 | tf_op jit(solution)/shard_map/ppermute | solution.py:564
  62.6 1.3 collective-permute-start.5
  63.9 1.6 %collective-permute-start.2 = (bf16[10,304,128]{2,1,0:T(8,128)(2,1)}, bf16[10,304,128]{2,1,0:T(8,128)(2,1)}, u32[]{:S(2)}, u32[]{:S(2)}) collective-permute-start(bf16[10,304,128]{2,1,0:T(8,128)(2,1)} %collective-permute-done.1.refs_2_), channel_id=1, source_target_pairs={{16,24},{20,28},{17,25},{21,29},{18,26},{22,30},{19,27},{23,31}} | collective-permute-start | bytes 2334728 | tf_op jit(solution)/shard_map/ppermute | solution.py:539
  65.7 0.7 select_reduce_fusion.8
  67.5 4.1 %left_rows.2.row_ref = bf16[9,2432,128]{2,1,0:T(8,128)(2,1)S(1)} custom-call(s32[72]{0:T(128)S(1)} %select_reduce_fusion.7.slots, s32[72]{0:T(128)S(1)} %select_reduce_fusion.6.irreps, s32[300,128]{1,0:T(8,128)S(1)} %broadcast_xor_fusion.code_ref, bf16[150,300,128]{2,1,0:T(8,128)(2,1)} %integrals.3), custom_call_target="tpu_custom_call" | custom-call | bytes 18000000 | tf_op jit(solution)/shard_map/left_rows/pallas_call | solution.py:407
  71.6 2.4 %copy-done.1 = bf16[9,2432,128]{2,1,0:T(8,128)(2,1)} copy-done((bf16[9,2432,128]{2,1,0:T(8,128)(2,1)}, bf16[9,2432,128]{2,1,0:T(8,128)(2,1)S(1)}, u32[]{:S(2)}) %copy-start.1) | copy-done | bytes 5603352
  74.0 2.7 %bins_product.3 = f32[16,128]{1,0:T(8,128)S(1)} custom-call(s32[16]{0:T(128)S(1)} %get-tuple-element.216.info, s32[8,300]{1,0:T(8,128)S(1)} %broadcast_in_dim.197.irr_ref, s32[1,128]{1,0:T(1,128)S(1)} %bitcast.32, bf16[4,10,8,2432]{3,2,1,0:T(8,128)(2,1)S(1)} %route_rows.10.own, bf16[2,10,8,2432]{3,2,1,0:T(8,128)(2,1)S(1)} %collective-permute-done.6.refs_0_, ...), custom_call_target="tpu_custom_call" | custom-call | bytes 10800000 | tf_op jit(solution)/shard_map/bins_product/pallas_call | solution.py:355
  76.8 31.6 %collective-permute-done.7.refs_1_ = bf16[2,10,8,2432]{3,2,1,0:T(8,128)(2,1)S(1)} collective-permute-done((bf16[2,10,8,2432]{3,2,1,0:T(8,128)(2,1)}, bf16[2,10,8,2432]{3,2,1,0:T(8,128)(2,1)S(1)}, u32[]{:S(2)}, u32[]{:S(2)}) %collective-permute-start.7) | collective-permute-done | bytes 778272 | tf_op jit(solution)/shard_map/ppermute | solution.py:564
  108.4 1.9 %choose_rows.1.chosen = bf16[10,128,300]{2,1,0:T(8,128)(2,1)S(1)} custom-call(s32[16]{0:T(128)S(1)} %get-tuple-element.216.info, s32[8,300]{1,0:T(8,128)S(1)} %broadcast_in_dim.197.irr_ref, bf16[4,10,8,2432]{3,2,1,0:T(8,128)(2,1)S(1)} %route_rows.10.own, bf16[2,10,8,2432]{3,2,1,0:T(8,128)(2,1)S(1)} %collective-permute-done.6.refs_0_, ...), custom_call_target="tpu_custom_call" | custom-call | bytes 10800000 | tf_op jit(solution)/shard_map/choose_rows/pallas_call | solution.py:279
  110.3 0.9 copy-done.3
  111.2 4.1 %bins_product.5 = f32[16,128]{1,0:T(8,128)S(1)} custom-call(s32[16]{0:T(128)S(1)} %get-tuple-element.216.info, s32[8,300]{1,0:T(8,128)S(1)} %broadcast_in_dim.197.irr_ref, s32[1,128]{1,0:T(1,128)S(1)} %bitcast.33, bf16[4,10,8,2432]{3,2,1,0:T(8,128)(2,1)S(1)} %route_rows.10.own, bf16[2,10,8,2432]{3,2,1,0:T(8,128)(2,1)S(1)} %collective-permute-done.6.refs_0_, ...), custom_call_target="tpu_custom_call" | custom-call | bytes 10800000 | tf_op jit(solution)/shard_map/bins_product/pallas_call | solution.py:355
  115.3 4.1 %bins_product.4 = f32[16,128]{1,0:T(8,128)S(1)} custom-call(s32[16]{0:T(128)S(1)} %get-tuple-element.216.info, s32[8,300]{1,0:T(8,128)S(1)} %broadcast_in_dim.197.irr_ref, s32[1,128]{1,0:T(1,128)S(1)} %bitcast.34, bf16[4,10,8,2432]{3,2,1,0:T(8,128)(2,1)S(1)} %route_rows.10.own, bf16[2,10,8,2432]{3,2,1,0:T(8,128)(2,1)S(1)} %collective-permute-done.6.refs_0_, ...), custom_call_target="tpu_custom_call" | custom-call | bytes 10800000 | tf_op jit(solution)/shard_map/bins_product/pallas_call | solution.py:355
  119.5 3.4 %all-to-all-done.1.amp_ref = bf16[8,9,8,2432]{3,2,1,0:T(8,128)(2,1)} async-done(((bf16[8,9,8,2432]{3,2,1,0:T(8,128)(2,1)}), bf16[8,9,8,2432]{3,2,1,0:T(8,128)(2,1)}, u32[]{:S(2)}, u32[]{:S(2)}) %all-to-all-start.1) | async-done | bytes 2801696 | tf_op jit(solution)/shard_map/all_to_all | solution.py:550
  122.9 5.1 %left_product.5 = f32[64,128]{1,0:T(8,128)S(1)} custom-call(bf16[8,9,8,2432]{3,2,1,0:T(8,128)(2,1)} %all-to-all-done.1.amp_ref, bf16[9,2432,128]{2,1,0:T(8,128)(2,1)} %copy-done.1), custom_call_target="tpu_custom_call" | custom-call | bytes 18000000 | tf_op jit(solution)/shard_map/left_product/pallas_call | solution.py:448
  128.0 2.3 %last_product.1 = f32[16,128]{1,0:T(8,128)S(1)} custom-call(s32[16]{0:T(128)S(1)} %get-tuple-element.216.info, s32[1,128]{1,0:T(1,128)S(1)} %bitcast.35, bf16[10,128,300]{2,1,0:T(8,128)(2,1)S(1)} %copy-done.4, bf16[10,304,128]{2,1,0:T(8,128)(2,1)} %collective-permute-done.2.refs_0_, bf16[10,304,128]{2,1,0:T(8,128)(2,1)} %collective-permute-done.5.refs_1_), custom_call_target="tpu_custom_call" | custom-call | bytes 7200000 | tf_op jit(solution)/shard_map/last_product/pallas_call | solution.py:316
  130.7 10.9 %all_to_all.17.parts_ref = f32[32,1,256]{2,1,0:T(1,128)} all-to-all(f32[32,1,256]{2,1,0:T(1,128)S(1)} %reshape.399), channel_id=1, replica_groups=mesh['remap'=8,'rep'=4] {'remap','rep'}, dimensions={0} | all-to-all | bytes 65536 | tf_op jit(solution)/shard_map/all_to_all | solution.py:37
  141.6 1.5 %sum_parts.1 = f32[8,32]{1,0:T(8,128)} custom-call(f32[32,1,256]{2,1,0:T(1,128)} %all_to_all.17.parts_ref), custom_call_target="tpu_custom_call" | custom-call | tf_op jit(solution)/shard_map/sum_parts/pallas_call | solution.py:38
  (69 shorter events, 5.7 us)
Async XLA Ops:
  0.7 0.7 copy-start.8
  1.4 13.1 %copy-start.9 = (s32[1200]{0:T(1024)S(1)}, s32[1200]{0:T(1024)}, u32[]{:S(2)}) copy-start(s32[1200]{0:T(1024)} %irreps.1) | copy-start | bytes 14404
  6.2 21.1 %copy-start.5 = (bf16[10,304,128]{2,1,0:T(8,128)(2,1)}, bf16[10,304,128]{2,1,0:T(8,128)(2,1)S(1)}, u32[]{:S(2)}) copy-start(bf16[10,304,128]{2,1,0:T(8,128)(2,1)S(1)} %pack_bins.1.refs_1_) | copy-start | bytes 2334724
  6.2 27.8 %collective-permute-start.3 = (bf16[10,304,128]{2,1,0:T(8,128)(2,1)S(1)}, bf16[10,304,128]{2,1,0:T(8,128)(2,1)}, u32[]{:S(2)}, u32[]{:S(2)}) collective-permute-start(bf16[10,304,128]{2,1,0:T(8,128)(2,1)S(1)} %pack_bins.1.refs_1_), channel_id=1, source_target_pairs={{24,16},{28,20},{16,8},{20,12},{8,0},{12,4},{25,17},{29,21},{17,9}... | collective-permute-start | bytes 2334728 | tf_op jit(solution)/shard_map/ppermute | solution.py:540
  7.5 27.8 %collective-permute-start = (bf16[10,304,128]{2,1,0:T(8,128)(2,1)S(1)}, bf16[10,304,128]{2,1,0:T(8,128)(2,1)}, u32[]{:S(2)}, u32[]{:S(2)}) collective-permute-start(bf16[10,304,128]{2,1,0:T(8,128)(2,1)S(1)} %pack_bins.1.refs_1_), channel_id=1, source_target_pairs={{0,8},{4,12},{8,16},{12,20},{16,24},{20,28},{1,9},{5,13},{9,17},{1... | collective-permute-start | bytes 2334728 | tf_op jit(solution)/shard_map/ppermute | solution.py:539
  30.7 23.1 %collective-permute-start.6 = (bf16[2,10,8,2432]{3,2,1,0:T(8,128)(2,1)S(1)}, bf16[2,10,8,2432]{3,2,1,0:T(8,128)(2,1)S(1)}, u32[]{:S(2)}, u32[]{:S(2)}) collective-permute-start(bf16[2,10,8,2432]{3,2,1,0:T(8,128)(2,1)S(1)} %route_rows.11), channel_id=1, source_target_pairs={{0,4},{4,0},{8,12},{12,8},{16,20},{20,16},{24,28},{28,24},{1,5},{5... | collective-permute-start | bytes 2334728 | tf_op jit(solution)/shard_map/ppermute | solution.py:554
  33.9 20.5 %collective-permute-start.4 = (bf16[10,304,128]{2,1,0:T(8,128)(2,1)}, bf16[10,304,128]{2,1,0:T(8,128)(2,1)}, u32[]{:S(2)}, u32[]{:S(2)}) collective-permute-start(bf16[10,304,128]{2,1,0:T(8,128)(2,1)} %collective-permute-done.3.refs_3_), channel_id=1, source_target_pairs={{16,8},{20,12},{8,0},{12,4},{17,9},{21,13},{9,1},{13,5},{18,10},{2... | collective-permute-start | bytes 2334728 | tf_op jit(solution)/shard_map/ppermute | solution.py:540
  35.2 19.2 %collective-permute-start.1 = (bf16[10,304,128]{2,1,0:T(8,128)(2,1)}, bf16[10,304,128]{2,1,0:T(8,128)(2,1)}, u32[]{:S(2)}, u32[]{:S(2)}) collective-permute-start(bf16[10,304,128]{2,1,0:T(8,128)(2,1)} %collective-permute-done.refs_2_), channel_id=1, source_target_pairs={{8,16},{12,20},{16,24},{20,28},{9,17},{13,21},{17,25},{21,29},{10,... | collective-permute-start | bytes 2334728 | tf_op jit(solution)/shard_map/ppermute | solution.py:539
  37.4 4.6 %copy-start.10 = (bf16[8,1200,300]{2,0,1:T(8,128)(2,1)S(1)}, bf16[8,1200,300]{2,0,1:T(8,128)(2,1)}, u32[]{:S(2)}) copy-start(bf16[8,1200,300]{2,0,1:T(8,128)(2,1)} %copy.11) | copy-start | bytes 17280004
  41.1 0.9 copy-start.7
  52.2 1.5 %copy-start.2 = (bf16[8,9,8,2432]{3,2,1,0:T(8,128)(2,1)}, bf16[8,9,8,2432]{3,2,1,0:T(8,128)(2,1)S(1)}, u32[]{:S(2)}) copy-start(bf16[8,9,8,2432]{3,2,1,0:T(8,128)(2,1)S(1)} %route_rows.8) | copy-start | bytes 8404996
  54.4 68.5 %all-to-all-start.1 = ((bf16[8,9,8,2432]{3,2,1,0:T(8,128)(2,1)}), bf16[8,9,8,2432]{3,2,1,0:T(8,128)(2,1)}, u32[]{:S(2)}, u32[]{:S(2)}) async-start(bf16[8,9,8,2432]{3,2,1,0:T(8,128)(2,1)} %copy-done.2), calls=%async_computation.1 | async-start | bytes 5603328 | tf_op jit(solution)/shard_map/all_to_all | solution.py:550
  60.6 47.8 %collective-permute-start.7 = (bf16[2,10,8,2432]{3,2,1,0:T(8,128)(2,1)}, bf16[2,10,8,2432]{3,2,1,0:T(8,128)(2,1)S(1)}, u32[]{:S(2)}, u32[]{:S(2)}) collective-permute-start(bf16[2,10,8,2432]{3,2,1,0:T(8,128)(2,1)} %copy-done.7), channel_id=1, source_target_pairs={{0,4},{4,0},{8,12},{12,8},{16,20},{20,16},{24,28},{28,24},{1,5},{5... | collective-permute-start | bytes 2334728 | tf_op jit(solution)/shard_map/ppermute | solution.py:564
  62.6 65.4 %collective-permute-start.5 = (bf16[10,304,128]{2,1,0:T(8,128)(2,1)}, bf16[10,304,128]{2,1,0:T(8,128)(2,1)}, u32[]{:S(2)}, u32[]{:S(2)}) collective-permute-start(bf16[10,304,128]{2,1,0:T(8,128)(2,1)} %collective-permute-done.4.refs_3_), channel_id=1, source_target_pairs={{8,0},{12,4},{9,1},{13,5},{10,2},{14,6},{11,3},{15,7}} | collective-permute-start | bytes 2334728 | tf_op jit(solution)/shard_map/ppermute | solution.py:540
  63.9 64.1 %collective-permute-start.2 = (bf16[10,304,128]{2,1,0:T(8,128)(2,1)}, bf16[10,304,128]{2,1,0:T(8,128)(2,1)}, u32[]{:S(2)}, u32[]{:S(2)}) collective-permute-start(bf16[10,304,128]{2,1,0:T(8,128)(2,1)} %collective-permute-done.1.refs_2_), channel_id=1, source_target_pairs={{16,24},{20,28},{17,25},{21,29},{18,26},{22,30},{19,27},{23,31}} | collective-permute-start | bytes 2334728 | tf_op jit(solution)/shard_map/ppermute | solution.py:539
  67.5 6.5 %copy-start.6 = (bf16[10,304,128]{2,1,0:T(8,128)(2,1)S(1)}, bf16[10,304,128]{2,1,0:T(8,128)(2,1)}, u32[]{:S(2)}) copy-start(bf16[10,304,128]{2,1,0:T(8,128)(2,1)} %copy-done.5) | copy-start | bytes 2334724
  71.6 2.4 %copy-start.1 = (bf16[9,2432,128]{2,1,0:T(8,128)(2,1)}, bf16[9,2432,128]{2,1,0:T(8,128)(2,1)S(1)}, u32[]{:S(2)}) copy-start(bf16[9,2432,128]{2,1,0:T(8,128)(2,1)S(1)} %left_rows.2.row_ref) | copy-start | bytes 16809988
  110.3 0.9 copy-start.3
  119.5 8.5 %copy-start.4 = (bf16[10,128,300]{2,1,0:T(8,128)(2,1)S(1)}, bf16[10,128,300]{2,1,0:T(8,128)(2,1)}, u32[]{:S(2)}) copy-start(bf16[10,128,300]{2,1,0:T(8,128)(2,1)} %copy-done.3) | copy-start | bytes 2304004

commit v4 on v3

--- a/solution.py
+++ b/solution.py
@@ -12,6 +12,7 @@
 IRREPS = 8
 BINS = 10
 LEFT = 9
+LEFT_MORE = 1
 VMEM_BYTES = 48 * 1024 * 1024
 BYTES_A_US = 3_600_000
 
@@ -63,7 +64,7 @@
     return main, tail, pitch
 
 
-def pack_kernel(irreps, slab, integrals, out_ref, rows, code_ref, counts, arrived):
+def pack_kernel(irreps, slab, integrals, out_ref, rows, code_ref, arrived):
     c_rows, d_cols, ab = integrals.shape
     bins = out_ref.shape[0]
     virtual = irreps.shape[0]
@@ -71,22 +72,23 @@
     def fetch(c, i):
         return pltpu.make_async_copy(integrals.at[c], rows.at[i], arrived.at[i])
 
-    for h in range(IRREPS):
-        counts[h] = 0
     c_first = lax.axis_index("remap") * c_rows
 
-    def place(c, carry):
+    def place(c, words):
         h = irreps[c_first + c]
-        g = counts[h]
-        counts[h] = g + 1
+        shift = (h & 3) * 8
+        low = h < 4
+        g = (jnp.where(low, words[0], words[1]) >> shift) & 255
 
         @pl.when(g < bins)
         def _():
             fetch(c, g * IRREPS + h).start()
 
-        return carry
-
-    lax.fori_loop(0, c_rows, place, 0, unroll=15)
+        step = jnp.where(g < bins, jnp.int32(1) << shift, 0)
+        return words[0] + jnp.where(low, step, 0), words[1] + jnp.where(low, 0, step)
+
+    words = lax.fori_loop(0, c_rows, place, (jnp.int32(0), jnp.int32(0)), unroll=15)
+    counts = [(words[h // 4] >> (h % 4 * 8)) & 255 for h in range(IRREPS)]
 
     pair = slab[0] * (virtual * virtual // SLABS)
     a_first = pair // virtual
@@ -98,14 +100,14 @@
         value = irreps[a_first + over] ^ irreps[b_first + k - over * virtual]
         return jnp.where(lane == k, value, sym)
 
-    sym = lax.fori_loop(0, ab, symmetry, jnp.zeros((1, ab), jnp.int32), unroll=32)
+    sym = lax.fori_loop(0, ab, symmetry, jnp.zeros((1, ab), jnp.int32), unroll=64)
     d_first = lax.axis_index("rep") * d_cols
 
     def code_row(d, carry):
         code_ref[pl.ds(d, 1), :] = sym ^ irreps[d_first + d]
         return carry
 
-    lax.fori_loop(0, d_cols, code_row, 0, unroll=50)
+    lax.fori_loop(0, d_cols, code_row, 0, unroll=75)
 
     code = code_ref[...].astype(jnp.float32).astype(rows.dtype)
 
@@ -145,7 +147,6 @@
             scratch_shapes=[
                 pltpu.VMEM((BINS * IRREPS, d_cols, ab), integrals.dtype),
                 pltpu.VMEM((d_cols, ab), jnp.int32),
-                pltpu.SMEM((IRREPS,), jnp.int32),
                 pltpu.SemaphoreType.DMA((BINS * IRREPS,)),
             ],
         ),
@@ -291,20 +292,28 @@
     )(info, *tensors)
 
 
-def last_kernel(places, info, sym_ref, chosen, *refs):
-    bins, (out, total) = refs[:2], refs[2:]
+def last_kernel(places, info, sym_ref, chosen_ref, up, down, out, total, chosen, bins, arrived):
+    rows = pltpu.make_async_copy(chosen_ref, chosen, arrived.at[0])
+    rows.start()
     total[...] = jnp.zeros_like(total)
-    for place, part in zip(places, bins):
+    for place, part in zip(places, (up, down)):
 
         @pl.when(info[place] >= 0)
         def _():
-            sum_ = jnp.zeros(total.shape, jnp.float32)
-            for g in range(part.shape[0]):
-                sum_ += jnp.dot(
-                    chosen[g], part[g, pl.ds(0, chosen.shape[2])],
-                    preferred_element_type=jnp.float32,
-                )
-            total[...] = sum_
+            copy = pltpu.make_async_copy(part, bins, arrived.at[1])
+            copy.start()
+            copy.wait()
+
+    rows.wait()
+
+    @pl.when(jnp.maximum(info[places[0]], info[places[1]]) >= 0)
+    def _():
+        sum_ = jnp.zeros(total.shape, jnp.float32)
+        for g in range(bins.shape[0]):
+            sum_ += jnp.dot(
+                chosen[g], bins[g, pl.ds(0, chosen.shape[2])], preferred_element_type=jnp.float32
+            )
+        total[...] = sum_
 
     out[...] = pick_symmetry(total, sym_ref[...], out.shape[0])
 
@@ -312,21 +321,25 @@
 def last_product(places, parts, chosen, info, sym):
     rows, ab = chosen.shape[1], sym.shape[1]
     out = jax.ShapeDtypeStruct((rows // IRREPS, ab), jnp.float32)
-    tensors = [sym, chosen, *parts]
     return pl.pallas_call(
         functools.partial(last_kernel, places),
         out_shape=out,
         grid_spec=pltpu.PrefetchScalarGridSpec(
             num_scalar_prefetch=1,
             grid=(1,),
-            in_specs=[pl.BlockSpec(memory_space=pltpu.VMEM)] * len(tensors),
+            in_specs=[whole(sym)] + [pl.BlockSpec(memory_space=pl.ANY)] * 3,
             out_specs=whole(out),
-            scratch_shapes=[pltpu.VMEM((rows, ab), jnp.float32)],
+            scratch_shapes=[
+                pltpu.VMEM((rows, ab), jnp.float32),
+                pltpu.VMEM(chosen.shape, chosen.dtype),
+                pltpu.VMEM(parts[0].shape, parts[0].dtype),
+                pltpu.SemaphoreType.DMA((2,)),
+            ],
         ),
         cost_estimate=takes(2),
-        compiler_params=pltpu.CompilerParams(vmem_limit_bytes=VMEM_BYTES // 3),
+        compiler_params=pltpu.CompilerParams(vmem_limit_bytes=VMEM_BYTES),
         name="last_product",
-    )(info, *tensors)
+    )(info, sym, chosen, *parts)
 
 
 def bins_kernel(places, n_other, info, irr_ref, sym_ref, own, *refs):
@@ -423,37 +436,54 @@
     )(slots, irreps, code, integrals)
 
 
-def left_kernel(amp_ref, row_ref, out_ref):
+def left_kernel(amp_ref, row_ref, out_ref, amps, rows, amps_here, rows_here):
     sources, groups, pair_rows, depth = amp_ref.shape
-    step = pl.program_id(0)
-
-    @pl.when(step == 0)
-    def _():
-        out_ref[...] = jnp.zeros_like(out_ref)
-
-    total = out_ref[...]
-    for g in range(groups):
-        amps = amp_ref[:, g].astype(jnp.float32).reshape(sources * pair_rows, depth)
-        total += jnp.dot(
-            amps.astype(row_ref.dtype), row_ref[step * groups + g],
-            preferred_element_type=jnp.float32,
+    first = groups // 2
+    halves = [(0, first), (first, groups - first)] if first else [(0, groups)]
+    halves = [(at, pl.ds(lo, size), lo, size) for at, (lo, size) in enumerate(halves)]
+    copies = []
+    for at, span, lo, size in halves:
+        copies.append(
+            [
+                pltpu.make_async_copy(
+                    amp_ref.at[source, span], amps.at[source, span], amps_here.at[at, source]
+                )
+                for source in range(sources)
+            ]
+            + [
+                pltpu.make_async_copy(row_ref.at[group], rows.at[group], rows_here.at[group])
+                for group in range(lo, lo + size)
+            ]
         )
+    for half in copies:
+        for copy in half:
+            copy.start()
+    total = jnp.zeros(out_ref.shape, jnp.float32)
+    for half, (_, _, lo, size) in zip(copies, halves):
+        for copy in half:
+            copy.wait()
+        for group in range(lo, lo + size):
+            lhs = amps[:, group].astype(jnp.float32).reshape(sources * pair_rows, depth)
+            total += jnp.dot(
+                lhs.astype(rows.dtype), rows[group], preferred_element_type=jnp.float32
+            )
     out_ref[...] = total
 
 
 def left_product(amps, rows):
     sources, groups, pair_rows, depth = amps.shape
     ab = rows.shape[2]
-    at_once = max(n for n in (1, 2, 3) if groups % n == 0)
     return pl.pallas_call(
         left_kernel,
         out_shape=jax.ShapeDtypeStruct((sources * pair_rows, ab), jnp.float32),
-        grid=(groups // at_once,),
-        in_specs=[
-            pl.BlockSpec((sources, at_once, pair_rows, depth), lambda i: (0, i, 0, 0)),
-            pl.BlockSpec(memory_space=pltpu.VMEM),
+        in_specs=[pl.BlockSpec(memory_space=pl.ANY)] * 2,
+        out_specs=pl.BlockSpec(memory_space=pltpu.VMEM),
+        scratch_shapes=[
+            pltpu.VMEM(amps.shape, amps.dtype),
+            pltpu.VMEM(rows.shape, rows.dtype),
+            pltpu.SemaphoreType.DMA((2, sources)),
+            pltpu.SemaphoreType.DMA((groups,)),
         ],
-        out_specs=pl.BlockSpec((sources * pair_rows, ab), lambda i: (0, 0)),
         cost_estimate=takes(5),
         compiler_params=pltpu.CompilerParams(vmem_limit_bytes=VMEM_BYTES),
         name="left_product",
@@ -470,7 +500,7 @@
     assert levels >= 2 and blocks == levels * sides
     block = lax.axis_index("remap")
     level, side = block // sides, block % sides
-    left = LEFT * IRREPS
+    slots = (BINS + LEFT) * IRREPS
 
     bins = pack(integrals, orbital_irreps, slab_index)
     amplitudes, orbital_irreps, bins = lax.optimization_barrier((amplitudes, orbital_irreps, bins))
@@ -491,9 +521,8 @@
     own_irr = lax.dynamic_slice_in_dim(orbital_irreps, block * c_rows, c_rows, 0)
     own_places = places_of(own_irr[None])
 
-    def own_left(index):
-        first = BINS * IRREPS + index * left
-        match = own_places[0][:, None] == first + jnp.arange(left, dtype=jnp.int32)[None, :]
+    def own_left(first, count):
+        match = own_places[0][:, None] == first + jnp.arange(count, dtype=jnp.int32)[None, :]
         irreps = jnp.sum(jnp.where(match, own_irr[:, None], 0), axis=0)
         return first_plus_one(match[None])[0], irreps
 
@@ -541,8 +570,9 @@
             )
         )
     places = places_of(orbital_irreps.reshape(blocks, c_rows))
-    left_rounds = (jnp.max(places) - BINS * IRREPS + left) // left
-    c_at = jnp.maximum(table(places, 0, BINS * IRREPS + left) - 1, 0)
+    more = LEFT_MORE * IRREPS
+    more_rounds = jnp.maximum(jnp.max(places) - slots + more, 0) // more
+    c_at = jnp.maximum(table(places, 0, slots) - 1, 0)
     in_bins = [(0, BINS)]
     split = levels // 2
     stay = hops([(z, z) for z in range(levels)], True)
@@ -557,9 +587,9 @@
     (sent,) = route(by_c, c_at, every, [(BINS, LEFT)], c_rows, True)
     (far,) = route(by_c, c_at, info[split:levels], in_bins, c_rows, False)
     (own,) = route(by_c, c_at, info[levels:blocks], in_bins, c_rows, False)
-    left_at = own_left(0)
-    sent, far, own, left_at, near, rounds[2], code, irr_rows, sym_ab = lax.optimization_barrier(
-        (sent, far, own, left_at, near, rounds[2], code, irr_rows, sym_ab)
+    left_at = own_left(BINS * IRREPS, LEFT * IRREPS)
+    sent, left_at, near, rounds[2], code, irr_rows, sym_ab = lax.optimization_barrier(
+        (sent, left_at, near, rounds[2], code, irr_rows, sym_ab)
     )
     other = [near, lax.ppermute(far, "remap", stay)]
     total = left_term(sent, left_rows(integrals, code, *left_at))
@@ -577,11 +607,12 @@
         mine += bins_product(ways, parts, own, other[: 1 + (reach >= split)], info, irr_rows, sym_ab[None, :])
 
     def next_round(index, total):
-        c_at = jnp.maximum(table(places, BINS * IRREPS + index * left, left) - 1, 0)
-        (sent,) = route(by_c, c_at, every, [(0, LEFT)], c_rows, True)
-        return total + left_term(sent, left_rows(integrals, code, *own_left(index)))
-
-    total = lax.fori_loop(1, left_rounds, next_round, total)
+        first = slots + index * more
+        c_at = jnp.maximum(table(places, first, more) - 1, 0)
+        (sent,) = route(by_c, c_at, every, [(0, LEFT_MORE)], c_rows, True)
+        return total + left_term(sent, left_rows(integrals, code, *own_left(first, more)))
+
+    total = lax.fori_loop(0, more_rounds, next_round, total)
 
     total = total.reshape(blocks, pair_rows, ab_cols)
     ids = jnp.arange(blocks)[:, None, None]

time: 144 us -> 143 us (level)
  waiting for transfers between devices: 35.6 us -> 32 us
  Pallas kernels: 48 us -> 51.1 us
    ppermute x1, waiting for transfers between devices: 31.6 us -> 20.6 us  [body(): other = [near, lax.ppermute(far, 'remap', stay)]]
    pallas_call x4, Pallas kernels: 17.4 us -> 22.3 us  [route(): pl.pallas_call(functools.partial(route_kernel, [first for first, _ in spa...]
    ppermute x3, waiting for transfers between devices: 0.61 us -> 4.45 us  [body(): lax.ppermute(rounds[-1][1], 'remap', hops(down, False))]
    all_to_all x1, waiting for transfers between devices: 3.41 us -> 5.32 us  [left_term(): lax.all_to_all(sent, 'remap', split_axis=0, concat_axis=0, tiled=True)]
    ppermute x1, waiting for transfers between devices: 0.01 us -> 1.64 us  [body(): near = lax.ppermute(near, 'remap', stay)]
    unnamed x20 -> x18, local copies, waits for them, and re-layouts: 6.45 us -> 5.19 us
  transfers between devices with their start and end apart: 9 -> 9, of which waited for: 3 -> 4; matrix products, arithmetic and copies ran while one was open for 11% -> 12% of each run, Pallas kernels for 28% -> 31%
where the time goes in v4:
time: 143 us; the launch traced here: 142 us
  Pallas kernels  51.1 us (36%)
  waiting for transfers between devices  32 us (22%)
  starting transfers between devices  23.6 us (17%)
  local copies, waits for them, and re-layouts  18.8 us (13%)
  blocking collectives  10.9 us (8%)
  other arithmetic  3.58 us (3%)
  between operations  1.79 us (1%)
    pallas_call x4, Pallas kernels, route(): pl.pallas_call(functools.partial(route_kernel, [first for first, _ in spa...  22.3 us
    ppermute x1, waiting for transfers between devices, body(): other = [near, lax.ppermute(far, 'remap', stay)]  20.6 us
    all_to_all x1, blocking collectives, reduce_to_owners(): lax.all_to_all(blocks, ('remap', 'rep'), split_axis=0, concat_axis=0, til...  10.9 us
    optimization_barrier x1, local copies, waits for them, and re-layouts, body(): lax.optimization_barrier((amplitudes, orbital_irreps, bins))  10.9 us
    pallas_call x3, Pallas kernels, bins_product(): pl.pallas_call(functools.partial(bins_kernel, places, len(other)), out_sh...  10.7 us
    ppermute x3, starting transfers between devices, body(): lax.ppermute(rounds[-1][0], 'remap', hops(up, False))  9.59 us
    all_to_all x1, starting transfers between devices, left_term(): lax.all_to_all(sent, 'remap', split_axis=0, concat_axis=0, tiled=True)  6.06 us
    all_to_all x1, waiting for transfers between devices, left_term(): lax.all_to_all(sent, 'remap', split_axis=0, concat_axis=0, tiled=True)  5.32 us
  transfers between devices with their start and end apart: 9, of which 4 were waited for; matrix products, arithmetic and copies ran while one was open for 12% of the time, Pallas kernels for 31%

profile of v4, /device:TPU:0, one launch (start us, length us, event | category | flops | bytes accessed | tf_op | source)
XLA Modules:
  0.0 141.9 jit_solution(1271830063344357419)
XLA Ops:
  1.4 4.6 %pack_bins.1.refs_1_ = bf16[10,304,128]{2,1,0:T(8,128)(2,1)S(1)} custom-call(s32[1200]{0:T(1024)S(1)} %copy-done.4, s32[1]{0:T(128)S(6)} %copy.21.slab, bf16[150,300,128]{2,1,0:T(8,128)(2,1)} %integrals.3), custom_call_target="tpu_custom_call" | custom-call | bytes 14400000 | tf_op jit(solution)/shard_map/pack_bins/pallas_call | solution.py:139
  6.0 1.3 collective-permute-start.3
  7.3 6.5 %collective-permute-start = (bf16[10,304,128]{2,1,0:T(8,128)(2,1)S(1)}, bf16[10,304,128]{2,1,0:T(8,128)(2,1)}, u32[]{:S(2)}, u32[]{:S(2)}) collective-permute-start(bf16[10,304,128]{2,1,0:T(8,128)(2,1)S(1)} %pack_bins.1.refs_1_), channel_id=1, source_target_pairs={{0,8},{4,12},{8,16},{12,20},{16,24},{20,28},{1,9},{5,13},{9,17},{1... | collective-permute-start | bytes 2334728 | tf_op jit(solution)/shard_map/ppermute | solution.py:568
  14.8 0.8 select_reduce_fusion.3
  16.5 10.9 %copy.11 = bf16[8,1200,300]{2,0,1:T(8,128)(2,1)} copy(bf16[8,1200,300]{1,0,2:T(8,128)(2,1)} %param.7) | data formatting | bytes 11520000 | tf_op jit(solution)/shard_map/optimization_barrier | solution.py:506
  27.4 3.4 %route_rows.9 = bf16[2,10,8,2432]{3,2,1,0:T(8,128)(2,1)S(1)} custom-call(s32[1216]{0:T(1024)S(1)} %max.25.c_at, s32[2]{0:T(128)S(1)} %get-tuple-element.215.blocks, bf16[1200,8,300]{2,1,0:T(8,128)(2,1)} %bitcast.36), custom_call_target="tpu_custom_call" | custom-call | bytes 7200000 | tf_op jit(solution)/shard_map/route_rows/pallas_call | solution.py:186
  30.8 2.1 %collective-permute-start.6 = (bf16[2,10,8,2432]{3,2,1,0:T(8,128)(2,1)S(1)}, bf16[2,10,8,2432]{3,2,1,0:T(8,128)(2,1)S(1)}, u32[]{:S(2)}, u32[]{:S(2)}) collective-permute-start(bf16[2,10,8,2432]{3,2,1,0:T(8,128)(2,1)S(1)} %route_rows.9), channel_id=1, source_target_pairs={{0,4},{4,0},{8,12},{12,8},{16,20},{20,16},{24,28},{28,24},{1,5},{5... | collective-permute-start | bytes 2334728 | tf_op jit(solution)/shard_map/ppermute | solution.py:584
  33.9 1.3 collective-permute-start.4
  35.2 1.6 %collective-permute-start.1 = (bf16[10,304,128]{2,1,0:T(8,128)(2,1)}, bf16[10,304,128]{2,1,0:T(8,128)(2,1)}, u32[]{:S(2)}, u32[]{:S(2)}) collective-permute-start(bf16[10,304,128]{2,1,0:T(8,128)(2,1)} %collective-permute-done.refs_2_), channel_id=1, source_target_pairs={{8,16},{12,20},{16,24},{20,28},{9,17},{13,21},{17,25},{21,29},{10,... | collective-permute-start | bytes 2334728 | tf_op jit(solution)/shard_map/ppermute | solution.py:568
  37.3 9.2 %route_rows.8 = bf16[8,9,8,2432]{3,2,1,0:T(8,128)(2,1)S(1)} custom-call(s32[1216]{0:T(1024)S(1)} %max.25.c_at, s32[8]{0:T(128)S(1)} %iota.95.blocks, bf16[1200,8,300]{2,1,0:T(8,128)(2,1)} %bitcast.37), custom_call_target="tpu_custom_call" | custom-call | bytes 25920000 | tf_op jit(solution)/shard_map/route_rows/pallas_call | solution.py:186
  46.5 1.5 %copy-done.1 = bf16[8,9,8,2432]{3,2,1,0:T(8,128)(2,1)} copy-done((bf16[8,9,8,2432]{3,2,1,0:T(8,128)(2,1)}, bf16[8,9,8,2432]{3,2,1,0:T(8,128)(2,1)S(1)}, u32[]{:S(2)}) %copy-start.1) | copy-done | bytes 2801688
  48.1 1.6 %collective-permute-done.6.refs_0_ = bf16[2,10,8,2432]{3,2,1,0:T(8,128)(2,1)S(1)} collective-permute-done((bf16[2,10,8,2432]{3,2,1,0:T(8,128)(2,1)S(1)}, bf16[2,10,8,2432]{3,2,1,0:T(8,128)(2,1)S(1)}, u32[]{:S(2)}, u32[]{:S(2)}) %collective-permute-start.6) | collective-permute-done | bytes 778272 | tf_op jit(solution)/shard_map/ppermute | solution.py:584
  49.7 4.4 %collective-permute-done.4.refs_3_ = bf16[10,304,128]{2,1,0:T(8,128)(2,1)} collective-permute-done((bf16[10,304,128]{2,1,0:T(8,128)(2,1)S(1)}, bf16[10,304,128]{2,1,0:T(8,128)(2,1)}, u32[]{:S(2)}, u32[]{:S(2)}) %collective-permute-start.4) | collective-permute-done | bytes 778272 | tf_op jit(solution)/shard_map/ppermute | solution.py:569
  54.2 6.1 %all-to-all-start.1 = ((bf16[8,9,8,2432]{3,2,1,0:T(8,128)(2,1)}), bf16[8,9,8,2432]{3,2,1,0:T(8,128)(2,1)}, u32[]{:S(2)}, u32[]{:S(2)}) async-start(bf16[8,9,8,2432]{3,2,1,0:T(8,128)(2,1)} %copy-done.1), calls=%async_computation.1 | async-start | bytes 5603328 | tf_op jit(solution)/shard_map/all_to_all | solution.py:580
  60.2 4.2 %route_rows.11 = bf16[2,10,8,2432]{3,2,1,0:T(8,128)(2,1)} custom-call(s32[1216]{0:T(1024)S(1)} %max.25.c_at, s32[2]{0:T(128)S(1)} %get-tuple-element.214.blocks, bf16[1200,8,300]{2,1,0:T(8,128)(2,1)} %bitcast.38), custom_call_target="tpu_custom_call" | custom-call | bytes 7200000 | tf_op jit(solution)/shard_map/route_rows/pallas_call | solution.py:186
  64.4 2.0 %collective-permute-start.7 = (bf16[2,10,8,2432]{3,2,1,0:T(8,128)(2,1)}, bf16[2,10,8,2432]{3,2,1,0:T(8,128)(2,1)S(1)}, u32[]{:S(2)}, u32[]{:S(2)}) collective-permute-start(bf16[2,10,8,2432]{3,2,1,0:T(8,128)(2,1)} %route_rows.11), channel_id=1, source_target_pairs={{0,4},{4,0},{8,12},{12,8},{16,20},{20,16},{24,28},{28,24},{1,5},{5... | collective-permute-start | bytes 2334728 | tf_op jit(solution)/shard_map/ppermute | solution.py:594
  66.4 1.3 collective-permute-start.5
  67.7 1.5 %collective-permute-start.2 = (bf16[10,304,128]{2,1,0:T(8,128)(2,1)}, bf16[10,304,128]{2,1,0:T(8,128)(2,1)}, u32[]{:S(2)}, u32[]{:S(2)}) collective-permute-start(bf16[10,304,128]{2,1,0:T(8,128)(2,1)} %collective-permute-done.1.refs_2_), channel_id=1, source_target_pairs={{16,24},{20,28},{17,25},{21,29},{18,26},{22,30},{19,27},{23,31}} | collective-permute-start | bytes 2334728 | tf_op jit(solution)/shard_map/ppermute | solution.py:568
  70.4 0.7 select_reduce_fusion.8
  71.9 5.5 %route_rows.10.own = bf16[4,10,8,2432]{3,2,1,0:T(8,128)(2,1)S(1)} custom-call(s32[1216]{0:T(1024)S(1)} %max.25.c_at, s32[4]{0:T(128)S(1)} %slice_bitcast_fusion.1.blocks, bf16[1200,8,300]{2,1,0:T(8,128)(2,1)} %bitcast.39), custom_call_target="tpu_custom_call" | custom-call | bytes 14400000 | tf_op jit(solution)/shard_map/route_rows/pallas_call | solution.py:186
  77.4 4.1 %left_rows.2.row_ref = bf16[9,2432,128]{2,1,0:T(8,128)(2,1)S(1)} custom-call(s32[72]{0:T(128)S(1)} %select_reduce_fusion.7.slots, s32[72]{0:T(128)S(1)} %select_reduce_fusion.6.irreps, s32[300,128]{1,0:T(8,128)S(1)} %broadcast_xor_fusion.code_ref, bf16[150,300,128]{2,1,0:T(8,128)(2,1)} %integrals.3), custom_call_target="tpu_custom_call" | custom-call | bytes 18000000 | tf_op jit(solution)/shard_map/left_rows/pallas_call | solution.py:420
  81.5 2.4 %copy-done = bf16[9,2432,128]{2,1,0:T(8,128)(2,1)} copy-done((bf16[9,2432,128]{2,1,0:T(8,128)(2,1)}, bf16[9,2432,128]{2,1,0:T(8,128)(2,1)S(1)}, u32[]{:S(2)}) %copy-start) | copy-done | bytes 5603352
  83.9 2.7 %bins_product.3 = f32[16,128]{1,0:T(8,128)S(1)} custom-call(s32[16]{0:T(128)S(1)} %get-tuple-element.212.info, s32[8,300]{1,0:T(8,128)S(1)} %broadcast_in_dim.197.irr_ref, s32[1,128]{1,0:T(1,128)S(1)} %bitcast.32, bf16[4,10,8,2432]{3,2,1,0:T(8,128)(2,1)S(1)} %route_rows.10.own, bf16[2,10,8,2432]{3,2,1,0:T(8,128)(2,1)S(1)} %collective-permute-done.6.refs_0_, ...), custom_call_target="tpu_custom_call" | custom-call | bytes 10800000 | tf_op jit(solution)/shard_map/bins_product/pallas_call | solution.py:368
  86.6 20.6 %collective-permute-done.7.refs_1_ = bf16[2,10,8,2432]{3,2,1,0:T(8,128)(2,1)S(1)} collective-permute-done((bf16[2,10,8,2432]{3,2,1,0:T(8,128)(2,1)}, bf16[2,10,8,2432]{3,2,1,0:T(8,128)(2,1)S(1)}, u32[]{:S(2)}, u32[]{:S(2)}) %collective-permute-start.7) | collective-permute-done | bytes 778272 | tf_op jit(solution)/shard_map/ppermute | solution.py:594
  107.2 1.9 %choose_rows.1.chosen_ref = bf16[10,128,300]{2,1,0:T(8,128)(2,1)S(1)} custom-call(s32[16]{0:T(128)S(1)} %get-tuple-element.212.info, s32[8,300]{1,0:T(8,128)S(1)} %broadcast_in_dim.197.irr_ref, bf16[4,10,8,2432]{3,2,1,0:T(8,128)(2,1)S(1)} %route_rows.10.own, bf16[2,10,8,2432]{3,2,1,0:T(8,128)(2,1)S(1)} %collective-permute-done.6.refs_0_, ...), custom_call_target="tpu_custom_call" | custom-call | bytes 10800000 | tf_op jit(solution)/shard_map/choose_rows/pallas_call | solution.py:280
  109.1 3.9 %bins_product.4 = f32[16,128]{1,0:T(8,128)S(1)} custom-call(s32[16]{0:T(128)S(1)} %get-tuple-element.212.info, s32[8,300]{1,0:T(8,128)S(1)} %broadcast_in_dim.197.irr_ref, s32[1,128]{1,0:T(1,128)S(1)} %bitcast.33, bf16[4,10,8,2432]{3,2,1,0:T(8,128)(2,1)S(1)} %route_rows.10.own, bf16[2,10,8,2432]{3,2,1,0:T(8,128)(2,1)S(1)} %collective-permute-done.6.refs_0_, ...), custom_call_target="tpu_custom_call" | custom-call | bytes 10800000 | tf_op jit(solution)/shard_map/bins_product/pallas_call | solution.py:368
  113.0 4.1 %bins_product.5 = f32[16,128]{1,0:T(8,128)S(1)} custom-call(s32[16]{0:T(128)S(1)} %get-tuple-element.212.info, s32[8,300]{1,0:T(8,128)S(1)} %broadcast_in_dim.197.irr_ref, s32[1,128]{1,0:T(1,128)S(1)} %bitcast.34, bf16[4,10,8,2432]{3,2,1,0:T(8,128)(2,1)S(1)} %route_rows.10.own, bf16[2,10,8,2432]{3,2,1,0:T(8,128)(2,1)S(1)} %collective-permute-done.6.refs_0_, ...), custom_call_target="tpu_custom_call" | custom-call | bytes 10800000 | tf_op jit(solution)/shard_map/bins_product/pallas_call | solution.py:368
  117.1 5.3 %all-to-all-done.1.amp_ref = bf16[8,9,8,2432]{3,2,1,0:T(8,128)(2,1)} async-done(((bf16[8,9,8,2432]{3,2,1,0:T(8,128)(2,1)}), bf16[8,9,8,2432]{3,2,1,0:T(8,128)(2,1)}, u32[]{:S(2)}, u32[]{:S(2)}) %all-to-all-start.1) | async-done | bytes 2801696 | tf_op jit(solution)/shard_map/all_to_all | solution.py:580
  122.4 4.4 %left_product.5 = f32[64,128]{1,0:T(8,128)S(1)} custom-call(bf16[8,9,8,2432]{3,2,1,0:T(8,128)(2,1)} %all-to-all-done.1.amp_ref, bf16[9,2432,128]{2,1,0:T(8,128)(2,1)} %copy-done), custom_call_target="tpu_custom_call" | custom-call | bytes 18000000 | tf_op jit(solution)/shard_map/left_product/pallas_call | solution.py:476
  126.9 1.7 %last_product.1 = f32[16,128]{1,0:T(8,128)S(1)} custom-call(s32[16]{0:T(128)S(1)} %get-tuple-element.212.info, s32[1,128]{1,0:T(1,128)S(1)} %bitcast.35, bf16[10,128,300]{2,1,0:T(8,128)(2,1)S(1)} %choose_rows.1.chosen_ref, bf16[10,304,128]{2,1,0:T(8,128)(2,1)} %collective-permute-done.2.up, bf16[10,304,128]{2,1,0:T(8,128)(2,1)S(1)} %collective-permute-done.5.down), custom_call_target="tpu_custom_call" | custom-call | bytes 7200000 | tf_op jit(solution)/shard_map/last_product/pallas_call | solution.py:324
  129.5 10.9 %all_to_all.17.parts_ref = f32[32,1,256]{2,1,0:T(1,128)} all-to-all(f32[32,1,256]{2,1,0:T(1,128)S(1)} %reshape.399), channel_id=1, replica_groups=mesh['remap'=8,'rep'=4] {'remap','rep'}, dimensions={0} | all-to-all | bytes 65536 | tf_op jit(solution)/shard_map/all_to_all | solution.py:38
  140.4 1.5 %sum_parts.1 = f32[8,32]{1,0:T(8,128)} custom-call(f32[32,1,256]{2,1,0:T(1,128)} %all_to_all.17.parts_ref), custom_call_target="tpu_custom_call" | custom-call | tf_op jit(solution)/shard_map/sum_parts/pallas_call | solution.py:39
  (67 shorter events, 6.1 us)
Async XLA Ops:
  0.7 0.7 copy-start.4
  1.4 12.4 %copy-start.5 = (s32[1200]{0:T(1024)S(1)}, s32[1200]{0:T(1024)}, u32[]{:S(2)}) copy-start(s32[1200]{0:T(1024)} %irreps.1) | copy-start | bytes 14404
  6.0 27.9 %collective-permute-start.3 = (bf16[10,304,128]{2,1,0:T(8,128)(2,1)S(1)}, bf16[10,304,128]{2,1,0:T(8,128)(2,1)S(1)}, u32[]{:S(2)}, u32[]{:S(2)}) collective-permute-start(bf16[10,304,128]{2,1,0:T(8,128)(2,1)S(1)} %pack_bins.1.refs_1_), channel_id=1, source_target_pairs={{24,16},{28,20},{16,8},{20,12},{8,0},{12,4},{25,17},{29,21},{17,9}... | collective-permute-start | bytes 2334728 | tf_op jit(solution)/shard_map/ppermute | solution.py:569
  7.3 27.9 %collective-permute-start = (bf16[10,304,128]{2,1,0:T(8,128)(2,1)S(1)}, bf16[10,304,128]{2,1,0:T(8,128)(2,1)}, u32[]{:S(2)}, u32[]{:S(2)}) collective-permute-start(bf16[10,304,128]{2,1,0:T(8,128)(2,1)S(1)} %pack_bins.1.refs_1_), channel_id=1, source_target_pairs={{0,8},{4,12},{8,16},{12,20},{16,24},{20,28},{1,9},{5,13},{9,17},{1... | collective-permute-start | bytes 2334728 | tf_op jit(solution)/shard_map/ppermute | solution.py:568
  16.4 11.0 %copy-start.6 = (s32[1,16]{1,0:T(1,128)}, s32[1,16]{1,0:T(1,128)S(1)}, u32[]{:S(2)}) copy-start(s32[1,16]{1,0:T(1,128)S(1)} %get-tuple-element.213) | copy-start | bytes 196
  30.8 18.9 %collective-permute-start.6 = (bf16[2,10,8,2432]{3,2,1,0:T(8,128)(2,1)S(1)}, bf16[2,10,8,2432]{3,2,1,0:T(8,128)(2,1)S(1)}, u32[]{:S(2)}, u32[]{:S(2)}) collective-permute-start(bf16[2,10,8,2432]{3,2,1,0:T(8,128)(2,1)S(1)} %route_rows.9), channel_id=1, source_target_pairs={{0,4},{4,0},{8,12},{12,8},{16,20},{20,16},{24,28},{28,24},{1,5},{5... | collective-permute-start | bytes 2334728 | tf_op jit(solution)/shard_map/ppermute | solution.py:584
  33.9 12.6 %copy-start.2 = (bf16[10,304,128]{2,1,0:T(8,128)(2,1)}, bf16[10,304,128]{2,1,0:T(8,128)(2,1)S(1)}, u32[]{:S(2)}) copy-start(bf16[10,304,128]{2,1,0:T(8,128)(2,1)S(1)} %collective-permute-done.3.refs_3_) | copy-start | bytes 2334724
  33.9 20.3 %collective-permute-start.4 = (bf16[10,304,128]{2,1,0:T(8,128)(2,1)S(1)}, bf16[10,304,128]{2,1,0:T(8,128)(2,1)}, u32[]{:S(2)}, u32[]{:S(2)}) collective-permute-start(bf16[10,304,128]{2,1,0:T(8,128)(2,1)S(1)} %collective-permute-done.3.refs_3_), channel_id=1, source_target_pairs={{16,8},{20,12},{8,0},{12,4},{17,9},{21,13},{9,1},{13,5},{18,10},{2... | collective-permute-start | bytes 2334728 | tf_op jit(solution)/shard_map/ppermute | solution.py:569
  35.2 19.0 %collective-permute-start.1 = (bf16[10,304,128]{2,1,0:T(8,128)(2,1)}, bf16[10,304,128]{2,1,0:T(8,128)(2,1)}, u32[]{:S(2)}, u32[]{:S(2)}) collective-permute-start(bf16[10,304,128]{2,1,0:T(8,128)(2,1)} %collective-permute-done.refs_2_), channel_id=1, source_target_pairs={{8,16},{12,20},{16,24},{20,28},{9,17},{13,21},{17,25},{21,29},{10,... | collective-permute-start | bytes 2334728 | tf_op jit(solution)/shard_map/ppermute | solution.py:568
  46.5 1.5 %copy-start.1 = (bf16[8,9,8,2432]{3,2,1,0:T(8,128)(2,1)}, bf16[8,9,8,2432]{3,2,1,0:T(8,128)(2,1)S(1)}, u32[]{:S(2)}) copy-start(bf16[8,9,8,2432]{3,2,1,0:T(8,128)(2,1)S(1)} %route_rows.8) | copy-start | bytes 8404996
  54.2 68.3 %all-to-all-start.1 = ((bf16[8,9,8,2432]{3,2,1,0:T(8,128)(2,1)}), bf16[8,9,8,2432]{3,2,1,0:T(8,128)(2,1)}, u32[]{:S(2)}, u32[]{:S(2)}) async-start(bf16[8,9,8,2432]{3,2,1,0:T(8,128)(2,1)} %copy-done.1), calls=%async_computation.1 | async-start | bytes 5603328 | tf_op jit(solution)/shard_map/all_to_all | solution.py:580
  60.2 11.6 %copy-start.7 = (s32[1,16]{1,0:T(1,128)S(1)}, s32[1,16]{1,0:T(1,128)}, u32[]{:S(2)}) copy-start(s32[1,16]{1,0:T(1,128)} %copy-done.6) | copy-start | bytes 196
  64.4 42.8 %collective-permute-start.7 = (bf16[2,10,8,2432]{3,2,1,0:T(8,128)(2,1)}, bf16[2,10,8,2432]{3,2,1,0:T(8,128)(2,1)S(1)}, u32[]{:S(2)}, u32[]{:S(2)}) collective-permute-start(bf16[2,10,8,2432]{3,2,1,0:T(8,128)(2,1)} %route_rows.11), channel_id=1, source_target_pairs={{0,4},{4,0},{8,12},{12,8},{16,20},{20,16},{24,28},{28,24},{1,5},{5... | collective-permute-start | bytes 2334728 | tf_op jit(solution)/shard_map/ppermute | solution.py:594
  66.4 60.4 %collective-permute-start.5 = (bf16[10,304,128]{2,1,0:T(8,128)(2,1)}, bf16[10,304,128]{2,1,0:T(8,128)(2,1)S(1)}, u32[]{:S(2)}, u32[]{:S(2)}) collective-permute-start(bf16[10,304,128]{2,1,0:T(8,128)(2,1)} %collective-permute-done.4.refs_3_), channel_id=1, source_target_pairs={{8,0},{12,4},{9,1},{13,5},{10,2},{14,6},{11,3},{15,7}} | collective-permute-start | bytes 2334728 | tf_op jit(solution)/shard_map/ppermute | solution.py:569
  67.7 59.1 %collective-permute-start.2 = (bf16[10,304,128]{2,1,0:T(8,128)(2,1)}, bf16[10,304,128]{2,1,0:T(8,128)(2,1)}, u32[]{:S(2)}, u32[]{:S(2)}) collective-permute-start(bf16[10,304,128]{2,1,0:T(8,128)(2,1)} %collective-permute-done.1.refs_2_), channel_id=1, source_target_pairs={{16,24},{20,28},{17,25},{21,29},{18,26},{22,30},{19,27},{23,31}} | collective-permute-start | bytes 2334728 | tf_op jit(solution)/shard_map/ppermute | solution.py:568
  81.5 2.4 %copy-start = (bf16[9,2432,128]{2,1,0:T(8,128)(2,1)}, bf16[9,2432,128]{2,1,0:T(8,128)(2,1)S(1)}, u32[]{:S(2)}) copy-start(bf16[9,2432,128]{2,1,0:T(8,128)(2,1)S(1)} %left_rows.2.row_ref) | copy-start | bytes 16809988
  86.6 22.5 %copy-start.3 = (bf16[10,304,128]{2,1,0:T(8,128)(2,1)S(1)}, bf16[10,304,128]{2,1,0:T(8,128)(2,1)}, u32[]{:S(2)}) copy-start(bf16[10,304,128]{2,1,0:T(8,128)(2,1)} %copy-done.2) | copy-start | bytes 2334724
  128.5 0.6 copy-start.8

commit v5 on v4

--- a/solution.py
+++ b/solution.py
@@ -292,7 +292,7 @@
     )(info, *tensors)
 
 
-def last_kernel(places, info, sym_ref, chosen_ref, up, down, out, total, chosen, bins, arrived):
+def last_kernel(places, info, sym_ref, before_ref, chosen_ref, up, down, out, total, chosen, bins, arrived):
     rows = pltpu.make_async_copy(chosen_ref, chosen, arrived.at[0])
     rows.start()
     total[...] = jnp.zeros_like(total)
@@ -315,10 +315,10 @@
             )
         total[...] = sum_
 
-    out[...] = pick_symmetry(total, sym_ref[...], out.shape[0])
-
-
-def last_product(places, parts, chosen, info, sym):
+    out[...] = before_ref[...] + pick_symmetry(total, sym_ref[...], out.shape[0])
+
+
+def last_product(places, parts, before, chosen, info, sym):
     rows, ab = chosen.shape[1], sym.shape[1]
     out = jax.ShapeDtypeStruct((rows // IRREPS, ab), jnp.float32)
     return pl.pallas_call(
@@ -327,7 +327,7 @@
         grid_spec=pltpu.PrefetchScalarGridSpec(
             num_scalar_prefetch=1,
             grid=(1,),
-            in_specs=[whole(sym)] + [pl.BlockSpec(memory_space=pl.ANY)] * 3,
+            in_specs=[whole(sym), whole(before)] + [pl.BlockSpec(memory_space=pl.ANY)] * 3,
             out_specs=whole(out),
             scratch_shapes=[
                 pltpu.VMEM((rows, ab), jnp.float32),
@@ -339,24 +339,49 @@
         cost_estimate=takes(2),
         compiler_params=pltpu.CompilerParams(vmem_limit_bytes=VMEM_BYTES),
         name="last_product",
-    )(info, sym, chosen, *parts)
-
-
-def bins_kernel(places, n_other, info, irr_ref, sym_ref, own, *refs):
-    others, refs = refs[:n_other], refs[n_other:]
-    bins, (out, total) = refs[:-2], refs[-2:]
+    )(info, sym, before, chosen, *parts)
+
+
+def bins_kernel(places, n_other, info, irr_ref, sym_ref, own_ref, *refs):
+    other_refs, refs = refs[:n_other], refs[n_other:]
+    bins_refs, (out, total, own, other, bins, arrived) = refs[:-6], refs[-6:]
     irr_d, sym = irr_ref[...], sym_ref[...]
-    total[...] = jnp.zeros_like(total)
-    for place, part in zip(places, bins):
+
+    def own_copy(way, level):
+        return pltpu.make_async_copy(own_ref.at[level], own.at[way], arrived.at[way, 0])
+
+    def other_copy(way, ref, level):
+        return pltpu.make_async_copy(ref.at[level], other.at[way], arrived.at[way, 1])
+
+    def bins_copy(way):
+        return pltpu.make_async_copy(bins_refs[way], bins.at[way], arrived.at[way, 2])
+
+    for way, place in enumerate(places):
         level, first = info[place], 0
-        for other in others:
-            last = first + other.shape[0]
+
+        @pl.when(level >= 0)
+        def _():
+            own_copy(way, level).start()
+            bins_copy(way).start()
+
+        for ref in other_refs:
+            last = first + ref.shape[0]
 
             @pl.when((level >= first) & (level < last))
             def _():
-                add_bins(total, part, own, other, level, level - first, irr_d)
+                other_copy(way, ref, level - first).start()
 
             first = last
+
+    total[...] = jnp.zeros_like(total)
+    for way, place in enumerate(places):
+
+        @pl.when(info[place] >= 0)
+        def _():
+            own_copy(way, 0).wait()
+            other_copy(way, other_refs[0], 0).wait()
+            bins_copy(way).wait()
+            add_bins(total, bins.at[way], own, other, way, way, irr_d)
 
     out[...] = pick_symmetry(total, sym, out.shape[0])
 
@@ -364,21 +389,29 @@
 def bins_product(places, parts, own, other, info, irr_d, sym):
     pair_rows, ab = irr_d.shape[0], sym.shape[1]
     out = jax.ShapeDtypeStruct((2 * pair_rows, ab), jnp.float32)
-    tensors = [irr_d, sym, own, *other, *parts]
+    tensors = [own, *other, *parts]
+    ways = len(parts)
     return pl.pallas_call(
         functools.partial(bins_kernel, places, len(other)),
         out_shape=out,
         grid_spec=pltpu.PrefetchScalarGridSpec(
             num_scalar_prefetch=1,
             grid=(1,),
-            in_specs=[pl.BlockSpec(memory_space=pltpu.VMEM)] * len(tensors),
+            in_specs=[whole(irr_d), whole(sym)]
+            + [pl.BlockSpec(memory_space=pl.ANY)] * len(tensors),
             out_specs=whole(out),
-            scratch_shapes=[pltpu.VMEM((IRREPS * 2 * pair_rows, ab), jnp.float32)],
+            scratch_shapes=[
+                pltpu.VMEM((IRREPS * 2 * pair_rows, ab), jnp.float32),
+                pltpu.VMEM((ways, *own.shape[1:]), own.dtype),
+                pltpu.VMEM((ways, *own.shape[1:]), own.dtype),
+                pltpu.VMEM((ways, *parts[0].shape), parts[0].dtype),
+                pltpu.SemaphoreType.DMA((ways, 3)),
+            ],
         ),
         cost_estimate=takes(3),
-        compiler_params=pltpu.CompilerParams(vmem_limit_bytes=VMEM_BYTES // 3),
+        compiler_params=pltpu.CompilerParams(vmem_limit_bytes=VMEM_BYTES),
         name="bins_product",
-    )(info, *tensors)
+    )(info, irr_d, sym, *tensors)
 
 
 def left_rows_kernel(slots, irreps, code_ref, integrals, out_ref, rows, arrived):
@@ -602,7 +635,7 @@
         reach = max(row[way] for row in plan for way in ways)
         if t == levels - 1:
             chosen = choose(ways, own, other, info, irr_rows)
-            mine += last_product(ways, parts, chosen, info, sym_ab[None, :])
+            mine = last_product(ways, parts, mine, chosen, info, sym_ab[None, :])
             continue
         mine += bins_product(ways, parts, own, other[: 1 + (reach >= split)], info, irr_rows, sym_ab[None, :])
 

time: 143 us -> 143 us (level)
  starting transfers between devices: 23.6 us -> 21.4 us
  waiting for transfers between devices: 32 us -> 33.8 us
    all_to_all x1, starting transfers between devices: 6.06 us -> 4.42 us  [left_term(): lax.all_to_all(sent, 'remap', split_axis=0, concat_axis=0, tiled=True)]
    unnamed x18 -> x20, local copies, waits for them, and re-layouts: 5.19 us -> 6.42 us
  transfers between devices with their start and end apart: 9 -> 9, of which waited for: 4 -> 4; matrix products, arithmetic and copies ran while one was open for 12% -> 12% of each run, Pallas kernels for 31% -> 30%
where the time goes in v5:
time: 143 us; the launch traced here: 142 us
  Pallas kernels  50.9 us (36%)
  waiting for transfers between devices  33.8 us (24%)
  starting transfers between devices  21.4 us (15%)
  local copies, waits for them, and re-layouts  19.6 us (14%)
  blocking collectives  10.8 us (8%)
  other arithmetic  3.55 us (2%)
  between operations  1.75 us (1%)
    ppermute x1, waiting for transfers between devices, body(): other = [near, lax.ppermute(far, 'remap', stay)]  21.6 us
    pallas_call x4, Pallas kernels, route(): pl.pallas_call(functools.partial(route_kernel, [first for first, _ in spa...  21.5 us
    optimization_barrier x1, local copies, waits for them, and re-layouts, body(): lax.optimization_barrier((amplitudes, orbital_irreps, bins))  10.9 us
    all_to_all x1, blocking collectives, reduce_to_owners(): lax.all_to_all(blocks, ('remap', 'rep'), split_axis=0, concat_axis=0, til...  10.8 us
    pallas_call x3, Pallas kernels, bins_product(): pl.pallas_call(functools.partial(bins_kernel, places, len(other)), out_sh...  10.6 us
    ppermute x3, starting transfers between devices, body(): lax.ppermute(rounds[-1][0], 'remap', hops(up, False))  9.04 us
    unnamed x20, local copies, waits for them, and re-layouts  6.42 us
    all_to_all x1, waiting for transfers between devices, left_term(): lax.all_to_all(sent, 'remap', split_axis=0, concat_axis=0, tiled=True)  5.44 us
  transfers between devices with their start and end apart: 9, of which 4 were waited for; matrix products, arithmetic and copies ran while one was open for 12% of the time, Pallas kernels for 30%

profile of v5, /device:TPU:0, one launch (start us, length us, event | category | flops | bytes accessed | tf_op | source)
XLA Modules:
  0.0 141.9 jit_solution(1411978043593543908)
XLA Ops:
  1.4 4.6 %pack_bins.1.refs_1_ = bf16[10,304,128]{2,1,0:T(8,128)(2,1)S(1)} custom-call(s32[1200]{0:T(1024)S(1)} %copy-done.8, s32[1]{0:T(128)S(6)} %copy.21.slab, bf16[150,300,128]{2,1,0:T(8,128)(2,1)} %integrals.3), custom_call_target="tpu_custom_call" | custom-call | bytes 14400000 | tf_op jit(solution)/shard_map/pack_bins/pallas_call | solution.py:139
  5.9 1.3 collective-permute-start.3
  7.2 6.8 %collective-permute-start = (bf16[10,304,128]{2,1,0:T(8,128)(2,1)S(1)}, bf16[10,304,128]{2,1,0:T(8,128)(2,1)}, u32[]{:S(2)}, u32[]{:S(2)}) collective-permute-start(bf16[10,304,128]{2,1,0:T(8,128)(2,1)S(1)} %pack_bins.1.refs_1_), channel_id=1, source_target_pairs={{0,8},{4,12},{8,16},{12,20},{16,24},{20,28},{1,9},{5,13},{9,17},{1... | collective-permute-start | bytes 2334728 | tf_op jit(solution)/shard_map/ppermute | solution.py:601
  15.1 0.8 select_reduce_fusion.3
  16.8 10.9 %copy.11 = bf16[8,1200,300]{2,0,1:T(8,128)(2,1)} copy(bf16[8,1200,300]{1,0,2:T(8,128)(2,1)} %param.7) | data formatting | bytes 11520000 | tf_op jit(solution)/shard_map/optimization_barrier | solution.py:539
  27.6 3.4 %route_rows.9 = bf16[2,10,8,2432]{3,2,1,0:T(8,128)(2,1)S(1)} custom-call(s32[1216]{0:T(1024)S(1)} %max.25.c_at, s32[2]{0:T(128)S(1)} %get-tuple-element.215.blocks, bf16[1200,8,300]{2,1,0:T(8,128)(2,1)} %bitcast.36), custom_call_target="tpu_custom_call" | custom-call | bytes 7200000 | tf_op jit(solution)/shard_map/route_rows/pallas_call | solution.py:186
  31.1 2.0 %collective-permute-start.6 = (bf16[2,10,8,2432]{3,2,1,0:T(8,128)(2,1)S(1)}, bf16[2,10,8,2432]{3,2,1,0:T(8,128)(2,1)S(1)}, u32[]{:S(2)}, u32[]{:S(2)}) collective-permute-start(bf16[2,10,8,2432]{3,2,1,0:T(8,128)(2,1)S(1)} %route_rows.9), channel_id=1, source_target_pairs={{0,4},{4,0},{8,12},{12,8},{16,20},{20,16},{24,28},{28,24},{1,5},{5... | collective-permute-start | bytes 2334728 | tf_op jit(solution)/shard_map/ppermute | solution.py:617
  34.0 1.3 collective-permute-start.4
  36.7 9.2 %route_rows.8 = bf16[8,9,8,2432]{3,2,1,0:T(8,128)(2,1)S(1)} custom-call(s32[1216]{0:T(1024)S(1)} %max.25.c_at, s32[8]{0:T(128)S(1)} %iota.95.blocks, bf16[1200,8,300]{2,1,0:T(8,128)(2,1)} %bitcast.37), custom_call_target="tpu_custom_call" | custom-call | bytes 25920000 | tf_op jit(solution)/shard_map/route_rows/pallas_call | solution.py:186
  45.9 1.5 %copy-done.1 = bf16[8,9,8,2432]{3,2,1,0:T(8,128)(2,1)} copy-done((bf16[8,9,8,2432]{3,2,1,0:T(8,128)(2,1)}, bf16[8,9,8,2432]{3,2,1,0:T(8,128)(2,1)S(1)}, u32[]{:S(2)}) %copy-start.1) | copy-done | bytes 2801688
  47.4 2.5 %collective-permute-done.6.refs_0_ = bf16[2,10,8,2432]{3,2,1,0:T(8,128)(2,1)S(1)} collective-permute-done((bf16[2,10,8,2432]{3,2,1,0:T(8,128)(2,1)S(1)}, bf16[2,10,8,2432]{3,2,1,0:T(8,128)(2,1)S(1)}, u32[]{:S(2)}, u32[]{:S(2)}) %collective-permute-start.6) | collective-permute-done | bytes 778272 | tf_op jit(solution)/shard_map/ppermute | solution.py:617
  49.9 4.3 %collective-permute-done.4.refs_3_ = bf16[10,304,128]{2,1,0:T(8,128)(2,1)S(1)} collective-permute-done((bf16[10,304,128]{2,1,0:T(8,128)(2,1)S(1)}, bf16[10,304,128]{2,1,0:T(8,128)(2,1)S(1)}, u32[]{:S(2)}, u32[]{:S(2)}) %collective-permute-start.4) | collective-permute-done | bytes 778272 | tf_op jit(solution)/shard_map/ppermute | solution.py:602
  54.2 0.9 copy-done.4
  55.1 0.9 copy-done.6
  56.0 4.4 %all-to-all-start.1 = ((bf16[8,9,8,2432]{3,2,1,0:T(8,128)(2,1)}), bf16[8,9,8,2432]{3,2,1,0:T(8,128)(2,1)}, u32[]{:S(2)}, u32[]{:S(2)}) async-start(bf16[8,9,8,2432]{3,2,1,0:T(8,128)(2,1)} %copy-done.1), calls=%async_computation.1 | async-start | bytes 5603328 | tf_op jit(solution)/shard_map/all_to_all | solution.py:613
  60.4 3.4 %route_rows.11 = bf16[2,10,8,2432]{3,2,1,0:T(8,128)(2,1)S(1)} custom-call(s32[1216]{0:T(1024)S(1)} %max.25.c_at, s32[2]{0:T(128)S(1)} %get-tuple-element.214.blocks, bf16[1200,8,300]{2,1,0:T(8,128)(2,1)} %bitcast.38), custom_call_target="tpu_custom_call" | custom-call | bytes 7200000 | tf_op jit(solution)/shard_map/route_rows/pallas_call | solution.py:186
  63.8 2.1 %collective-permute-start.7 = (bf16[2,10,8,2432]{3,2,1,0:T(8,128)(2,1)S(1)}, bf16[2,10,8,2432]{3,2,1,0:T(8,128)(2,1)S(1)}, u32[]{:S(2)}, u32[]{:S(2)}) collective-permute-start(bf16[2,10,8,2432]{3,2,1,0:T(8,128)(2,1)S(1)} %route_rows.11), channel_id=1, source_target_pairs={{0,4},{4,0},{8,12},{12,8},{16,20},{20,16},{24,28},{28,24},{1,5},{5... | collective-permute-start | bytes 2334728 | tf_op jit(solution)/shard_map/ppermute | solution.py:627
  66.0 1.3 collective-permute-start.5
  67.3 1.5 %collective-permute-start.2 = (bf16[10,304,128]{2,1,0:T(8,128)(2,1)}, bf16[10,304,128]{2,1,0:T(8,128)(2,1)}, u32[]{:S(2)}, u32[]{:S(2)}) collective-permute-start(bf16[10,304,128]{2,1,0:T(8,128)(2,1)} %copy-done.6), channel_id=1, source_target_pairs={{16,24},{20,28},{17,25},{21,29},{18,26},{22,30},{19,27},{23,31}} | collective-permute-start | bytes 2334728 | tf_op jit(solution)/shard_map/ppermute | solution.py:601
  70.8 5.5 %route_rows.10.own_ref.own = bf16[4,10,8,2432]{3,2,1,0:T(8,128)(2,1)S(1)} custom-call(s32[1216]{0:T(1024)S(1)} %max.25.c_at, s32[4]{0:T(128)S(1)} %slice_bitcast_fusion.1.blocks, bf16[1200,8,300]{2,1,0:T(8,128)(2,1)} %bitcast.39), custom_call_target="tpu_custom_call" | custom-call | bytes 14400000 | tf_op jit(solution)/shard_map/route_rows/pallas_call | solution.py:186
  76.3 4.1 %left_rows.2.row_ref = bf16[9,2432,128]{2,1,0:T(8,128)(2,1)S(1)} custom-call(s32[72]{0:T(128)S(1)} %select_reduce_fusion.7.slots, s32[72]{0:T(128)S(1)} %select_reduce_fusion.6.irreps, s32[300,128]{1,0:T(8,128)S(1)} %broadcast_xor_fusion.code_ref, bf16[150,300,128]{2,1,0:T(8,128)(2,1)} %integrals.3), custom_call_target="tpu_custom_call" | custom-call | bytes 18000000 | tf_op jit(solution)/shard_map/left_rows/pallas_call | solution.py:453
  80.4 2.4 %copy-done = bf16[9,2432,128]{2,1,0:T(8,128)(2,1)} copy-done((bf16[9,2432,128]{2,1,0:T(8,128)(2,1)}, bf16[9,2432,128]{2,1,0:T(8,128)(2,1)S(1)}, u32[]{:S(2)}) %copy-start) | copy-done | bytes 5603352
  82.8 3.5 %bins_product.3 = f32[16,128]{1,0:T(8,128)S(1)} custom-call(s32[16]{0:T(128)S(1)} %get-tuple-element.212.info, s32[8,300]{1,0:T(8,128)S(1)} %broadcast_in_dim.197.irr_ref, s32[1,128]{1,0:T(1,128)S(1)} %bitcast.32, bf16[4,10,8,2432]{3,2,1,0:T(8,128)(2,1)S(1)} %route_rows.10.own_ref.own, bf16[2,10,8,2432]{3,2,1,0:T(8,128)(2,1)S(1)} %collective-permute-done.6.refs_0_, ...), custom_call_target="tpu_custom_call" | custom-call | bytes 10800000 | tf_op jit(solution)/shard_map/bins_product/pallas_call | solution.py:394
  86.3 21.6 %collective-permute-done.7.refs_1_ = bf16[2,10,8,2432]{3,2,1,0:T(8,128)(2,1)S(1)} collective-permute-done((bf16[2,10,8,2432]{3,2,1,0:T(8,128)(2,1)S(1)}, bf16[2,10,8,2432]{3,2,1,0:T(8,128)(2,1)S(1)}, u32[]{:S(2)}, u32[]{:S(2)}) %collective-permute-start.7) | collective-permute-done | bytes 778272 | tf_op jit(solution)/shard_map/ppermute | solution.py:627
  107.9 1.9 %choose_rows.1.chosen_ref = bf16[10,128,300]{2,1,0:T(8,128)(2,1)S(1)} custom-call(s32[16]{0:T(128)S(1)} %get-tuple-element.212.info, s32[8,300]{1,0:T(8,128)S(1)} %broadcast_in_dim.197.irr_ref, bf16[4,10,8,2432]{3,2,1,0:T(8,128)(2,1)S(1)} %route_rows.10.own_ref.own, bf16[2,10,8,2432]{3,2,1,0:T(8,128)(2,1)S(1)} %collective-permute-done.6.refs_0_, ...), custom_call_target="tpu_custom_call" | custom-call | bytes 10800000 | tf_op jit(solution)/shard_map/choose_rows/pallas_call | solution.py:280
  109.8 3.6 %bins_product.4 = f32[16,128]{1,0:T(8,128)S(1)} custom-call(s32[16]{0:T(128)S(1)} %get-tuple-element.212.info, s32[8,300]{1,0:T(8,128)S(1)} %broadcast_in_dim.197.irr_ref, s32[1,128]{1,0:T(1,128)S(1)} %bitcast.33, bf16[4,10,8,2432]{3,2,1,0:T(8,128)(2,1)S(1)} %route_rows.10.own_ref.own, bf16[2,10,8,2432]{3,2,1,0:T(8,128)(2,1)S(1)} %collective-permute-done.6.refs_0_, ...), custom_call_target="tpu_custom_call" | custom-call | bytes 10800000 | tf_op jit(solution)/shard_map/bins_product/pallas_call | solution.py:394
  113.3 3.6 %bins_product.5 = f32[16,128]{1,0:T(8,128)S(1)} custom-call(s32[16]{0:T(128)S(1)} %get-tuple-element.212.info, s32[8,300]{1,0:T(8,128)S(1)} %broadcast_in_dim.197.irr_ref, s32[1,128]{1,0:T(1,128)S(1)} %bitcast.34, bf16[4,10,8,2432]{3,2,1,0:T(8,128)(2,1)S(1)} %route_rows.10.own_ref.own, bf16[2,10,8,2432]{3,2,1,0:T(8,128)(2,1)S(1)} %collective-permute-done.6.refs_0_, ...), custom_call_target="tpu_custom_call" | custom-call | bytes 10800000 | tf_op jit(solution)/shard_map/bins_product/pallas_call | solution.py:394
  116.9 5.4 %all-to-all-done.1.amp_ref = bf16[8,9,8,2432]{3,2,1,0:T(8,128)(2,1)} async-done(((bf16[8,9,8,2432]{3,2,1,0:T(8,128)(2,1)}), bf16[8,9,8,2432]{3,2,1,0:T(8,128)(2,1)}, u32[]{:S(2)}, u32[]{:S(2)}) %all-to-all-start.1) | async-done | bytes 2801696 | tf_op jit(solution)/shard_map/all_to_all | solution.py:613
  122.4 4.4 %left_product.5 = f32[64,128]{1,0:T(8,128)S(1)} custom-call(bf16[8,9,8,2432]{3,2,1,0:T(8,128)(2,1)} %all-to-all-done.1.amp_ref, bf16[9,2432,128]{2,1,0:T(8,128)(2,1)} %copy-done), custom_call_target="tpu_custom_call" | custom-call | bytes 18000000 | tf_op jit(solution)/shard_map/left_product/pallas_call | solution.py:509
  126.8 2.4 %last_product.1 = f32[16,128]{1,0:T(8,128)S(1)} custom-call(s32[16]{0:T(128)S(1)} %get-tuple-element.212.info, s32[1,128]{1,0:T(1,128)S(1)} %bitcast.35, f32[16,128]{1,0:T(8,128)S(1)} %add_add_fusion.before_ref, bf16[10,128,300]{2,1,0:T(8,128)(2,1)S(1)} %choose_rows.1.chosen_ref, bf16[10,304,128]{2,1,0:T(8,128)(2,1)} %collective-permute-done.2.up, ...), custom_call_target="tpu_custom_call" | custom-call | bytes 7200000 | tf_op jit(solution)/shard_map/last_product/pallas_call | solution.py:324
  129.6 10.8 %all_to_all.17.parts_ref = f32[32,1,256]{2,1,0:T(1,128)} all-to-all(f32[32,1,256]{2,1,0:T(1,128)S(1)} %reshape.399), channel_id=1, replica_groups=mesh['remap'=8,'rep'=4] {'remap','rep'}, dimensions={0} | all-to-all | bytes 65536 | tf_op jit(solution)/shard_map/all_to_all | solution.py:38
  140.4 1.5 %sum_parts.1 = f32[8,32]{1,0:T(8,128)} custom-call(f32[32,1,256]{2,1,0:T(1,128)} %all_to_all.17.parts_ref), custom_call_target="tpu_custom_call" | custom-call | tf_op jit(solution)/shard_map/sum_parts/pallas_call | solution.py:39
  (69 shorter events, 6.5 us)
Async XLA Ops:
  0.7 0.7 copy-start.8
  1.4 12.7 %copy-start.9 = (s32[1200]{0:T(1024)S(1)}, s32[1200]{0:T(1024)}, u32[]{:S(2)}) copy-start(s32[1200]{0:T(1024)} %irreps.1) | copy-start | bytes 14404
  5.9 28.1 %collective-permute-start.3 = (bf16[10,304,128]{2,1,0:T(8,128)(2,1)S(1)}, bf16[10,304,128]{2,1,0:T(8,128)(2,1)S(1)}, u32[]{:S(2)}, u32[]{:S(2)}) collective-permute-start(bf16[10,304,128]{2,1,0:T(8,128)(2,1)S(1)} %pack_bins.1.refs_1_), channel_id=1, source_target_pairs={{24,16},{28,20},{16,8},{20,12},{8,0},{12,4},{25,17},{29,21},{17,9}... | collective-permute-start | bytes 2334728 | tf_op jit(solution)/shard_map/ppermute | solution.py:602
  7.2 28.1 %collective-permute-start = (bf16[10,304,128]{2,1,0:T(8,128)(2,1)S(1)}, bf16[10,304,128]{2,1,0:T(8,128)(2,1)}, u32[]{:S(2)}, u32[]{:S(2)}) collective-permute-start(bf16[10,304,128]{2,1,0:T(8,128)(2,1)S(1)} %pack_bins.1.refs_1_), channel_id=1, source_target_pairs={{0,8},{4,12},{8,16},{12,20},{16,24},{20,28},{1,9},{5,13},{9,17},{1... | collective-permute-start | bytes 2334728 | tf_op jit(solution)/shard_map/ppermute | solution.py:601
  31.1 18.9 %collective-permute-start.6 = (bf16[2,10,8,2432]{3,2,1,0:T(8,128)(2,1)S(1)}, bf16[2,10,8,2432]{3,2,1,0:T(8,128)(2,1)S(1)}, u32[]{:S(2)}, u32[]{:S(2)}) collective-permute-start(bf16[2,10,8,2432]{3,2,1,0:T(8,128)(2,1)S(1)} %route_rows.9), channel_id=1, source_target_pairs={{0,4},{4,0},{8,12},{12,8},{16,20},{20,16},{24,28},{28,24},{1,5},{5... | collective-permute-start | bytes 2334728 | tf_op jit(solution)/shard_map/ppermute | solution.py:617
  34.0 11.8 %copy-start.2 = (bf16[10,304,128]{2,1,0:T(8,128)(2,1)}, bf16[10,304,128]{2,1,0:T(8,128)(2,1)S(1)}, u32[]{:S(2)}) copy-start(bf16[10,304,128]{2,1,0:T(8,128)(2,1)S(1)} %collective-permute-done.3.refs_3_) | copy-start | bytes 2334724
  34.0 20.2 %collective-permute-start.4 = (bf16[10,304,128]{2,1,0:T(8,128)(2,1)S(1)}, bf16[10,304,128]{2,1,0:T(8,128)(2,1)S(1)}, u32[]{:S(2)}, u32[]{:S(2)}) collective-permute-start(bf16[10,304,128]{2,1,0:T(8,128)(2,1)S(1)} %collective-permute-done.3.refs_3_), channel_id=1, source_target_pairs={{16,8},{20,12},{8,0},{12,4},{17,9},{21,13},{9,1},{13,5},{18,10},{2... | collective-permute-start | bytes 2334728 | tf_op jit(solution)/shard_map/ppermute | solution.py:602
  35.4 19.8 %collective-permute-start.1 = (bf16[10,304,128]{2,1,0:T(8,128)(2,1)}, bf16[10,304,128]{2,1,0:T(8,128)(2,1)S(1)}, u32[]{:S(2)}, u32[]{:S(2)}) collective-permute-start(bf16[10,304,128]{2,1,0:T(8,128)(2,1)} %collective-permute-done.refs_2_), channel_id=1, source_target_pairs={{8,16},{12,20},{16,24},{20,28},{9,17},{13,21},{17,25},{21,29},{10,... | collective-permute-start | bytes 2334728 | tf_op jit(solution)/shard_map/ppermute | solution.py:601
  45.9 1.5 %copy-start.1 = (bf16[8,9,8,2432]{3,2,1,0:T(8,128)(2,1)}, bf16[8,9,8,2432]{3,2,1,0:T(8,128)(2,1)S(1)}, u32[]{:S(2)}) copy-start(bf16[8,9,8,2432]{3,2,1,0:T(8,128)(2,1)S(1)} %route_rows.8) | copy-start | bytes 8404996
  54.2 0.9 copy-start.4
  55.1 0.9 copy-start.6
  56.0 66.4 %all-to-all-start.1 = ((bf16[8,9,8,2432]{3,2,1,0:T(8,128)(2,1)}), bf16[8,9,8,2432]{3,2,1,0:T(8,128)(2,1)}, u32[]{:S(2)}, u32[]{:S(2)}) async-start(bf16[8,9,8,2432]{3,2,1,0:T(8,128)(2,1)} %copy-done.1), calls=%async_computation.1 | async-start | bytes 5603328 | tf_op jit(solution)/shard_map/all_to_all | solution.py:613
  63.8 44.0 %collective-permute-start.7 = (bf16[2,10,8,2432]{3,2,1,0:T(8,128)(2,1)S(1)}, bf16[2,10,8,2432]{3,2,1,0:T(8,128)(2,1)S(1)}, u32[]{:S(2)}, u32[]{:S(2)}) collective-permute-start(bf16[2,10,8,2432]{3,2,1,0:T(8,128)(2,1)S(1)} %route_rows.11), channel_id=1, source_target_pairs={{0,4},{4,0},{8,12},{12,8},{16,20},{20,16},{24,28},{28,24},{1,5},{5... | collective-permute-start | bytes 2334728 | tf_op jit(solution)/shard_map/ppermute | solution.py:627
  66.0 60.7 %collective-permute-start.5 = (bf16[10,304,128]{2,1,0:T(8,128)(2,1)}, bf16[10,304,128]{2,1,0:T(8,128)(2,1)}, u32[]{:S(2)}, u32[]{:S(2)}) collective-permute-start(bf16[10,304,128]{2,1,0:T(8,128)(2,1)} %copy-done.4), channel_id=1, source_target_pairs={{8,0},{12,4},{9,1},{13,5},{10,2},{14,6},{11,3},{15,7}} | collective-permute-start | bytes 2334728 | tf_op jit(solution)/shard_map/ppermute | solution.py:602
  67.3 59.4 %collective-permute-start.2 = (bf16[10,304,128]{2,1,0:T(8,128)(2,1)}, bf16[10,304,128]{2,1,0:T(8,128)(2,1)}, u32[]{:S(2)}, u32[]{:S(2)}) collective-permute-start(bf16[10,304,128]{2,1,0:T(8,128)(2,1)} %copy-done.6), channel_id=1, source_target_pairs={{16,24},{20,28},{17,25},{21,29},{18,26},{22,30},{19,27},{23,31}} | collective-permute-start | bytes 2334728 | tf_op jit(solution)/shard_map/ppermute | solution.py:601
  80.4 2.4 %copy-start = (bf16[9,2432,128]{2,1,0:T(8,128)(2,1)}, bf16[9,2432,128]{2,1,0:T(8,128)(2,1)S(1)}, u32[]{:S(2)}) copy-start(bf16[9,2432,128]{2,1,0:T(8,128)(2,1)S(1)} %left_rows.2.row_ref) | copy-start | bytes 16809988
  86.3 23.4 %copy-start.3 = (bf16[10,304,128]{2,1,0:T(8,128)(2,1)S(1)}, bf16[10,304,128]{2,1,0:T(8,128)(2,1)}, u32[]{:S(2)}) copy-start(bf16[10,304,128]{2,1,0:T(8,128)(2,1)} %copy-done.2) | copy-start | bytes 2334724
  109.7 3.6 %copy-start.5 = (bf16[10,304,128]{2,1,0:T(8,128)(2,1)S(1)}, bf16[10,304,128]{2,1,0:T(8,128)(2,1)}, u32[]{:S(2)}) copy-start(bf16[10,304,128]{2,1,0:T(8,128)(2,1)} %copy-done.4) | copy-start | bytes 2334724
  109.8 3.6 %copy-start.7 = (bf16[10,304,128]{2,1,0:T(8,128)(2,1)S(1)}, bf16[10,304,128]{2,1,0:T(8,128)(2,1)}, u32[]{:S(2)}) copy-start(bf16[10,304,128]{2,1,0:T(8,128)(2,1)} %copy-done.6) | copy-start | bytes 2334724

commit v6 on v5

--- a/solution.py
+++ b/solution.py
@@ -471,11 +471,11 @@
 
 def left_kernel(amp_ref, row_ref, out_ref, amps, rows, amps_here, rows_here):
     sources, groups, pair_rows, depth = amp_ref.shape
-    first = groups // 2
-    halves = [(0, first), (first, groups - first)] if first else [(0, groups)]
-    halves = [(at, pl.ds(lo, size), lo, size) for at, (lo, size) in enumerate(halves)]
+    edges = [groups * i // 3 for i in range(4)]
+    parts = [(lo, hi - lo) for lo, hi in zip(edges, edges[1:]) if hi > lo]
+    parts = [(at, pl.ds(lo, size), lo, size) for at, (lo, size) in enumerate(parts)]
     copies = []
-    for at, span, lo, size in halves:
+    for at, span, lo, size in parts:
         copies.append(
             [
                 pltpu.make_async_copy(
@@ -488,12 +488,12 @@
                 for group in range(lo, lo + size)
             ]
         )
-    for half in copies:
-        for copy in half:
+    for part in copies:
+        for copy in part:
             copy.start()
     total = jnp.zeros(out_ref.shape, jnp.float32)
-    for half, (_, _, lo, size) in zip(copies, halves):
-        for copy in half:
+    for part, (_, _, lo, size) in zip(copies, parts):
+        for copy in part:
             copy.wait()
         for group in range(lo, lo + size):
             lhs = amps[:, group].astype(jnp.float32).reshape(sources * pair_rows, depth)
@@ -514,7 +514,7 @@
         scratch_shapes=[
             pltpu.VMEM(amps.shape, amps.dtype),
             pltpu.VMEM(rows.shape, rows.dtype),
-            pltpu.SemaphoreType.DMA((2, sources)),
+            pltpu.SemaphoreType.DMA((3, sources)),
             pltpu.SemaphoreType.DMA((groups,)),
         ],
         cost_estimate=takes(5),

time: 143 us -> 143 us (level)
  no operation moved by 1% of the time
where the time goes in v6:
time: 143 us; the launch traced here: 142 us
  Pallas kernels  50.7 us (35%)
  waiting for transfers between devices  33.9 us (24%)
  starting transfers between devices  21.3 us (15%)
  local copies, waits for them, and re-layouts  19.6 us (14%)
  blocking collectives  10.8 us (8%)
  other arithmetic  3.55 us (2%)
  between operations  1.75 us (1%)
    ppermute x1, waiting for transfers between devices, body(): other = [near, lax.ppermute(far, 'remap', stay)]  21.7 us
    pallas_call x4, Pallas kernels, route(): pl.pallas_call(functools.partial(route_kernel, [first for first, _ in spa...  21.5 us
    optimization_barrier x1, local copies, waits for them, and re-layouts, body(): lax.optimization_barrier((amplitudes, orbital_irreps, bins))  10.9 us
    all_to_all x1, blocking collectives, reduce_to_owners(): lax.all_to_all(blocks, ('remap', 'rep'), split_axis=0, concat_axis=0, til...  10.8 us
    pallas_call x3, Pallas kernels, bins_product(): pl.pallas_call(functools.partial(bins_kernel, places, len(other)), out_sh...  10.6 us
    ppermute x3, starting transfers between devices, body(): lax.ppermute(rounds[-1][0], 'remap', hops(up, False))  8.68 us
    unnamed x20, local copies, waits for them, and re-layouts  6.42 us
    all_to_all x1, waiting for transfers between devices, left_term(): lax.all_to_all(sent, 'remap', split_axis=0, concat_axis=0, tiled=True)  5.44 us
  transfers between devices with their start and end apart: 9, of which 4 were waited for; matrix products, arithmetic and copies ran while one was open for 12% of the time, Pallas kernels for 30%

profile of v6, /device:TPU:0, one launch (start us, length us, event | category | flops | bytes accessed | tf_op | source)
XLA Modules:
  0.0 141.7 jit_solution(11794671380549519190)
XLA Ops:
  1.4 4.5 %pack_bins.1.refs_1_ = bf16[10,304,128]{2,1,0:T(8,128)(2,1)S(1)} custom-call(s32[1200]{0:T(1024)S(1)} %copy-done.8, s32[1]{0:T(128)S(6)} %copy.21.slab, bf16[150,300,128]{2,1,0:T(8,128)(2,1)} %integrals.3), custom_call_target="tpu_custom_call" | custom-call | bytes 14400000 | tf_op jit(solution)/shard_map/pack_bins/pallas_call | solution.py:139
  5.8 1.3 collective-permute-start.3
  7.1 6.4 %collective-permute-start = (bf16[10,304,128]{2,1,0:T(8,128)(2,1)S(1)}, bf16[10,304,128]{2,1,0:T(8,128)(2,1)}, u32[]{:S(2)}, u32[]{:S(2)}) collective-permute-start(bf16[10,304,128]{2,1,0:T(8,128)(2,1)S(1)} %pack_bins.1.refs_1_), channel_id=1, source_target_pairs={{0,8},{4,12},{8,16},{12,20},{16,24},{20,28},{1,9},{5,13},{9,17},{1... | collective-permute-start | bytes 2334728 | tf_op jit(solution)/shard_map/ppermute | solution.py:601
  14.6 0.8 select_reduce_fusion.3
  16.3 10.9 %copy.11 = bf16[8,1200,300]{2,0,1:T(8,128)(2,1)} copy(bf16[8,1200,300]{1,0,2:T(8,128)(2,1)} %param.7) | data formatting | bytes 11520000 | tf_op jit(solution)/shard_map/optimization_barrier | solution.py:539
  27.2 3.4 %route_rows.9 = bf16[2,10,8,2432]{3,2,1,0:T(8,128)(2,1)S(1)} custom-call(s32[1216]{0:T(1024)S(1)} %max.25.c_at, s32[2]{0:T(128)S(1)} %get-tuple-element.215.blocks, bf16[1200,8,300]{2,1,0:T(8,128)(2,1)} %bitcast.36), custom_call_target="tpu_custom_call" | custom-call | bytes 7200000 | tf_op jit(solution)/shard_map/route_rows/pallas_call | solution.py:186
  30.6 2.4 %collective-permute-start.6 = (bf16[2,10,8,2432]{3,2,1,0:T(8,128)(2,1)S(1)}, bf16[2,10,8,2432]{3,2,1,0:T(8,128)(2,1)S(1)}, u32[]{:S(2)}, u32[]{:S(2)}) collective-permute-start(bf16[2,10,8,2432]{3,2,1,0:T(8,128)(2,1)S(1)} %route_rows.9), channel_id=1, source_target_pairs={{0,4},{4,0},{8,12},{12,8},{16,20},{20,16},{24,28},{28,24},{1,5},{5... | collective-permute-start | bytes 2334728 | tf_op jit(solution)/shard_map/ppermute | solution.py:617
  34.0 1.3 collective-permute-start.4
  36.6 9.2 %route_rows.8 = bf16[8,9,8,2432]{3,2,1,0:T(8,128)(2,1)S(1)} custom-call(s32[1216]{0:T(1024)S(1)} %max.25.c_at, s32[8]{0:T(128)S(1)} %iota.95.blocks, bf16[1200,8,300]{2,1,0:T(8,128)(2,1)} %bitcast.37), custom_call_target="tpu_custom_call" | custom-call | bytes 25920000 | tf_op jit(solution)/shard_map/route_rows/pallas_call | solution.py:186
  45.8 1.5 %copy-done.1 = bf16[8,9,8,2432]{3,2,1,0:T(8,128)(2,1)} copy-done((bf16[8,9,8,2432]{3,2,1,0:T(8,128)(2,1)}, bf16[8,9,8,2432]{3,2,1,0:T(8,128)(2,1)S(1)}, u32[]{:S(2)}) %copy-start.1) | copy-done | bytes 2801688
  47.3 2.5 %collective-permute-done.6.refs_0_ = bf16[2,10,8,2432]{3,2,1,0:T(8,128)(2,1)S(1)} collective-permute-done((bf16[2,10,8,2432]{3,2,1,0:T(8,128)(2,1)S(1)}, bf16[2,10,8,2432]{3,2,1,0:T(8,128)(2,1)S(1)}, u32[]{:S(2)}, u32[]{:S(2)}) %collective-permute-start.6) | collective-permute-done | bytes 778272 | tf_op jit(solution)/shard_map/ppermute | solution.py:617
  49.8 4.3 %collective-permute-done.4.refs_3_ = bf16[10,304,128]{2,1,0:T(8,128)(2,1)S(1)} collective-permute-done((bf16[10,304,128]{2,1,0:T(8,128)(2,1)S(1)}, bf16[10,304,128]{2,1,0:T(8,128)(2,1)S(1)}, u32[]{:S(2)}, u32[]{:S(2)}) %collective-permute-start.4) | collective-permute-done | bytes 778272 | tf_op jit(solution)/shard_map/ppermute | solution.py:602
  54.2 0.9 copy-done.4
  55.1 0.9 copy-done.6
  55.9 4.4 %all-to-all-start.1 = ((bf16[8,9,8,2432]{3,2,1,0:T(8,128)(2,1)}), bf16[8,9,8,2432]{3,2,1,0:T(8,128)(2,1)}, u32[]{:S(2)}, u32[]{:S(2)}) async-start(bf16[8,9,8,2432]{3,2,1,0:T(8,128)(2,1)} %copy-done.1), calls=%async_computation.1 | async-start | bytes 5603328 | tf_op jit(solution)/shard_map/all_to_all | solution.py:613
  60.4 3.4 %route_rows.11 = bf16[2,10,8,2432]{3,2,1,0:T(8,128)(2,1)S(1)} custom-call(s32[1216]{0:T(1024)S(1)} %max.25.c_at, s32[2]{0:T(128)S(1)} %get-tuple-element.214.blocks, bf16[1200,8,300]{2,1,0:T(8,128)(2,1)} %bitcast.38), custom_call_target="tpu_custom_call" | custom-call | bytes 7200000 | tf_op jit(solution)/shard_map/route_rows/pallas_call | solution.py:186
  63.8 2.0 %collective-permute-start.7 = (bf16[2,10,8,2432]{3,2,1,0:T(8,128)(2,1)S(1)}, bf16[2,10,8,2432]{3,2,1,0:T(8,128)(2,1)S(1)}, u32[]{:S(2)}, u32[]{:S(2)}) collective-permute-start(bf16[2,10,8,2432]{3,2,1,0:T(8,128)(2,1)S(1)} %route_rows.11), channel_id=1, source_target_pairs={{0,4},{4,0},{8,12},{12,8},{16,20},{20,16},{24,28},{28,24},{1,5},{5... | collective-permute-start | bytes 2334728 | tf_op jit(solution)/shard_map/ppermute | solution.py:627
  65.9 1.3 collective-permute-start.5
  67.2 1.5 %collective-permute-start.2 = (bf16[10,304,128]{2,1,0:T(8,128)(2,1)}, bf16[10,304,128]{2,1,0:T(8,128)(2,1)}, u32[]{:S(2)}, u32[]{:S(2)}) collective-permute-start(bf16[10,304,128]{2,1,0:T(8,128)(2,1)} %copy-done.6), channel_id=1, source_target_pairs={{16,24},{20,28},{17,25},{21,29},{18,26},{22,30},{19,27},{23,31}} | collective-permute-start | bytes 2334728 | tf_op jit(solution)/shard_map/ppermute | solution.py:601
  70.6 5.5 %route_rows.10.own_ref.own = bf16[4,10,8,2432]{3,2,1,0:T(8,128)(2,1)S(1)} custom-call(s32[1216]{0:T(1024)S(1)} %max.25.c_at, s32[4]{0:T(128)S(1)} %slice_bitcast_fusion.1.blocks, bf16[1200,8,300]{2,1,0:T(8,128)(2,1)} %bitcast.39), custom_call_target="tpu_custom_call" | custom-call | bytes 14400000 | tf_op jit(solution)/shard_map/route_rows/pallas_call | solution.py:186
  76.1 4.1 %left_rows.2.row_ref = bf16[9,2432,128]{2,1,0:T(8,128)(2,1)S(1)} custom-call(s32[72]{0:T(128)S(1)} %select_reduce_fusion.7.slots, s32[72]{0:T(128)S(1)} %select_reduce_fusion.6.irreps, s32[300,128]{1,0:T(8,128)S(1)} %broadcast_xor_fusion.code_ref, bf16[150,300,128]{2,1,0:T(8,128)(2,1)} %integrals.3), custom_call_target="tpu_custom_call" | custom-call | bytes 18000000 | tf_op jit(solution)/shard_map/left_rows/pallas_call | solution.py:453
  80.2 2.4 %copy-done = bf16[9,2432,128]{2,1,0:T(8,128)(2,1)} copy-done((bf16[9,2432,128]{2,1,0:T(8,128)(2,1)}, bf16[9,2432,128]{2,1,0:T(8,128)(2,1)S(1)}, u32[]{:S(2)}) %copy-start) | copy-done | bytes 5603352
  82.6 3.5 %bins_product.3 = f32[16,128]{1,0:T(8,128)S(1)} custom-call(s32[16]{0:T(128)S(1)} %get-tuple-element.212.info, s32[8,300]{1,0:T(8,128)S(1)} %broadcast_in_dim.197.irr_ref, s32[1,128]{1,0:T(1,128)S(1)} %bitcast.32, bf16[4,10,8,2432]{3,2,1,0:T(8,128)(2,1)S(1)} %route_rows.10.own_ref.own, bf16[2,10,8,2432]{3,2,1,0:T(8,128)(2,1)S(1)} %collective-permute-done.6.refs_0_, ...), custom_call_target="tpu_custom_call" | custom-call | bytes 10800000 | tf_op jit(solution)/shard_map/bins_product/pallas_call | solution.py:394
  86.1 21.7 %collective-permute-done.7.refs_1_ = bf16[2,10,8,2432]{3,2,1,0:T(8,128)(2,1)S(1)} collective-permute-done((bf16[2,10,8,2432]{3,2,1,0:T(8,128)(2,1)S(1)}, bf16[2,10,8,2432]{3,2,1,0:T(8,128)(2,1)S(1)}, u32[]{:S(2)}, u32[]{:S(2)}) %collective-permute-start.7) | collective-permute-done | bytes 778272 | tf_op jit(solution)/shard_map/ppermute | solution.py:627
  107.8 1.9 %choose_rows.1.chosen_ref = bf16[10,128,300]{2,1,0:T(8,128)(2,1)S(1)} custom-call(s32[16]{0:T(128)S(1)} %get-tuple-element.212.info, s32[8,300]{1,0:T(8,128)S(1)} %broadcast_in_dim.197.irr_ref, bf16[4,10,8,2432]{3,2,1,0:T(8,128)(2,1)S(1)} %route_rows.10.own_ref.own, bf16[2,10,8,2432]{3,2,1,0:T(8,128)(2,1)S(1)} %collective-permute-done.6.refs_0_, ...), custom_call_target="tpu_custom_call" | custom-call | bytes 10800000 | tf_op jit(solution)/shard_map/choose_rows/pallas_call | solution.py:280
  109.7 3.6 %bins_product.4 = f32[16,128]{1,0:T(8,128)S(1)} custom-call(s32[16]{0:T(128)S(1)} %get-tuple-element.212.info, s32[8,300]{1,0:T(8,128)S(1)} %broadcast_in_dim.197.irr_ref, s32[1,128]{1,0:T(1,128)S(1)} %bitcast.33, bf16[4,10,8,2432]{3,2,1,0:T(8,128)(2,1)S(1)} %route_rows.10.own_ref.own, bf16[2,10,8,2432]{3,2,1,0:T(8,128)(2,1)S(1)} %collective-permute-done.6.refs_0_, ...), custom_call_target="tpu_custom_call" | custom-call | bytes 10800000 | tf_op jit(solution)/shard_map/bins_product/pallas_call | solution.py:394
  113.3 3.6 %bins_product.5 = f32[16,128]{1,0:T(8,128)S(1)} custom-call(s32[16]{0:T(128)S(1)} %get-tuple-element.212.info, s32[8,300]{1,0:T(8,128)S(1)} %broadcast_in_dim.197.irr_ref, s32[1,128]{1,0:T(1,128)S(1)} %bitcast.34, bf16[4,10,8,2432]{3,2,1,0:T(8,128)(2,1)S(1)} %route_rows.10.own_ref.own, bf16[2,10,8,2432]{3,2,1,0:T(8,128)(2,1)S(1)} %collective-permute-done.6.refs_0_, ...), custom_call_target="tpu_custom_call" | custom-call | bytes 10800000 | tf_op jit(solution)/shard_map/bins_product/pallas_call | solution.py:394
  116.9 5.4 %all-to-all-done.1.amp_ref = bf16[8,9,8,2432]{3,2,1,0:T(8,128)(2,1)} async-done(((bf16[8,9,8,2432]{3,2,1,0:T(8,128)(2,1)}), bf16[8,9,8,2432]{3,2,1,0:T(8,128)(2,1)}, u32[]{:S(2)}, u32[]{:S(2)}) %all-to-all-start.1) | async-done | bytes 2801696 | tf_op jit(solution)/shard_map/all_to_all | solution.py:613
  122.3 4.3 %left_product.5 = f32[64,128]{1,0:T(8,128)S(1)} custom-call(bf16[8,9,8,2432]{3,2,1,0:T(8,128)(2,1)} %all-to-all-done.1.amp_ref, bf16[9,2432,128]{2,1,0:T(8,128)(2,1)} %copy-done), custom_call_target="tpu_custom_call" | custom-call | bytes 18000000 | tf_op jit(solution)/shard_map/left_product/pallas_call | solution.py:509
  126.6 2.4 %last_product.1 = f32[16,128]{1,0:T(8,128)S(1)} custom-call(s32[16]{0:T(128)S(1)} %get-tuple-element.212.info, s32[1,128]{1,0:T(1,128)S(1)} %bitcast.35, f32[16,128]{1,0:T(8,128)S(1)} %add_add_fusion.before_ref, bf16[10,128,300]{2,1,0:T(8,128)(2,1)S(1)} %choose_rows.1.chosen_ref, bf16[10,304,128]{2,1,0:T(8,128)(2,1)} %collective-permute-done.2.up, ...), custom_call_target="tpu_custom_call" | custom-call | bytes 7200000 | tf_op jit(solution)/shard_map/last_product/pallas_call | solution.py:324
  129.4 10.8 %all_to_all.17.parts_ref = f32[32,1,256]{2,1,0:T(1,128)} all-to-all(f32[32,1,256]{2,1,0:T(1,128)S(1)} %reshape.399), channel_id=1, replica_groups=mesh['remap'=8,'rep'=4] {'remap','rep'}, dimensions={0} | all-to-all | bytes 65536 | tf_op jit(solution)/shard_map/all_to_all | solution.py:38
  140.2 1.5 %sum_parts.1 = f32[8,32]{1,0:T(8,128)} custom-call(f32[32,1,256]{2,1,0:T(1,128)} %all_to_all.17.parts_ref), custom_call_target="tpu_custom_call" | custom-call | tf_op jit(solution)/shard_map/sum_parts/pallas_call | solution.py:39
  (69 shorter events, 6.5 us)
Async XLA Ops:
  0.7 0.7 copy-start.8
  1.4 12.2 %copy-start.9 = (s32[1200]{0:T(1024)S(1)}, s32[1200]{0:T(1024)}, u32[]{:S(2)}) copy-start(s32[1200]{0:T(1024)} %irreps.1) | copy-start | bytes 14404
  5.8 28.1 %collective-permute-start.3 = (bf16[10,304,128]{2,1,0:T(8,128)(2,1)S(1)}, bf16[10,304,128]{2,1,0:T(8,128)(2,1)S(1)}, u32[]{:S(2)}, u32[]{:S(2)}) collective-permute-start(bf16[10,304,128]{2,1,0:T(8,128)(2,1)S(1)} %pack_bins.1.refs_1_), channel_id=1, source_target_pairs={{24,16},{28,20},{16,8},{20,12},{8,0},{12,4},{25,17},{29,21},{17,9}... | collective-permute-start | bytes 2334728 | tf_op jit(solution)/shard_map/ppermute | solution.py:602
  7.1 28.1 %collective-permute-start = (bf16[10,304,128]{2,1,0:T(8,128)(2,1)S(1)}, bf16[10,304,128]{2,1,0:T(8,128)(2,1)}, u32[]{:S(2)}, u32[]{:S(2)}) collective-permute-start(bf16[10,304,128]{2,1,0:T(8,128)(2,1)S(1)} %pack_bins.1.refs_1_), channel_id=1, source_target_pairs={{0,8},{4,12},{8,16},{12,20},{16,24},{20,28},{1,9},{5,13},{9,17},{1... | collective-permute-start | bytes 2334728 | tf_op jit(solution)/shard_map/ppermute | solution.py:601
  30.6 19.2 %collective-permute-start.6 = (bf16[2,10,8,2432]{3,2,1,0:T(8,128)(2,1)S(1)}, bf16[2,10,8,2432]{3,2,1,0:T(8,128)(2,1)S(1)}, u32[]{:S(2)}, u32[]{:S(2)}) collective-permute-start(bf16[2,10,8,2432]{3,2,1,0:T(8,128)(2,1)S(1)} %route_rows.9), channel_id=1, source_target_pairs={{0,4},{4,0},{8,12},{12,8},{16,20},{20,16},{24,28},{28,24},{1,5},{5... | collective-permute-start | bytes 2334728 | tf_op jit(solution)/shard_map/ppermute | solution.py:617
  34.0 11.8 %copy-start.2 = (bf16[10,304,128]{2,1,0:T(8,128)(2,1)}, bf16[10,304,128]{2,1,0:T(8,128)(2,1)S(1)}, u32[]{:S(2)}) copy-start(bf16[10,304,128]{2,1,0:T(8,128)(2,1)S(1)} %collective-permute-done.3.refs_3_) | copy-start | bytes 2334724
  34.0 20.2 %collective-permute-start.4 = (bf16[10,304,128]{2,1,0:T(8,128)(2,1)S(1)}, bf16[10,304,128]{2,1,0:T(8,128)(2,1)S(1)}, u32[]{:S(2)}, u32[]{:S(2)}) collective-permute-start(bf16[10,304,128]{2,1,0:T(8,128)(2,1)S(1)} %collective-permute-done.3.refs_3_), channel_id=1, source_target_pairs={{16,8},{20,12},{8,0},{12,4},{17,9},{21,13},{9,1},{13,5},{18,10},{2... | collective-permute-start | bytes 2334728 | tf_op jit(solution)/shard_map/ppermute | solution.py:602
  35.3 19.8 %collective-permute-start.1 = (bf16[10,304,128]{2,1,0:T(8,128)(2,1)}, bf16[10,304,128]{2,1,0:T(8,128)(2,1)S(1)}, u32[]{:S(2)}, u32[]{:S(2)}) collective-permute-start(bf16[10,304,128]{2,1,0:T(8,128)(2,1)} %collective-permute-done.refs_2_), channel_id=1, source_target_pairs={{8,16},{12,20},{16,24},{20,28},{9,17},{13,21},{17,25},{21,29},{10,... | collective-permute-start | bytes 2334728 | tf_op jit(solution)/shard_map/ppermute | solution.py:601
  45.8 1.5 %copy-start.1 = (bf16[8,9,8,2432]{3,2,1,0:T(8,128)(2,1)}, bf16[8,9,8,2432]{3,2,1,0:T(8,128)(2,1)S(1)}, u32[]{:S(2)}) copy-start(bf16[8,9,8,2432]{3,2,1,0:T(8,128)(2,1)S(1)} %route_rows.8) | copy-start | bytes 8404996
  54.1 0.9 copy-start.4
  55.1 0.9 copy-start.6
  55.9 66.4 %all-to-all-start.1 = ((bf16[8,9,8,2432]{3,2,1,0:T(8,128)(2,1)}), bf16[8,9,8,2432]{3,2,1,0:T(8,128)(2,1)}, u32[]{:S(2)}, u32[]{:S(2)}) async-start(bf16[8,9,8,2432]{3,2,1,0:T(8,128)(2,1)} %copy-done.1), calls=%async_computation.1 | async-start | bytes 5603328 | tf_op jit(solution)/shard_map/all_to_all | solution.py:613
  63.8 44.0 %collective-permute-start.7 = (bf16[2,10,8,2432]{3,2,1,0:T(8,128)(2,1)S(1)}, bf16[2,10,8,2432]{3,2,1,0:T(8,128)(2,1)S(1)}, u32[]{:S(2)}, u32[]{:S(2)}) collective-permute-start(bf16[2,10,8,2432]{3,2,1,0:T(8,128)(2,1)S(1)} %route_rows.11), channel_id=1, source_target_pairs={{0,4},{4,0},{8,12},{12,8},{16,20},{20,16},{24,28},{28,24},{1,5},{5... | collective-permute-start | bytes 2334728 | tf_op jit(solution)/shard_map/ppermute | solution.py:627
  65.9 60.7 %collective-permute-start.5 = (bf16[10,304,128]{2,1,0:T(8,128)(2,1)}, bf16[10,304,128]{2,1,0:T(8,128)(2,1)}, u32[]{:S(2)}, u32[]{:S(2)}) collective-permute-start(bf16[10,304,128]{2,1,0:T(8,128)(2,1)} %copy-done.4), channel_id=1, source_target_pairs={{8,0},{12,4},{9,1},{13,5},{10,2},{14,6},{11,3},{15,7}} | collective-permute-start | bytes 2334728 | tf_op jit(solution)/shard_map/ppermute | solution.py:602
  67.2 59.4 %collective-permute-start.2 = (bf16[10,304,128]{2,1,0:T(8,128)(2,1)}, bf16[10,304,128]{2,1,0:T(8,128)(2,1)}, u32[]{:S(2)}, u32[]{:S(2)}) collective-permute-start(bf16[10,304,128]{2,1,0:T(8,128)(2,1)} %copy-done.6), channel_id=1, source_target_pairs={{16,24},{20,28},{17,25},{21,29},{18,26},{22,30},{19,27},{23,31}} | collective-permute-start | bytes 2334728 | tf_op jit(solution)/shard_map/ppermute | solution.py:601
  80.2 2.4 %copy-start = (bf16[9,2432,128]{2,1,0:T(8,128)(2,1)}, bf16[9,2432,128]{2,1,0:T(8,128)(2,1)S(1)}, u32[]{:S(2)}) copy-start(bf16[9,2432,128]{2,1,0:T(8,128)(2,1)S(1)} %left_rows.2.row_ref) | copy-start | bytes 16809988
  86.1 23.6 %copy-start.3 = (bf16[10,304,128]{2,1,0:T(8,128)(2,1)S(1)}, bf16[10,304,128]{2,1,0:T(8,128)(2,1)}, u32[]{:S(2)}) copy-start(bf16[10,304,128]{2,1,0:T(8,128)(2,1)} %copy-done.2) | copy-start | bytes 2334724
  109.7 3.6 %copy-start.5 = (bf16[10,304,128]{2,1,0:T(8,128)(2,1)S(1)}, bf16[10,304,128]{2,1,0:T(8,128)(2,1)}, u32[]{:S(2)}) copy-start(bf16[10,304,128]{2,1,0:T(8,128)(2,1)} %copy-done.4) | copy-start | bytes 2334724
  109.7 3.6 %copy-start.7 = (bf16[10,304,128]{2,1,0:T(8,128)(2,1)S(1)}, bf16[10,304,128]{2,1,0:T(8,128)(2,1)}, u32[]{:S(2)}) copy-start(bf16[10,304,128]{2,1,0:T(8,128)(2,1)} %copy-done.6) | copy-start | bytes 2334724

commit v7 on v6

--- a/solution.py
+++ b/solution.py
@@ -129,7 +129,7 @@
         out_ref[g, pl.ds(0, d_cols)] = total
         return carry
 
-    lax.fori_loop(0, bins, one, 0)
+    lax.fori_loop(0, bins, one, 0, unroll=2)
 
 
 def pack(integrals, irreps, slab):

time: 143 us -> 142 us (level)
  no operation moved by 1% of the time
where the time goes in v7:
time: 142 us; the launch traced here: 141 us
  Pallas kernels  51 us (36%)
  waiting for transfers between devices  34.3 us (24%)
  starting transfers between devices  21.1 us (15%)
  local copies, waits for them, and re-layouts  19.6 us (14%)
  blocking collectives  10.2 us (7%)
  other arithmetic  3.55 us (2%)
  between operations  1.75 us (1%)
    pallas_call x4, Pallas kernels, route(): pl.pallas_call(functools.partial(route_kernel, [first for first, _ in spa...  21.5 us
    ppermute x1, waiting for transfers between devices, body(): other = [near, lax.ppermute(far, 'remap', stay)]  21.4 us
    optimization_barrier x1, local copies, waits for them, and re-layouts, body(): lax.optimization_barrier((amplitudes, orbital_irreps, bins))  10.9 us
    pallas_call x3, Pallas kernels, bins_product(): pl.pallas_call(functools.partial(bins_kernel, places, len(other)), out_sh...  10.6 us
    all_to_all x1, blocking collectives, reduce_to_owners(): lax.all_to_all(blocks, ('remap', 'rep'), split_axis=0, concat_axis=0, til...  10.2 us
    ppermute x3, starting transfers between devices, body(): lax.ppermute(rounds[-1][0], 'remap', hops(up, False))  8.48 us
    unnamed x20, local copies, waits for them, and re-layouts  6.42 us
    all_to_all x1, waiting for transfers between devices, left_term(): lax.all_to_all(sent, 'remap', split_axis=0, concat_axis=0, tiled=True)  6.09 us
  transfers between devices with their start and end apart: 9, of which 4 were waited for; matrix products, arithmetic and copies ran while one was open for 12% of the time, Pallas kernels for 30%

profile of v7, /device:TPU:0, one launch (start us, length us, event | category | flops | bytes accessed | tf_op | source)
XLA Modules:
  0.0 141.5 jit_solution(348267003371253913)
XLA Ops:
  1.4 4.7 %pack_bins.1.refs_1_ = bf16[10,304,128]{2,1,0:T(8,128)(2,1)S(1)} custom-call(s32[1200]{0:T(1024)S(1)} %copy-done.8, s32[1]{0:T(128)S(6)} %copy.21.slab, bf16[150,300,128]{2,1,0:T(8,128)(2,1)} %integrals.3), custom_call_target="tpu_custom_call" | custom-call | bytes 14400000 | tf_op jit(solution)/shard_map/pack_bins/pallas_call | solution.py:139
  6.1 1.3 collective-permute-start.3
  7.4 6.2 %collective-permute-start = (bf16[10,304,128]{2,1,0:T(8,128)(2,1)S(1)}, bf16[10,304,128]{2,1,0:T(8,128)(2,1)}, u32[]{:S(2)}, u32[]{:S(2)}) collective-permute-start(bf16[10,304,128]{2,1,0:T(8,128)(2,1)S(1)} %pack_bins.1.refs_1_), channel_id=1, source_target_pairs={{0,8},{4,12},{8,16},{12,20},{16,24},{20,28},{1,9},{5,13},{9,17},{1... | collective-permute-start | bytes 2334728 | tf_op jit(solution)/shard_map/ppermute | solution.py:601
  14.7 0.8 select_reduce_fusion.3
  16.4 10.9 %copy.11 = bf16[8,1200,300]{2,0,1:T(8,128)(2,1)} copy(bf16[8,1200,300]{1,0,2:T(8,128)(2,1)} %param.7) | data formatting | bytes 11520000 | tf_op jit(solution)/shard_map/optimization_barrier | solution.py:539
  27.2 3.4 %route_rows.9 = bf16[2,10,8,2432]{3,2,1,0:T(8,128)(2,1)S(1)} custom-call(s32[1216]{0:T(1024)S(1)} %max.25.c_at, s32[2]{0:T(128)S(1)} %get-tuple-element.215.blocks, bf16[1200,8,300]{2,1,0:T(8,128)(2,1)} %bitcast.36), custom_call_target="tpu_custom_call" | custom-call | bytes 7200000 | tf_op jit(solution)/shard_map/route_rows/pallas_call | solution.py:186
  30.7 2.1 %collective-permute-start.6 = (bf16[2,10,8,2432]{3,2,1,0:T(8,128)(2,1)S(1)}, bf16[2,10,8,2432]{3,2,1,0:T(8,128)(2,1)S(1)}, u32[]{:S(2)}, u32[]{:S(2)}) collective-permute-start(bf16[2,10,8,2432]{3,2,1,0:T(8,128)(2,1)S(1)} %route_rows.9), channel_id=1, source_target_pairs={{0,4},{4,0},{8,12},{12,8},{16,20},{20,16},{24,28},{28,24},{1,5},{5... | collective-permute-start | bytes 2334728 | tf_op jit(solution)/shard_map/ppermute | solution.py:617
  33.7 1.3 collective-permute-start.4
  36.4 9.2 %route_rows.8 = bf16[8,9,8,2432]{3,2,1,0:T(8,128)(2,1)S(1)} custom-call(s32[1216]{0:T(1024)S(1)} %max.25.c_at, s32[8]{0:T(128)S(1)} %iota.95.blocks, bf16[1200,8,300]{2,1,0:T(8,128)(2,1)} %bitcast.37), custom_call_target="tpu_custom_call" | custom-call | bytes 25920000 | tf_op jit(solution)/shard_map/route_rows/pallas_call | solution.py:186
  45.6 1.5 %copy-done.1 = bf16[8,9,8,2432]{3,2,1,0:T(8,128)(2,1)} copy-done((bf16[8,9,8,2432]{3,2,1,0:T(8,128)(2,1)}, bf16[8,9,8,2432]{3,2,1,0:T(8,128)(2,1)S(1)}, u32[]{:S(2)}) %copy-start.1) | copy-done | bytes 2801688
  47.1 2.5 %collective-permute-done.6.refs_0_ = bf16[2,10,8,2432]{3,2,1,0:T(8,128)(2,1)S(1)} collective-permute-done((bf16[2,10,8,2432]{3,2,1,0:T(8,128)(2,1)S(1)}, bf16[2,10,8,2432]{3,2,1,0:T(8,128)(2,1)S(1)}, u32[]{:S(2)}, u32[]{:S(2)}) %collective-permute-start.6) | collective-permute-done | bytes 778272 | tf_op jit(solution)/shard_map/ppermute | solution.py:617
  49.6 4.3 %collective-permute-done.4.refs_3_ = bf16[10,304,128]{2,1,0:T(8,128)(2,1)S(1)} collective-permute-done((bf16[10,304,128]{2,1,0:T(8,128)(2,1)S(1)}, bf16[10,304,128]{2,1,0:T(8,128)(2,1)S(1)}, u32[]{:S(2)}, u32[]{:S(2)}) %collective-permute-start.4) | collective-permute-done | bytes 778272 | tf_op jit(solution)/shard_map/ppermute | solution.py:602
  53.9 0.9 copy-done.4
  54.8 0.9 copy-done.6
  55.7 4.6 %all-to-all-start.1 = ((bf16[8,9,8,2432]{3,2,1,0:T(8,128)(2,1)}), bf16[8,9,8,2432]{3,2,1,0:T(8,128)(2,1)}, u32[]{:S(2)}, u32[]{:S(2)}) async-start(bf16[8,9,8,2432]{3,2,1,0:T(8,128)(2,1)} %copy-done.1), calls=%async_computation.1 | async-start | bytes 5603328 | tf_op jit(solution)/shard_map/all_to_all | solution.py:613
  60.3 3.4 %route_rows.11 = bf16[2,10,8,2432]{3,2,1,0:T(8,128)(2,1)S(1)} custom-call(s32[1216]{0:T(1024)S(1)} %max.25.c_at, s32[2]{0:T(128)S(1)} %get-tuple-element.214.blocks, bf16[1200,8,300]{2,1,0:T(8,128)(2,1)} %bitcast.38), custom_call_target="tpu_custom_call" | custom-call | bytes 7200000 | tf_op jit(solution)/shard_map/route_rows/pallas_call | solution.py:186
  63.7 2.1 %collective-permute-start.7 = (bf16[2,10,8,2432]{3,2,1,0:T(8,128)(2,1)S(1)}, bf16[2,10,8,2432]{3,2,1,0:T(8,128)(2,1)S(1)}, u32[]{:S(2)}, u32[]{:S(2)}) collective-permute-start(bf16[2,10,8,2432]{3,2,1,0:T(8,128)(2,1)S(1)} %route_rows.11), channel_id=1, source_target_pairs={{0,4},{4,0},{8,12},{12,8},{16,20},{20,16},{24,28},{28,24},{1,5},{5... | collective-permute-start | bytes 2334728 | tf_op jit(solution)/shard_map/ppermute | solution.py:627
  65.9 1.3 collective-permute-start.5
  67.2 1.5 %collective-permute-start.2 = (bf16[10,304,128]{2,1,0:T(8,128)(2,1)}, bf16[10,304,128]{2,1,0:T(8,128)(2,1)}, u32[]{:S(2)}, u32[]{:S(2)}) collective-permute-start(bf16[10,304,128]{2,1,0:T(8,128)(2,1)} %copy-done.6), channel_id=1, source_target_pairs={{16,24},{20,28},{17,25},{21,29},{18,26},{22,30},{19,27},{23,31}} | collective-permute-start | bytes 2334728 | tf_op jit(solution)/shard_map/ppermute | solution.py:601
  70.6 5.5 %route_rows.10.own_ref.own = bf16[4,10,8,2432]{3,2,1,0:T(8,128)(2,1)S(1)} custom-call(s32[1216]{0:T(1024)S(1)} %max.25.c_at, s32[4]{0:T(128)S(1)} %slice_bitcast_fusion.1.blocks, bf16[1200,8,300]{2,1,0:T(8,128)(2,1)} %bitcast.39), custom_call_target="tpu_custom_call" | custom-call | bytes 14400000 | tf_op jit(solution)/shard_map/route_rows/pallas_call | solution.py:186
  76.1 4.1 %left_rows.2.row_ref = bf16[9,2432,128]{2,1,0:T(8,128)(2,1)S(1)} custom-call(s32[72]{0:T(128)S(1)} %select_reduce_fusion.7.slots, s32[72]{0:T(128)S(1)} %select_reduce_fusion.6.irreps, s32[300,128]{1,0:T(8,128)S(1)} %broadcast_xor_fusion.code_ref, bf16[150,300,128]{2,1,0:T(8,128)(2,1)} %integrals.3), custom_call_target="tpu_custom_call" | custom-call | bytes 18000000 | tf_op jit(solution)/shard_map/left_rows/pallas_call | solution.py:453
  80.3 2.4 %copy-done = bf16[9,2432,128]{2,1,0:T(8,128)(2,1)} copy-done((bf16[9,2432,128]{2,1,0:T(8,128)(2,1)}, bf16[9,2432,128]{2,1,0:T(8,128)(2,1)S(1)}, u32[]{:S(2)}) %copy-start) | copy-done | bytes 5603352
  82.6 3.5 %bins_product.3 = f32[16,128]{1,0:T(8,128)S(1)} custom-call(s32[16]{0:T(128)S(1)} %get-tuple-element.212.info, s32[8,300]{1,0:T(8,128)S(1)} %broadcast_in_dim.197.irr_ref, s32[1,128]{1,0:T(1,128)S(1)} %bitcast.32, bf16[4,10,8,2432]{3,2,1,0:T(8,128)(2,1)S(1)} %route_rows.10.own_ref.own, bf16[2,10,8,2432]{3,2,1,0:T(8,128)(2,1)S(1)} %collective-permute-done.6.refs_0_, ...), custom_call_target="tpu_custom_call" | custom-call | bytes 10800000 | tf_op jit(solution)/shard_map/bins_product/pallas_call | solution.py:394
  86.2 21.4 %collective-permute-done.7.refs_1_ = bf16[2,10,8,2432]{3,2,1,0:T(8,128)(2,1)S(1)} collective-permute-done((bf16[2,10,8,2432]{3,2,1,0:T(8,128)(2,1)S(1)}, bf16[2,10,8,2432]{3,2,1,0:T(8,128)(2,1)S(1)}, u32[]{:S(2)}, u32[]{:S(2)}) %collective-permute-start.7) | collective-permute-done | bytes 778272 | tf_op jit(solution)/shard_map/ppermute | solution.py:627
  107.6 1.9 %choose_rows.1.chosen_ref = bf16[10,128,300]{2,1,0:T(8,128)(2,1)S(1)} custom-call(s32[16]{0:T(128)S(1)} %get-tuple-element.212.info, s32[8,300]{1,0:T(8,128)S(1)} %broadcast_in_dim.197.irr_ref, bf16[4,10,8,2432]{3,2,1,0:T(8,128)(2,1)S(1)} %route_rows.10.own_ref.own, bf16[2,10,8,2432]{3,2,1,0:T(8,128)(2,1)S(1)} %collective-permute-done.6.refs_0_, ...), custom_call_target="tpu_custom_call" | custom-call | bytes 10800000 | tf_op jit(solution)/shard_map/choose_rows/pallas_call | solution.py:280
  109.5 3.6 %bins_product.4 = f32[16,128]{1,0:T(8,128)S(1)} custom-call(s32[16]{0:T(128)S(1)} %get-tuple-element.212.info, s32[8,300]{1,0:T(8,128)S(1)} %broadcast_in_dim.197.irr_ref, s32[1,128]{1,0:T(1,128)S(1)} %bitcast.33, bf16[4,10,8,2432]{3,2,1,0:T(8,128)(2,1)S(1)} %route_rows.10.own_ref.own, bf16[2,10,8,2432]{3,2,1,0:T(8,128)(2,1)S(1)} %collective-permute-done.6.refs_0_, ...), custom_call_target="tpu_custom_call" | custom-call | bytes 10800000 | tf_op jit(solution)/shard_map/bins_product/pallas_call | solution.py:394
  113.0 3.6 %bins_product.5 = f32[16,128]{1,0:T(8,128)S(1)} custom-call(s32[16]{0:T(128)S(1)} %get-tuple-element.212.info, s32[8,300]{1,0:T(8,128)S(1)} %broadcast_in_dim.197.irr_ref, s32[1,128]{1,0:T(1,128)S(1)} %bitcast.34, bf16[4,10,8,2432]{3,2,1,0:T(8,128)(2,1)S(1)} %route_rows.10.own_ref.own, bf16[2,10,8,2432]{3,2,1,0:T(8,128)(2,1)S(1)} %collective-permute-done.6.refs_0_, ...), custom_call_target="tpu_custom_call" | custom-call | bytes 10800000 | tf_op jit(solution)/shard_map/bins_product/pallas_call | solution.py:394
  116.6 6.1 %all-to-all-done.1.amp_ref = bf16[8,9,8,2432]{3,2,1,0:T(8,128)(2,1)} async-done(((bf16[8,9,8,2432]{3,2,1,0:T(8,128)(2,1)}), bf16[8,9,8,2432]{3,2,1,0:T(8,128)(2,1)}, u32[]{:S(2)}, u32[]{:S(2)}) %all-to-all-start.1) | async-done | bytes 2801696 | tf_op jit(solution)/shard_map/all_to_all | solution.py:613
  122.7 4.3 %left_product.5 = f32[64,128]{1,0:T(8,128)S(1)} custom-call(bf16[8,9,8,2432]{3,2,1,0:T(8,128)(2,1)} %all-to-all-done.1.amp_ref, bf16[9,2432,128]{2,1,0:T(8,128)(2,1)} %copy-done), custom_call_target="tpu_custom_call" | custom-call | bytes 18000000 | tf_op jit(solution)/shard_map/left_product/pallas_call | solution.py:509
  127.0 2.4 %last_product.1 = f32[16,128]{1,0:T(8,128)S(1)} custom-call(s32[16]{0:T(128)S(1)} %get-tuple-element.212.info, s32[1,128]{1,0:T(1,128)S(1)} %bitcast.35, f32[16,128]{1,0:T(8,128)S(1)} %add_add_fusion.before_ref, bf16[10,128,300]{2,1,0:T(8,128)(2,1)S(1)} %choose_rows.1.chosen_ref, bf16[10,304,128]{2,1,0:T(8,128)(2,1)} %collective-permute-done.2.up, ...), custom_call_target="tpu_custom_call" | custom-call | bytes 7200000 | tf_op jit(solution)/shard_map/last_product/pallas_call | solution.py:324
  129.8 10.2 %all_to_all.17.parts_ref = f32[32,1,256]{2,1,0:T(1,128)} all-to-all(f32[32,1,256]{2,1,0:T(1,128)S(1)} %reshape.399), channel_id=1, replica_groups=mesh['remap'=8,'rep'=4] {'remap','rep'}, dimensions={0} | all-to-all | bytes 65536 | tf_op jit(solution)/shard_map/all_to_all | solution.py:38
  140.0 1.5 %sum_parts.1 = f32[8,32]{1,0:T(8,128)} custom-call(f32[32,1,256]{2,1,0:T(1,128)} %all_to_all.17.parts_ref), custom_call_target="tpu_custom_call" | custom-call | tf_op jit(solution)/shard_map/sum_parts/pallas_call | solution.py:39
  (69 shorter events, 6.5 us)
Async XLA Ops:
  0.7 0.7 copy-start.8
  1.4 12.3 %copy-start.9 = (s32[1200]{0:T(1024)S(1)}, s32[1200]{0:T(1024)}, u32[]{:S(2)}) copy-start(s32[1200]{0:T(1024)} %irreps.1) | copy-start | bytes 14404
  6.1 27.6 %collective-permute-start.3 = (bf16[10,304,128]{2,1,0:T(8,128)(2,1)S(1)}, bf16[10,304,128]{2,1,0:T(8,128)(2,1)S(1)}, u32[]{:S(2)}, u32[]{:S(2)}) collective-permute-start(bf16[10,304,128]{2,1,0:T(8,128)(2,1)S(1)} %pack_bins.1.refs_1_), channel_id=1, source_target_pairs={{24,16},{28,20},{16,8},{20,12},{8,0},{12,4},{25,17},{29,21},{17,9}... | collective-permute-start | bytes 2334728 | tf_op jit(solution)/shard_map/ppermute | solution.py:602
  7.4 27.7 %collective-permute-start = (bf16[10,304,128]{2,1,0:T(8,128)(2,1)S(1)}, bf16[10,304,128]{2,1,0:T(8,128)(2,1)}, u32[]{:S(2)}, u32[]{:S(2)}) collective-permute-start(bf16[10,304,128]{2,1,0:T(8,128)(2,1)S(1)} %pack_bins.1.refs_1_), channel_id=1, source_target_pairs={{0,8},{4,12},{8,16},{12,20},{16,24},{20,28},{1,9},{5,13},{9,17},{1... | collective-permute-start | bytes 2334728 | tf_op jit(solution)/shard_map/ppermute | solution.py:601
  30.7 18.9 %collective-permute-start.6 = (bf16[2,10,8,2432]{3,2,1,0:T(8,128)(2,1)S(1)}, bf16[2,10,8,2432]{3,2,1,0:T(8,128)(2,1)S(1)}, u32[]{:S(2)}, u32[]{:S(2)}) collective-permute-start(bf16[2,10,8,2432]{3,2,1,0:T(8,128)(2,1)S(1)} %route_rows.9), channel_id=1, source_target_pairs={{0,4},{4,0},{8,12},{12,8},{16,20},{20,16},{24,28},{28,24},{1,5},{5... | collective-permute-start | bytes 2334728 | tf_op jit(solution)/shard_map/ppermute | solution.py:617
  33.7 11.8 %copy-start.2 = (bf16[10,304,128]{2,1,0:T(8,128)(2,1)}, bf16[10,304,128]{2,1,0:T(8,128)(2,1)S(1)}, u32[]{:S(2)}) copy-start(bf16[10,304,128]{2,1,0:T(8,128)(2,1)S(1)} %collective-permute-done.3.refs_3_) | copy-start | bytes 2334724
  33.7 20.2 %collective-permute-start.4 = (bf16[10,304,128]{2,1,0:T(8,128)(2,1)S(1)}, bf16[10,304,128]{2,1,0:T(8,128)(2,1)S(1)}, u32[]{:S(2)}, u32[]{:S(2)}) collective-permute-start(bf16[10,304,128]{2,1,0:T(8,128)(2,1)S(1)} %collective-permute-done.3.refs_3_), channel_id=1, source_target_pairs={{16,8},{20,12},{8,0},{12,4},{17,9},{21,13},{9,1},{13,5},{18,10},{2... | collective-permute-start | bytes 2334728 | tf_op jit(solution)/shard_map/ppermute | solution.py:602
  35.1 19.8 %collective-permute-start.1 = (bf16[10,304,128]{2,1,0:T(8,128)(2,1)}, bf16[10,304,128]{2,1,0:T(8,128)(2,1)S(1)}, u32[]{:S(2)}, u32[]{:S(2)}) collective-permute-start(bf16[10,304,128]{2,1,0:T(8,128)(2,1)} %collective-permute-done.refs_2_), channel_id=1, source_target_pairs={{8,16},{12,20},{16,24},{20,28},{9,17},{13,21},{17,25},{21,29},{10,... | collective-permute-start | bytes 2334728 | tf_op jit(solution)/shard_map/ppermute | solution.py:601
  45.6 1.5 %copy-start.1 = (bf16[8,9,8,2432]{3,2,1,0:T(8,128)(2,1)}, bf16[8,9,8,2432]{3,2,1,0:T(8,128)(2,1)S(1)}, u32[]{:S(2)}) copy-start(bf16[8,9,8,2432]{3,2,1,0:T(8,128)(2,1)S(1)} %route_rows.8) | copy-start | bytes 8404996
  53.9 0.9 copy-start.4
  54.8 0.9 copy-start.6
  55.7 67.0 %all-to-all-start.1 = ((bf16[8,9,8,2432]{3,2,1,0:T(8,128)(2,1)}), bf16[8,9,8,2432]{3,2,1,0:T(8,128)(2,1)}, u32[]{:S(2)}, u32[]{:S(2)}) async-start(bf16[8,9,8,2432]{3,2,1,0:T(8,128)(2,1)} %copy-done.1), calls=%async_computation.1 | async-start | bytes 5603328 | tf_op jit(solution)/shard_map/all_to_all | solution.py:613
  63.7 43.8 %collective-permute-start.7 = (bf16[2,10,8,2432]{3,2,1,0:T(8,128)(2,1)S(1)}, bf16[2,10,8,2432]{3,2,1,0:T(8,128)(2,1)S(1)}, u32[]{:S(2)}, u32[]{:S(2)}) collective-permute-start(bf16[2,10,8,2432]{3,2,1,0:T(8,128)(2,1)S(1)} %route_rows.11), channel_id=1, source_target_pairs={{0,4},{4,0},{8,12},{12,8},{16,20},{20,16},{24,28},{28,24},{1,5},{5... | collective-permute-start | bytes 2334728 | tf_op jit(solution)/shard_map/ppermute | solution.py:627
  65.9 61.1 %collective-permute-start.5 = (bf16[10,304,128]{2,1,0:T(8,128)(2,1)}, bf16[10,304,128]{2,1,0:T(8,128)(2,1)}, u32[]{:S(2)}, u32[]{:S(2)}) collective-permute-start(bf16[10,304,128]{2,1,0:T(8,128)(2,1)} %copy-done.4), channel_id=1, source_target_pairs={{8,0},{12,4},{9,1},{13,5},{10,2},{14,6},{11,3},{15,7}} | collective-permute-start | bytes 2334728 | tf_op jit(solution)/shard_map/ppermute | solution.py:602
  67.2 59.8 %collective-permute-start.2 = (bf16[10,304,128]{2,1,0:T(8,128)(2,1)}, bf16[10,304,128]{2,1,0:T(8,128)(2,1)}, u32[]{:S(2)}, u32[]{:S(2)}) collective-permute-start(bf16[10,304,128]{2,1,0:T(8,128)(2,1)} %copy-done.6), channel_id=1, source_target_pairs={{16,24},{20,28},{17,25},{21,29},{18,26},{22,30},{19,27},{23,31}} | collective-permute-start | bytes 2334728 | tf_op jit(solution)/shard_map/ppermute | solution.py:601
  80.2 2.4 %copy-start = (bf16[9,2432,128]{2,1,0:T(8,128)(2,1)}, bf16[9,2432,128]{2,1,0:T(8,128)(2,1)S(1)}, u32[]{:S(2)}) copy-start(bf16[9,2432,128]{2,1,0:T(8,128)(2,1)S(1)} %left_rows.2.row_ref) | copy-start | bytes 16809988
  86.2 23.3 %copy-start.3 = (bf16[10,304,128]{2,1,0:T(8,128)(2,1)S(1)}, bf16[10,304,128]{2,1,0:T(8,128)(2,1)}, u32[]{:S(2)}) copy-start(bf16[10,304,128]{2,1,0:T(8,128)(2,1)} %copy-done.2) | copy-start | bytes 2334724
  109.4 3.6 %copy-start.5 = (bf16[10,304,128]{2,1,0:T(8,128)(2,1)S(1)}, bf16[10,304,128]{2,1,0:T(8,128)(2,1)}, u32[]{:S(2)}) copy-start(bf16[10,304,128]{2,1,0:T(8,128)(2,1)} %copy-done.4) | copy-start | bytes 2334724
  109.4 3.6 %copy-start.7 = (bf16[10,304,128]{2,1,0:T(8,128)(2,1)S(1)}, bf16[10,304,128]{2,1,0:T(8,128)(2,1)}, u32[]{:S(2)}) copy-start(bf16[10,304,128]{2,1,0:T(8,128)(2,1)} %copy-done.6) | copy-start | bytes 2334724
